TPU v7x, 32 devices: a whole 2x2x4 slice. The times are simulated.
32 devices in a mesh: dp: 4 (over x, core), seq: 8 (over z, y).
Axes of the slice: x: 2, y: 2, z: 4, core: 2. Of those that a mesh axis runs over, the one named last changes fastest.
Arguments:
- tokens: bfloat16 [2, 4096, 1024], P(None, ('dp', 'seq')), may hold values from -6 to 6
- text_states: bfloat16 [128, 1024], replicated, may hold values from -6 to 6
- image_ids: int32 [2, 4096], P(None, ('dp', 'seq')), may hold values from 0 to 7, as said below
- text_segments: int32 [128], replicated, may hold values from 0 to 7, never falling along the last dimension, each value on 1 to 32 neighbouring positions
- image_caption: int32 [2, 8], replicated, may hold values from 0 to 7
- norm_gains: bfloat16 [3, 1024], P(None, ('dp', 'seq')), may hold values from 0.099609375 to 1.8984375
- norm_shifts: bfloat16 [3, 1024], P(None, ('dp', 'seq')), may hold values from -3 to 3
- self_qkv: bfloat16 [1024, 3072], P(('dp', 'seq')), may hold values from -0.25 to 0.25
- self_out: bfloat16 [1024, 1024], P(('dp', 'seq')), may hold values from -3 to 3
- cross_query: bfloat16 [1024, 1024], P(('dp', 'seq')), may hold values from -0.25 to 0.25
- cross_keyval: bfloat16 [1024, 2048], P(('dp', 'seq')), may hold values from -0.25 to 0.25
- cross_out: bfloat16 [1024, 1024], P(('dp', 'seq')), may hold values from -0.75 to 0.75
- mlp_up: bfloat16 [1024, 4096], P(('dp', 'seq')), may hold values from -0.1875 to 0.1875
- mlp_down: bfloat16 [4096, 1024], P(('dp', 'seq')), may hold values from -0.09375 to 0.09375
- cotangent: bfloat16 [2, 4096, 1024], P(None, ('dp', 'seq')), may hold values from -6 to 6
Outputs:
- output: bfloat16 [2, 4096, 1024], P(None, ('dp', 'seq'))
- grad_tokens: float32 [2, 4096, 1024], P(None, ('dp', 'seq'))
- grad_text: float32 [128, 1024], replicated
- grad_gains: float32 [3, 1024], P(None, ('dp', 'seq'))
- grad_shifts: float32 [2, 1024], P(None, ('dp', 'seq'))
- grad_self_qkv: float32 [1024, 3072], P(('dp', 'seq'))
- grad_self_out: float32 [1024, 1024], P(('dp', 'seq'))
- grad_cross_query: float32 [1024, 1024], P(('dp', 'seq'))
- grad_cross_keyval: float32 [1024, 2048], P(('dp', 'seq'))
- grad_cross_out: float32 [1024, 1024], P(('dp', 'seq'))
- grad_mlp_up: float32 [1024, 4096], P(('dp', 'seq'))
- grad_mlp_down: float32 [4096, 1024], P(('dp', 'seq'))
- grad_mlp_shift: float32 [1024], P(('dp', 'seq'))
Inputs may be any that keep to these rules, and one draw needn't show every extreme that they name: `image_ids`: within each micro-batch, the 1024 tokens of group g are blocks of 64 rows; each run of 2 blocks in a row holds one block of every image of the group, the images g * 2 to (g + 1) * 2 - 1, so each image has 512 tokens. `text_segments`: caption numbers never fall along the text rows; every caption has one or more rows.
All inputs are finite; a program needn't handle non-finite values.
Results may differ from a plain program's by a relative error of at most 0.03.
Values may be sent and summed in bfloat16 or wider, within the bound.
No kernel may reach another device: no remote copies, remote signals or barrier semaphores. Data moves between devices by JAX's collectives and lax.ppermute only.
A program may use at most 384 MiB of HBM per device.

v0:
```python
import math

import jax
import jax.numpy as jnp
from jax import lax
from jax.sharding import PartitionSpec as P

H = 16


EPS = 1e-05
NEG = -1e30
GELU_C = 0.7978845608028654


def layer_norm(values, gain, shift):
    center = values - jnp.mean(values, -1, keepdims=True)
    spread = jnp.mean(center * center, -1, keepdims=True)
    return center * lax.rsqrt(spread + EPS) * gain + shift


def gelu_tanh(values):
    return 0.5 * values * (1.0 + jnp.tanh(GELU_C * (values + 0.044715 * values * values * values)))


def matmul(left, right):
    return jnp.dot(left, right, preferred_element_type=jnp.float32)


def contract_rows(left, right):
    return lax.dot_general(
        left, right, (((0,), (0,)), ((), ())), preferred_element_type=jnp.float32
    )


def contract_cols(left, right):
    return lax.dot_general(
        left, right, (((1,), (1,)), ((), ())), preferred_element_type=jnp.float32
    )


def unchanged(carry):
    return carry


def self_forward(queries, keys, values, ids, scale):
    rows, heads, head = queries.shape
    first = lax.axis_index("seq") * rows
    query_pos = first + jnp.arange(rows, dtype=jnp.int32)
    final_pos = first + rows - 1
    lowest = jnp.min(ids)
    start_state = (
        jnp.full((heads, rows), NEG, jnp.float32),
        jnp.zeros((heads, rows), jnp.float32),
        jnp.zeros((rows, heads, head), jnp.float32),
    )
    state = start_state
    key_piece = lax.all_gather(keys, "seq", axis=0, tiled=True)
    value_piece = lax.all_gather(values, "seq", axis=0, tiled=True)
    id_piece = lax.all_gather(ids, "seq", axis=0, tiled=True)
    count = key_piece.shape[0]
    size = math.gcd(count, 512)

    def fold_visit(inner, index):
        begin = index * size
        key_block = lax.dynamic_slice_in_dim(key_piece, begin, size, 0).reshape(size, heads, head)
        value_block = lax.dynamic_slice_in_dim(value_piece, begin, size, 0).reshape(
            size, heads, head
        )
        id_block = lax.dynamic_slice_in_dim(id_piece, begin, size, 0)
        key_pos = begin + jnp.arange(size, dtype=jnp.int32)

        def fold_attend(carry):
            highest, total, accum = carry
            scores = (
                jnp.einsum("qhd,khd->hqk", queries, key_block, preferred_element_type=jnp.float32)
                * scale
            )
            allowed = (
                (key_pos[None, :] <= query_pos[:, None]) & (id_block[None, :] == ids[:, None])
            )[None]
            fresh = jnp.maximum(highest, jnp.max(jnp.where(allowed, scores, NEG), -1))
            raised = jnp.where(allowed, jnp.exp(scores - fresh[:, :, None]), 0.0)
            factor = jnp.exp(highest - fresh)
            total = total * factor + jnp.sum(raised, -1)
            accum = accum * factor.T[:, :, None] + jnp.einsum(
                "hqk,khd->qhd",
                raised.astype(jnp.bfloat16),
                value_block,
                preferred_element_type=jnp.float32,
            )
            return (fresh, total, accum)

        skipped = (begin > final_pos) | (jnp.max(id_block) < lowest)
        return (lax.cond(skipped, unchanged, fold_attend, inner), None)

    state, _ = lax.scan(fold_visit, state, jnp.arange(count // size, dtype=jnp.int32))
    highest, total, accum = state
    attended = (accum / total.T[:, :, None]).reshape(rows, heads * head)
    return (attended, highest + jnp.log(total))


def self_backward(queries, grad_att, attended, logsum, keys, values, ids, scale):
    rows, heads, head = queries.shape
    width = heads * head
    first = lax.axis_index("seq") * rows
    query_pos = first + jnp.arange(rows, dtype=jnp.int32)
    final_pos = first + rows - 1
    lowest = jnp.min(ids)
    delta = jnp.sum(grad_att.astype(jnp.float32) * attended.reshape(rows, heads, head), -1).T
    all_keys, all_values, all_ids = (
        lax.all_gather(keys, "seq", axis=0, tiled=True),
        lax.all_gather(values, "seq", axis=0, tiled=True),
        lax.all_gather(ids, "seq", axis=0, tiled=True),
    )
    total_rows = all_keys.shape[0]
    size = math.gcd(total_rows, 512)

    def self_visit(grad_query, index):
        begin = index * size
        key_block = lax.dynamic_slice_in_dim(all_keys, begin, size, 0).reshape(size, heads, head)
        value_block = lax.dynamic_slice_in_dim(all_values, begin, size, 0).reshape(
            size, heads, head
        )
        id_block = lax.dynamic_slice_in_dim(all_ids, begin, size, 0)
        key_pos = begin + jnp.arange(size, dtype=jnp.int32)

        def self_attend(carry):
            scores = (
                jnp.einsum("qhd,khd->hqk", queries, key_block, preferred_element_type=jnp.float32)
                * scale
            )
            allowed = (
                (key_pos[None, :] <= query_pos[:, None]) & (id_block[None, :] == ids[:, None])
            )[None]
            probs = jnp.where(allowed, jnp.exp(scores - logsum[:, :, None]), 0.0)
            grad_values = jnp.einsum(
                "hqk,qhd->khd",
                probs.astype(jnp.bfloat16),
                grad_att,
                preferred_element_type=jnp.float32,
            )
            grad_probs = jnp.einsum(
                "qhd,khd->hqk", grad_att, value_block, preferred_element_type=jnp.float32
            )
            grad_scores = (probs * (grad_probs - delta[:, :, None])).astype(jnp.bfloat16)
            carry = (
                carry
                + jnp.einsum(
                    "hqk,khd->qhd", grad_scores, key_block, preferred_element_type=jnp.float32
                )
                * scale
            )
            grad_keys = (
                jnp.einsum("hqk,qhd->khd", grad_scores, queries, preferred_element_type=jnp.float32)
                * scale
            )
            return (
                carry,
                jnp.concatenate(
                    [grad_keys.reshape(size, width), grad_values.reshape(size, width)], 1
                ),
            )

        def passed(carry):
            return (carry, jnp.zeros((size, 2 * width), jnp.float32))

        skipped = (begin > final_pos) | (jnp.max(id_block) < lowest)
        return lax.cond(skipped, passed, self_attend, grad_query)

    grad_query, pieces = lax.scan(
        self_visit,
        jnp.zeros((rows, heads, head), jnp.float32),
        jnp.arange(total_rows // size, dtype=jnp.int32),
    )
    grad_keyval = lax.psum_scatter(
        pieces.reshape(total_rows, 2 * width).astype(jnp.bfloat16),
        "seq",
        scatter_dimension=0,
        tiled=True,
    )
    return jnp.concatenate([grad_query.reshape(rows, width).astype(jnp.bfloat16), grad_keyval], 1)


def micro_step(weights, cross_kv, tokens, ids, cotangent, captions, text_segments):
    gains, shifts, w_qkv, w_out, w_cq, w_ckv, w_co, w_up, w_down = weights
    rows, width = tokens.shape
    heads = H
    head = width // heads
    scale = head ** (-0.5)
    gain_all = gains.astype(jnp.float32)
    shift_all = shifts.astype(jnp.float32)
    resid = tokens.astype(jnp.float32)
    norm_one = layer_norm(resid, gain_all[0], shift_all[0]).astype(jnp.bfloat16)
    qkv = matmul(norm_one, w_qkv).astype(jnp.bfloat16)
    queries = qkv[:, :width].reshape(rows, heads, head)
    keys = qkv[:, width : 2 * width]
    values = qkv[:, 2 * width :]
    attended, logsum = self_forward(queries, keys, values, ids, scale)
    attended_low = attended.astype(jnp.bfloat16)
    hidden_one = resid + matmul(attended_low, w_out)
    norm_two = layer_norm(hidden_one, gain_all[1], shift_all[1]).astype(jnp.bfloat16)
    cquery = matmul(norm_two, w_cq).astype(jnp.bfloat16).reshape(rows, heads, head)
    text_rows = cross_kv.shape[0]
    ckeys = cross_kv[:, :width].reshape(text_rows, heads, head)
    cvals = cross_kv[:, width:].reshape(text_rows, heads, head)
    allowed = (captions[:, None] == text_segments[None, :])[None]
    cscores = jnp.einsum("qhd,khd->hqk", cquery, ckeys, preferred_element_type=jnp.float32) * scale
    cscores = jnp.where(allowed, cscores, NEG)
    raised = jnp.where(allowed, jnp.exp(cscores - jnp.max(cscores, -1, keepdims=True)), 0.0)
    cprobs = raised / jnp.sum(raised, -1, keepdims=True)
    cprobs_low = cprobs.astype(jnp.bfloat16)
    crossed = (
        jnp.einsum("hqk,khd->qhd", cprobs_low, cvals, preferred_element_type=jnp.float32)
        .reshape(rows, width)
        .astype(jnp.bfloat16)
    )
    hidden_two = hidden_one + matmul(crossed, w_co)
    norm_three = layer_norm(hidden_two, gain_all[2], shift_all[2]).astype(jnp.bfloat16)
    upward = matmul(norm_three, w_up)
    active = gelu_tanh(upward).astype(jnp.bfloat16)
    output = (hidden_two + matmul(active, w_down)).astype(jnp.bfloat16)
    grad_down = contract_rows(active, cotangent)
    grad_active = contract_cols(cotangent, w_down)
    _, gelu_back = jax.vjp(gelu_tanh, upward)
    grad_upward = gelu_back(grad_active)[0].astype(jnp.bfloat16)
    grad_up = contract_rows(norm_three, grad_upward)
    _, norm_back = jax.vjp(layer_norm, hidden_two, gain_all[2], shift_all[2])
    added, gain_three, shift_three = norm_back(contract_cols(grad_upward, w_up))
    grad_two = cotangent.astype(jnp.float32) + added
    grad_two_low = grad_two.astype(jnp.bfloat16)
    grad_co = contract_rows(crossed, grad_two_low)
    grad_crossed = contract_cols(grad_two_low, w_co).astype(jnp.bfloat16).reshape(rows, heads, head)
    grad_cvals = jnp.einsum(
        "hqk,qhd->khd", cprobs_low, grad_crossed, preferred_element_type=jnp.float32
    )
    grad_cprobs = jnp.einsum(
        "qhd,khd->hqk", grad_crossed, cvals, preferred_element_type=jnp.float32
    )
    grad_cscores = (
        cprobs * (grad_cprobs - jnp.sum(cprobs * grad_cprobs, -1, keepdims=True))
    ).astype(jnp.bfloat16)
    grad_cquery = (
        (
            jnp.einsum("hqk,khd->qhd", grad_cscores, ckeys, preferred_element_type=jnp.float32)
            * scale
        )
        .reshape(rows, width)
        .astype(jnp.bfloat16)
    )
    grad_ckeys = (
        jnp.einsum("hqk,qhd->khd", grad_cscores, cquery, preferred_element_type=jnp.float32) * scale
    )
    grad_ckv = jnp.concatenate(
        [grad_ckeys.reshape(text_rows, width), grad_cvals.reshape(text_rows, width)], 1
    )
    grad_cq = contract_rows(norm_two, grad_cquery)
    _, norm_back = jax.vjp(layer_norm, hidden_one, gain_all[1], shift_all[1])
    added, gain_two, shift_two = norm_back(contract_cols(grad_cquery, w_cq))
    grad_one = grad_two + added
    grad_one_low = grad_one.astype(jnp.bfloat16)
    grad_out = contract_rows(attended_low, grad_one_low)
    grad_att = contract_cols(grad_one_low, w_out).astype(jnp.bfloat16).reshape(rows, heads, head)
    grad_qkv_low = self_backward(queries, grad_att, attended, logsum, keys, values, ids, scale)
    grad_qkv = contract_rows(norm_one, grad_qkv_low)
    _, norm_back = jax.vjp(layer_norm, resid, gain_all[0], shift_all[0])
    added, gain_one, shift_one = norm_back(contract_cols(grad_qkv_low, w_qkv))
    grad_input = grad_one + added
    grads = (
        jnp.stack([gain_one, gain_two, gain_three]),
        jnp.stack([shift_one, shift_two, shift_three]),
        grad_qkv,
        grad_out,
        grad_cq,
        grad_co,
        grad_up,
        grad_down,
    )
    return (grads, output, grad_input, grad_ckv)


def local(
    tokens,
    text_states,
    image_ids,
    text_segments,
    image_caption,
    norm_gains,
    norm_shifts,
    self_qkv,
    self_out,
    cross_query,
    cross_keyval,
    cross_out,
    mlp_up,
    mlp_down,
    cotangent,
):
    local_weights = (
        norm_gains,
        norm_shifts,
        self_qkv,
        self_out,
        cross_query,
        cross_keyval,
        cross_out,
        mlp_up,
        mlp_down,
    )
    gathered = None
    totals = None
    cross_sum = None
    cross_kv = None
    outputs = []
    input_grads = []
    images = image_caption.shape[1]
    for batch in range(tokens.shape[0]):
        gathered = (
            lax.all_gather(local_weights[0], ("dp", "seq"), axis=1, tiled=True),
            lax.all_gather(local_weights[1], ("dp", "seq"), axis=1, tiled=True),
            lax.all_gather(local_weights[2], ("dp", "seq"), axis=0, tiled=True),
            lax.all_gather(local_weights[3], ("dp", "seq"), axis=0, tiled=True),
            lax.all_gather(local_weights[4], ("dp", "seq"), axis=0, tiled=True),
            lax.all_gather(local_weights[5], ("dp", "seq"), axis=0, tiled=True),
            lax.all_gather(local_weights[6], ("dp", "seq"), axis=0, tiled=True),
            lax.all_gather(local_weights[7], ("dp", "seq"), axis=0, tiled=True),
            lax.all_gather(local_weights[8], ("dp", "seq"), axis=0, tiled=True),
        )
        if cross_kv is None:
            cross_kv = matmul(text_states, gathered[5]).astype(jnp.bfloat16)
        ids = image_ids[batch]
        matches = ids[:, None] == jnp.arange(images, dtype=jnp.int32)[None, :]
        captions = jnp.sum(jnp.where(matches, image_caption[batch][None, :], 0), 1)
        grads, output, grad_input, grad_ckv = micro_step(
            gathered, cross_kv, tokens[batch], ids, cotangent[batch], captions, text_segments
        )
        grads = (
            lax.psum_scatter(grads[0], ("dp", "seq"), scatter_dimension=1, tiled=True),
            lax.psum_scatter(grads[1], ("dp", "seq"), scatter_dimension=1, tiled=True),
            lax.psum_scatter(grads[2], ("dp", "seq"), scatter_dimension=0, tiled=True),
            lax.psum_scatter(grads[3], ("dp", "seq"), scatter_dimension=0, tiled=True),
            lax.psum_scatter(grads[4], ("dp", "seq"), scatter_dimension=0, tiled=True),
            lax.psum_scatter(grads[5], ("dp", "seq"), scatter_dimension=0, tiled=True),
            lax.psum_scatter(grads[6], ("dp", "seq"), scatter_dimension=0, tiled=True),
            lax.psum_scatter(grads[7], ("dp", "seq"), scatter_dimension=0, tiled=True),
        )
        totals = grads if totals is None else jax.tree.map(jnp.add, totals, grads)
        cross_sum = grad_ckv if cross_sum is None else cross_sum + grad_ckv
        outputs.append(output)
        input_grads.append(grad_input)
    cross_total = lax.psum(cross_sum, ("dp", "seq")).astype(jnp.bfloat16)
    grad_text = contract_cols(cross_total, gathered[5])
    share = text_states.shape[1] // lax.axis_size(("dp", "seq"))
    text_cols = lax.dynamic_slice_in_dim(
        text_states, lax.axis_index(("dp", "seq")) * share, share, 1
    )
    grad_cross_keyval = contract_rows(text_cols, cross_total)
    return (
        jnp.stack(outputs),
        jnp.stack(input_grads),
        grad_text,
        totals[0],
        totals[1][:2],
        totals[2],
        totals[3],
        totals[4],
        grad_cross_keyval,
        totals[5],
        totals[6],
        totals[7],
        totals[1][2],
    )


def solution(mesh):
    in_specs = (
        P(None, ("dp", "seq"), None),
        P(),
        P(None, ("dp", "seq")),
        P(),
        P(),
        P(None, ("dp", "seq")),
        P(None, ("dp", "seq")),
        P(("dp", "seq"), None),
        P(("dp", "seq"), None),
        P(("dp", "seq"), None),
        P(("dp", "seq"), None),
        P(("dp", "seq"), None),
        P(("dp", "seq"), None),
        P(("dp", "seq"), None),
        P(None, ("dp", "seq"), None),
    )
    out_specs = (
        P(None, ("dp", "seq"), None),
        P(None, ("dp", "seq"), None),
        P(),
        P(None, ("dp", "seq")),
        P(None, ("dp", "seq")),
        P(("dp", "seq"), None),
        P(("dp", "seq"), None),
        P(("dp", "seq"), None),
        P(("dp", "seq"), None),
        P(("dp", "seq"), None),
        P(("dp", "seq"), None),
        P(("dp", "seq"), None),
        P(("dp", "seq")),
    )
    return jax.shard_map(local, mesh=mesh, in_specs=in_specs, out_specs=out_specs, check_vma=False)
```

profile of v0, /device:TPU:0, one launch (start us, length us, event | category | flops | bytes accessed | tf_op | source)
XLA Modules:
  0.0 2540.8 jit_solution(146075504138484600)
XLA Ops:
  8.7 70.2 %all-gather.3 = bf16[32,32,3]{1,2,0:T(4,128)(2,1)S(1)} all-gather(bf16[1,32,3]{1,2,0:T(4,128)(2,1)} %bitcast.534), channel_id=1, replica_groups=mesh['dp'=4,'seq'=8] {'dp','seq'}, dimensions={0}, use_global_device_ids=true | all-gather | bytes 6336 | tf_op jit(solution)/shard_map/all_gather | solution.py:320
  79.0 63.8 %all-gather.2 = bf16[32,32,3]{1,2,0:T(4,128)(2,1)S(1)} all-gather(bf16[1,32,3]{1,2,0:T(4,128)(2,1)} %bitcast.535), channel_id=1, replica_groups=mesh['dp'=4,'seq'=8] {'dp','seq'}, dimensions={0}, use_global_device_ids=true | all-gather | bytes 6336 | tf_op jit(solution)/shard_map/all_gather | solution.py:319
  146.1 4.0 convolution_convert_fusion
  161.1 18.4 all-gather.1
  179.5 16.4 all-gather
  201.1 4.5 copy.256
  205.6 43.4 %all-gather.36.cloned.1.call-done = bf16[1024,1024]{1,0:T(8,128)(2,1)} async-done(((bf16[128,1024]{1,0:T(8,128)(2,1)}), bf16[1024,1024]{1,0:T(8,128)(2,1)}) %all-gather.36.cloned.1.call-update) | async-done | bytes 2097168 | tf_op jit(solution)/shard_map/all_gather | solution.py:59
  249.0 3.9 copy.257
  253.0 12.7 while.63
  256.3 6.1 conditional.13
  265.8 41.1 %all-gather.22.cloned.1.call-done = bf16[1024,1024]{1,0:T(8,128)(2,1)} async-done(((bf16[32,1024]{1,0:T(8,128)(2,1)}), bf16[1024,1024]{1,0:T(8,128)(2,1)}) %all-gather.22.cloned.1.call-update) | async-done | bytes 2097168 | tf_op jit(solution)/shard_map/all_gather | solution.py:322
  309.3 55.8 %all-gather.26.cloned.1.call-done = bf16[1024,1024]{1,0:T(8,128)(2,1)} async-done(((bf16[32,1024]{1,0:T(8,128)(2,1)}), bf16[1024,1024]{1,0:T(8,128)(2,1)}) %all-gather.26.cloned.1.call-update) | async-done | bytes 2097168 | tf_op jit(solution)/shard_map/all_gather | solution.py:323
  368.1 47.9 %all-gather.18.cloned.1.call-done = bf16[1024,1024]{1,0:T(8,128)(2,1)} async-done(((bf16[128,1024]{1,0:T(8,128)(2,1)}), bf16[1024,1024]{1,0:T(8,128)(2,1)}) %all-gather.18.cloned.1.call-update) | async-done | bytes 2097168 | tf_op jit(solution)/shard_map/all_gather | solution.py:58
  418.9 47.6 %all-gather.20.cloned.1.call-done = bf16[1024,1024]{1,0:T(8,128)(2,1)} async-done(((bf16[128,1024]{1,0:T(8,128)(2,1)}), bf16[1024,1024]{1,0:T(8,128)(2,1)}) %all-gather.20.cloned.1.call-update) | async-done | bytes 2097168 | tf_op jit(solution)/shard_map/all_gather | solution.py:59
  466.5 3.9 copy.250
  471.3 13.3 while.62
  474.5 6.7 conditional.12
  492.4 32.2 %all-gather.28.cloned.1.call-done = bf16[1024,1024]{1,0:T(8,128)(2,1)} async-done(((bf16[32,1024]{1,0:T(8,128)(2,1)}), bf16[1024,1024]{1,0:T(8,128)(2,1)}) %all-gather.28.cloned.1.call-update) | async-done | bytes 2097168 | tf_op jit(solution)/shard_map/all_gather | solution.py:325
  534.0 69.7 %all-gather.30.cloned.1.call-done = bf16[1024,4096]{1,0:T(8,128)(2,1)} async-done(((bf16[32,4096]{1,0:T(8,128)(2,1)}), bf16[1024,4096]{1,0:T(8,128)(2,1)}) %all-gather.30.cloned.1.call-update) | async-done | bytes 8388624 | tf_op jit(solution)/shard_map/all_gather | solution.py:326
  603.7 6.2 fusion.188
  612.7 70.0 %all-gather.32.cloned.1.call-done = bf16[4096,1024]{1,0:T(8,128)(2,1)} async-done(((bf16[128,1024]{1,0:T(8,128)(2,1)}), bf16[4096,1024]{1,0:T(8,128)(2,1)}) %all-gather.32.cloned.1.call-update) | async-done | bytes 8388624 | tf_op jit(solution)/shard_map/all_gather | solution.py:327
  682.7 8.2 fusion.81
  691.9 6.6 fusion.210
  698.6 4.2 fusion.77
  731.5 28.4 %while.65 = (s32[]{:T(128)}, f32[128,16,64]{0,2,1:T(8,128)S(1)}, bf16[2,512,2048]{2,1,0:T(8,128)(2,1)}, s32[2]{0:T(128)S(1)}, s32[]{:T(128)}, /*index=5*/s32[102...) while((s32[]{:T(128)}, f32[128,16,64]{0,2,1:T(8,128)S(1)}, ...), condition=%wide.region_58.59_spmd.clone, body=%wide.region_54.58_spmd.clone.sunk | while | flops 687277184 | bytes 43230112 | solution.py:171
  735.1 10.0 conditional.15
  768.1 26.3 %while.64 = (s32[]{:T(128)}, f32[128,16,64]{0,2,1:T(8,128)S(1)}, bf16[2,512,2048]{2,1,0:T(8,128)(2,1)}, s32[2]{0:T(128)S(1)}, s32[]{:T(128)}, /*index=5*/s32[102...) while((s32[]{:T(128)}, f32[128,16,64]{0,2,1:T(8,128)S(1)}, ...), condition=%wide.region_44.45_spmd.clone, body=%wide.region_40.44_spmd.clone.sunk | while | flops 687277184 | bytes 43230112 | solution.py:171
  771.4 8.1 conditional.14
  798.5 57.8 %reduce-scatter.17.cloned.1.call-done = bf16[128,2048]{1,0:T(8,128)(2,1)} async-done(((bf16[1024,2048]{1,0:T(8,128)(2,1)}), bf16[128,2048]{1,0:T(8,128)(2,1)}) %reduce-scatter.17.cloned.1.call-update) | async-done | bytes 524304 | tf_op jit(solution)/shard_map/reduce_scatter | solution.py:176
  856.4 5.2 fusion.124
  861.6 86.5 %reduce-scatter.15.cloned.1.call-done = bf16[128,2048]{1,0:T(8,128)(2,1)} async-done(((bf16[1024,2048]{1,0:T(8,128)(2,1)}), bf16[128,2048]{1,0:T(8,128)(2,1)}) %reduce-scatter.15.cloned.1.call-update) | async-done | bytes 524304 | tf_op jit(solution)/shard_map/reduce_scatter | solution.py:176
  948.1 5.3 fusion.121
  957.3 4.9 convolution_add_fusion.5
  974.5 6.5 convolution_add_fusion.2
  985.8 8.3 convolution_add_fusion.1
  994.6 4.0 fusion.134
  998.6 9.8 convolution_add_fusion
  1017.9 5.6 fusion.98
  1026.3 50.9 %all-reduce.1 = bf16[128,2048]{0,1:T(8,128)(2,1)S(1)} all-reduce(f32[128,2048]{0,1:T(8,128)} %maximum_add_fusion), channel_id=1, replica_groups=mesh['dp'=4,'seq'=8] {'dp','seq'}, use_global_device_ids=true, to_apply=%region_62.63 | all-reduce | flops 262144 | bytes 1572864 | tf_op jit(solution)/shard_map/psum | solution.py:351
  1078.3 4.6 fusion.213
  1084.5 5.9 reduce-scatter.31.cloned.1.call-done
  1091.8 131.0 %reduce-scatter.33.cloned.1.call-done = f32[32,3]{1,0:T(8,128)} async-done(((f32[1024,3]{1,0:T(8,128)}), f32[32,3]{1,0:T(8,128)}) %reduce-scatter.33.cloned.1.call-update) | async-done | bytes 400
  1225.5 140.6 %reduce-scatter.21.cloned.1.call-done = f32[32,1024]{1,0:T(8,128)} async-done(((f32[1024,1024]{1,0:T(8,128)}), f32[32,1024]{1,0:T(8,128)}) %reduce-scatter.21.cloned.1.call-update) | async-done | bytes 131088 | tf_op jit(solution)/shard_map/reduce_scatter | solution.py:341
  1366.1 144.0 %reduce-scatter.23.cloned.1.call-done = f32[32,1024]{1,0:T(8,128)} async-done(((f32[1024,1024]{1,0:T(8,128)}), f32[32,1024]{1,0:T(8,128)}) %reduce-scatter.23.cloned.1.call-update) | async-done | bytes 131088 | tf_op jit(solution)/shard_map/reduce_scatter | solution.py:342
  1510.1 144.2 %reduce-scatter.25.cloned.1.call-done = f32[32,1024]{1,0:T(8,128)} async-done(((f32[1024,1024]{1,0:T(8,128)}), f32[32,1024]{1,0:T(8,128)}) %reduce-scatter.25.cloned.1.call-update) | async-done | bytes 131088 | tf_op jit(solution)/shard_map/reduce_scatter | solution.py:343
  1654.3 159.0 %reduce-scatter.19.cloned.1.call-done = f32[32,3072]{1,0:T(8,128)} async-done(((f32[1024,3072]{1,0:T(8,128)}), f32[32,3072]{1,0:T(8,128)}) %reduce-scatter.19.cloned.1.call-update) | async-done | bytes 393232 | tf_op jit(solution)/shard_map/reduce_scatter | solution.py:340
  1813.3 360.0 %reduce-scatter.27.cloned.1.call-done = f32[32,4096]{1,0:T(8,128)} async-done(((f32[1024,4096]{1,0:T(8,128)}), f32[32,4096]{1,0:T(8,128)}) %reduce-scatter.27.cloned.1.call-update) | async-done | bytes 524304 | tf_op jit(solution)/shard_map/reduce_scatter | solution.py:344
  2173.3 360.4 %reduce-scatter.29.cloned.1.call-done = f32[128,1024]{1,0:T(8,128)} async-done(((f32[4096,1024]{1,0:T(8,128)}), f32[128,1024]{1,0:T(8,128)}) %reduce-scatter.29.cloned.1.call-update) | async-done | bytes 524304 | tf_op jit(solution)/shard_map/reduce_scatter | solution.py:345
  (584 shorter events, 195.3 us)
Async XLA Ops:
  7.2 188.9 %copy-start = (bf16[128,1024]{1,0:T(8,128)(2,1)S(1)}, bf16[128,1024]{1,0:T(8,128)(2,1)}, u32[]{:S(2)}) copy-start(bf16[128,1024]{1,0:T(8,128)(2,1)} %param.32) | copy-start | bytes 786436
  7.2 138.9 %all-gather.16.cloned.1.call-start = ((), (), s32[]{:S(2)}) async-start(), calls=%async_computation.10 | async-start | bytes 6488064 | tf_op jit(solution)/shard_map/all_gather | solution.py:321
  7.9 188.2 %all-gather.24.cloned.1.call-start = ((), (), s32[]{:S(2)}) async-start(), calls=%async_computation.14 | async-start | bytes 4325376 | tf_op jit(solution)/shard_map/all_gather | solution.py:324
  8.7 192.5 %all-gather.34.cloned.1.call-start = ((), (), s32[]{:S(2)}) async-start(), calls=%async_computation.19 | async-start | bytes 2359296 | tf_op jit(solution)/shard_map/all_gather | solution.py:58
  146.0 342.8 %copy-start.96 = (f32[1,1024]{1,0:T(1,128)}, f32[1,1024]{1,0:T(1,128)S(1)}, u32[]{:S(2)}) copy-start(f32[1,1024]{1,0:T(1,128)S(1)} %get-tuple-element.1417) | copy-start | bytes 12292
  146.0 463.9 %copy-start.77 = (f32[1,1024]{1,0:T(1,128)}, f32[1,1024]{1,0:T(1,128)S(1)}, u32[]{:S(2)}) copy-start(f32[1,1024]{1,0:T(1,128)S(1)} %get-tuple-element.1416) | copy-start | bytes 12292
  146.0 560.4 %copy-start.73 = (f32[1,1024]{1,0:T(1,128)}, f32[1,1024]{1,0:T(1,128)S(1)}, u32[]{:S(2)}) copy-start(f32[1,1024]{1,0:T(1,128)S(1)} %get-tuple-element.1413) | copy-start | bytes 12292
  146.0 577.0 %copy-start.94 = (f32[1,1024]{1,0:T(1,128)}, f32[1,1024]{1,0:T(1,128)S(1)}, u32[]{:S(2)}) copy-start(f32[1,1024]{1,0:T(1,128)S(1)} %get-tuple-element.1414) | copy-start | bytes 12292
  150.9 98.1 %all-gather.36.cloned.1.call-start = ((), (), s32[]{:S(2)}) async-start(), calls=%async_computation.20 | async-start | bytes 2359296 | tf_op jit(solution)/shard_map/all_gather | solution.py:59
  151.5 155.4 %all-gather.22.cloned.1.call-start = ((), (), s32[]{:S(2)}) async-start(), calls=%async_computation.13 | async-start | bytes 2162688 | tf_op jit(solution)/shard_map/all_gather | solution.py:322
  152.1 213.0 %all-gather.26.cloned.1.call-start = ((), (), s32[]{:S(2)}) async-start(), calls=%async_computation.15 | async-start | bytes 2162688 | tf_op jit(solution)/shard_map/all_gather | solution.py:323
  152.7 263.3 %all-gather.18.cloned.1.call-start = ((), (), s32[]{:S(2)}) async-start(), calls=%async_computation.11 | async-start | bytes 2359296 | tf_op jit(solution)/shard_map/all_gather | solution.py:58
  157.6 308.9 %all-gather.20.cloned.1.call-start = ((), (), s32[]{:S(2)}) async-start(), calls=%async_computation.12 | async-start | bytes 2359296 | tf_op jit(solution)/shard_map/all_gather | solution.py:59
  158.3 366.2 %all-gather.28.cloned.1.call-start = ((), (), s32[]{:S(2)}) async-start(), calls=%async_computation.16 | async-start | bytes 2162688 | tf_op jit(solution)/shard_map/all_gather | solution.py:325
  159.1 444.6 %all-gather.30.cloned.1.call-start = ((), (), s32[]{:S(2)}) async-start(), calls=%async_computation.17 | async-start | bytes 8650752 | tf_op jit(solution)/shard_map/all_gather | solution.py:326
  159.7 523.1 %all-gather.32.cloned.1.call-start = ((), (), s32[]{:S(2)}) async-start(), calls=%async_computation.18 | async-start | bytes 8650752 | tf_op jit(solution)/shard_map/all_gather | solution.py:327
  160.4 696.0 %reduce-scatter.17.cloned.1.call-start = ((), (), s32[]{:S(2)}) async-start(), calls=%async_computation.22 | async-start | bytes 4718592 | tf_op jit(solution)/shard_map/reduce_scatter | solution.py:176
  196.1 295.5 %copy-start.118 = (pred[128,128]{0,1:T(8,128)(4,1)}, pred[128,128]{0,1:T(8,128)(4,1)S(1)}, u32[]{:S(2)}) copy-start(pred[128,128]{0,1:T(8,128)(4,1)S(1)} %get-tuple-element.1436) | copy-start | bytes 49156
  196.1 332.5 %copy-start.119 = (pred[128,128]{0,1:T(8,128)(4,1)}, pred[128,128]{0,1:T(8,128)(4,1)S(1)}, u32[]{:S(2)}) copy-start(pred[128,128]{0,1:T(8,128)(4,1)S(1)} %get-tuple-element.1435) | copy-start | bytes 49156
  265.8 101.4 %copy-start.51 = (bf16[128,16,64]{0,2,1:T(8,128)(2,1)}, bf16[128,16,64]{0,2,1:T(8,128)(2,1)S(1)}, u32[]{:S(2)}) copy-start(bf16[128,16,64]{0,2,1:T(8,128)(2,1)S(1)} %fusion.151) | copy-start | bytes 786436
  309.1 414.0 %copy-start.123 = (f32[128]{0:T(128)}, f32[128]{0:T(128)S(1)}, u32[]{:S(2)}) copy-start(f32[128]{0:T(128)S(1)} %broadcast_multiply_fusion.1) | copy-start | bytes 1540
  309.3 109.6 %copy-start.148 = (f32[128]{0:T(128)}, f32[128]{0:T(128)S(1)}, u32[]{:S(2)}) copy-start(f32[128]{0:T(128)S(1)} %multiply_reduce_fusion.13) | copy-start | bytes 1540
  309.3 413.8 %copy-start.131 = (f32[128]{0:T(128)}, f32[128]{0:T(128)S(1)}, u32[]{:S(2)}) copy-start(f32[128]{0:T(128)S(1)} %fusion.167) | copy-start | bytes 1540
  488.6 234.5 %copy-start.125 = (f32[128]{0:T(128)}, f32[128]{0:T(128)S(1)}, u32[]{:S(2)}) copy-start(f32[128]{0:T(128)S(1)} %broadcast_multiply_fusion.4) | copy-start | bytes 1540
  489.3 233.7 %copy-start.133 = (f32[128]{0:T(128)}, f32[128]{0:T(128)S(1)}, u32[]{:S(2)}) copy-start(f32[128]{0:T(128)S(1)} %fusion.164) | copy-start | bytes 1540
  491.6 221.6 %copy-start.127 = (f32[16,128]{1,0:T(8,128)}, f32[16,128]{1,0:T(8,128)S(1)}, u32[]{:S(2)}) copy-start(f32[16,128]{1,0:T(8,128)S(1)} %get-tuple-element.1439) | copy-start | bytes 24580
  526.7 179.7 %copy-start.10 = (f32[128,1024]{1,0:T(8,128)}, f32[128,1024]{1,0:T(8,128)S(1)}, u32[]{:S(2)}) copy-start(f32[128,1024]{1,0:T(8,128)S(1)} %get-tuple-element.1442) | copy-start | bytes 1572868
  526.7 179.7 %copy-start.102 = (f32[128]{0:T(128)}, f32[128]{0:T(128)S(1)}, u32[]{:S(2)}) copy-start(f32[128]{0:T(128)S(1)} %broadcast_multiply_fusion) | copy-start | bytes 1540
  528.5 190.1 %copy-start.129 = (f32[16,128]{1,0:T(8,128)}, f32[16,128]{1,0:T(8,128)S(1)}, u32[]{:S(2)}) copy-start(f32[16,128]{1,0:T(8,128)S(1)} %get-tuple-element.1445) | copy-start | bytes 24580
  533.0 173.5 %copy-start.104 = (f32[128]{0:T(128)}, f32[128]{0:T(128)S(1)}, u32[]{:S(2)}) copy-start(f32[128]{0:T(128)S(1)} %broadcast_multiply_fusion.3) | copy-start | bytes 1540
  533.9 172.6 %copy-start.110 = (f32[128]{0:T(128)}, f32[128]{0:T(128)S(1)}, u32[]{:S(2)}) copy-start(f32[128]{0:T(128)S(1)} %fusion.168) | copy-start | bytes 1540
  534.0 172.5 %copy-start.112 = (f32[128]{0:T(128)}, f32[128]{0:T(128)S(1)}, u32[]{:S(2)}) copy-start(f32[128]{0:T(128)S(1)} %fusion.165) | copy-start | bytes 1540
  760.6 187.5 %reduce-scatter.15.cloned.1.call-start = ((), (), s32[]{:S(2)}) async-start(), calls=%async_computation.21 | async-start | bytes 4718592 | tf_op jit(solution)/shard_map/reduce_scatter | solution.py:176
  794.4 296.0 %reduce-scatter.31.cloned.1.call-start = ((), (), s32[]{:S(2)}) async-start(), calls=%async_computation.29 | async-start | bytes 540672
  798.5 149.6 %copy-start.4 = (bf16[2,128,1024]{2,1,0:T(8,128)(2,1)S(1)}, bf16[2,128,1024]{2,1,0:T(8,128)(2,1)}, u32[]{:S(2)}) copy-start(bf16[2,128,1024]{2,1,0:T(8,128)(2,1)} %param.31) | copy-start | bytes 1572868
  798.5 149.6 %copy-start.72 = (f32[1,1024]{1,0:T(1,128)S(1)}, f32[1,1024]{1,0:T(1,128)}, u32[]{:S(2)}) copy-start(f32[1,1024]{1,0:T(1,128)} %copy-done.71) | copy-start | bytes 12292
  798.5 149.6 %copy-start.99 = (f32[128]{0:T(128)S(1)}, f32[128]{0:T(128)}, u32[]{:S(2)}) copy-start(f32[128]{0:T(128)} %copy-done.98) | copy-start | bytes 1540
  798.5 149.6 %copy-start.101 = (f32[128]{0:T(128)S(1)}, f32[128]{0:T(128)}, u32[]{:S(2)}) copy-start(f32[128]{0:T(128)} %copy-done.100) | copy-start | bytes 1540
  861.6 93.1 %copy-start.116 = (f32[1024]{0:T(1024)S(1)}, f32[1024]{0:T(1024)}, u32[]{:S(2)}) copy-start(f32[1024]{0:T(1024)} %get-tuple-element.1237) | copy-start | bytes 12292
  861.6 93.1 %copy-start.117 = (f32[1024]{0:T(1024)S(1)}, f32[1024]{0:T(1024)}, u32[]{:S(2)}) copy-start(f32[1024]{0:T(1024)} %get-tuple-element.1428) | copy-start | bytes 12292
  861.6 93.1 %copy-start.121 = (f32[1024]{0:T(1024)S(1)}, f32[1024]{0:T(1024)}, u32[]{:S(2)}) copy-start(f32[1024]{0:T(1024)} %get-tuple-element.1235) | copy-start | bytes 12292
  955.8 267.0 %reduce-scatter.33.cloned.1.call-start = ((), (), s32[]{:S(2)}) async-start(), calls=%async_computation.30 | async-start | bytes 540672
  957.0 409.1 %reduce-scatter.21.cloned.1.call-start = ((), (), s32[]{:S(2)}) async-start(), calls=%async_computation.24 | async-start | bytes 4325376 | tf_op jit(solution)/shard_map/reduce_scatter | solution.py:341
  962.4 547.7 %reduce-scatter.23.cloned.1.call-start = ((), (), s32[]{:S(2)}) async-start(), calls=%async_computation.25 | async-start | bytes 4325376 | tf_op jit(solution)/shard_map/reduce_scatter | solution.py:342
  967.2 687.1 %reduce-scatter.25.cloned.1.call-start = ((), (), s32[]{:S(2)}) async-start(), calls=%async_computation.26 | async-start | bytes 4325376 | tf_op jit(solution)/shard_map/reduce_scatter | solution.py:343
  971.5 841.8 %reduce-scatter.19.cloned.1.call-start = ((), (), s32[]{:S(2)}) async-start(), calls=%async_computation.23 | async-start | bytes 12976128 | tf_op jit(solution)/shard_map/reduce_scatter | solution.py:340
  981.0 1192.3 %reduce-scatter.27.cloned.1.call-start = ((), (), s32[]{:S(2)}) async-start(), calls=%async_computation.27 | async-start | bytes 17301504 | tf_op jit(solution)/shard_map/reduce_scatter | solution.py:344
  994.1 1539.6 %reduce-scatter.29.cloned.1.call-start = ((), (), s32[]{:S(2)}) async-start(), calls=%async_computation.28 | async-start | bytes 17301504 | tf_op jit(solution)/shard_map/reduce_scatter | solution.py:345
  (130 other events, 1228.3 us)
Sparse Core Ops, SparseCore 0:
  10.9 72.2 all-gather.15
  86.3 60.4 all-gather.23
  151.1 47.5 all-gather.33
  201.2 47.7 all-gather.35
  251.8 55.0 all-gather.21
  309.7 55.3 all-gather.25
  367.8 48.1 all-gather.17
  418.7 47.7 all-gather.19
  469.5 55.0 all-gather.27
  527.4 76.2 all-gather.29
  606.7 75.9 all-gather.31
  760.0 96.3 reduce-scatter.16
  860.4 87.6 reduce-scatter.14
  955.9 134.4 reduce-scatter.30
  1092.6 130.1 reduce-scatter.32
  1225.5 140.5 reduce-scatter.20
  1368.8 141.2 reduce-scatter.22
  1512.8 141.4 reduce-scatter.24
  1660.9 152.3 reduce-scatter.18
  1816.1 357.1 reduce-scatter.26
  2176.3 357.3 reduce-scatter.28
where the time goes:
time: 2550 us; the launch traced here: 2540 us
  waiting for transfers between devices  2000 us (78%)
  blocking collectives  220 us (9%)
  matrix products  168 us (7%)
  local copies, waits for them, and re-layouts  92.6 us (4%)
    reduce_scatter x1, waiting for transfers between devices, local(): lax.psum_scatter(grads[7], ('dp', 'seq'), scatter_dimension=0, tiled=True)  360 us
    reduce_scatter x1, waiting for transfers between devices, local(): lax.psum_scatter(grads[6], ('dp', 'seq'), scatter_dimension=0, tiled=True)  360 us
    reduce_scatter x1, waiting for transfers between devices, local(): lax.psum_scatter(grads[2], ('dp', 'seq'), scatter_dimension=0, tiled=True)  159 us
    reduce_scatter x2, waiting for transfers between devices, self_backward(): lax.psum_scatter(pieces.reshape(total_rows, 2 * width).astype(jnp.bfloat1...  144 us
    reduce_scatter x1, waiting for transfers between devices, local(): lax.psum_scatter(grads[5], ('dp', 'seq'), scatter_dimension=0, tiled=True)  144 us
    reduce_scatter x1, waiting for transfers between devices, local(): lax.psum_scatter(grads[4], ('dp', 'seq'), scatter_dimension=0, tiled=True)  144 us
    unnamed x23, waiting for transfers between devices  143 us
    reduce_scatter x1, waiting for transfers between devices, local(): lax.psum_scatter(grads[3], ('dp', 'seq'), scatter_dimension=0, tiled=True)  141 us
  transfers between devices with their start and end apart: 21, of which 18 were waited for; matrix products, arithmetic and copies ran while one was open for 8% of the time, Pallas kernels for 0%

commit v1 on v0

v1 whole, which is shorter than its diff:
```python
import functools

import jax
import jax.numpy as jnp
from jax import lax
from jax.experimental import pallas as pl
from jax.experimental.pallas import tpu as pltpu
from jax.sharding import PartitionSpec as P

H = 16
STRIPE = 64
EPS = 1e-05
NEG = -1e30
GELU_C = 0.7978845608028654
BF = jnp.bfloat16
F32 = jnp.float32
AXES = ("dp", "seq")


def mm(left, right):
    return jnp.dot(left, right, preferred_element_type=F32)


def mm_rows(left, right):
    return lax.dot_general(left, right, (((0,), (0,)), ((), ())), preferred_element_type=F32)


def mm_cols(left, right):
    return lax.dot_general(left, right, (((1,), (1,)), ((), ())), preferred_element_type=F32)


def pick(array, dim, index):
    return lax.dynamic_index_in_dim(array, index, dim, keepdims=False)


class Grid:
    def __init__(self, dp, seq):
        self.dp, self.seq, self.t = dp, seq, seq // 8
        self.count = dp * seq
        me = lax.axis_index(AXES)
        part = lax.rem(me, seq)
        self.me = me
        self.x = me // (2 * seq)
        self.c = lax.rem(me // seq, 2)
        self.z = part // (2 * self.t)
        self.r = lax.rem(part // 2, self.t)
        self.y = lax.rem(part, 2)

    def coords(self, d):
        part = d % self.seq
        return (
            d // (2 * self.seq),
            d // self.seq % 2,
            part // (2 * self.t),
            part // 2 % self.t,
            part % 2,
        )

    def index(self, x, c, z, r, y):
        return (x * 2 + c) * self.seq + (z * self.t + r) * 2 + y

    def send(self, value, move):
        perm = [(d, self.index(*move(*self.coords(d)))) for d in range(self.count)]
        return lax.ppermute(value, AXES, perm)

    def over_c(self, value):
        return self.send(value, lambda x, c, z, r, y: (x, 1 - c, z, r, y))

    def over_x(self, value):
        return self.send(value, lambda x, c, z, r, y: (1 - x, c, z, r, y))

    def over_y(self, value):
        return self.send(value, lambda x, c, z, r, y: (x, c, z, r, 1 - y))

    def over_z(self, value, step):
        return self.send(value, lambda x, c, z, r, y: (x, c, (z + step) % 4, r, y))

    def xor_z(self, value, bit):
        return self.send(value, lambda x, c, z, r, y: (x, c, z ^ bit, r, y))

    def over_r(self, value, step):
        return self.send(value, lambda x, c, z, r, y: (x, c, z, (r + step) % self.t, y))

    def regroup(self, value, step):
        return self.send(value, lambda x, c, z, r, y: (x, y, (z + step) % 4, r, c))


def place(scalars, sources, shapes, copies):
    def kernel(s_ref, *refs):
        ins = refs[: len(sources)]
        outs = refs[len(sources) : len(sources) + len(shapes)]
        sems = refs[-1]
        started = []
        for i, (source, at, target, to) in enumerate(copies):
            copy = pltpu.make_async_copy(
                ins[source].at[at(s_ref)], outs[target].at[to(s_ref)], sems.at[i]
            )
            copy.start()
            started.append(copy)
        for copy in started:
            copy.wait()

    moved = sum(source.size * 2 for source in sources)
    return pl.pallas_call(
        kernel,
        out_shape=[jax.ShapeDtypeStruct(shape, BF) for shape in shapes],
        in_specs=[pl.BlockSpec(memory_space=pltpu.SMEM)]
        + [pl.BlockSpec(memory_space=pl.ANY)] * len(sources),
        out_specs=[pl.BlockSpec(memory_space=pl.ANY)] * len(shapes),
        scratch_shapes=[pltpu.SemaphoreType.DMA((len(copies),))],
        cost_estimate=pl.CostEstimate(flops=0, bytes_accessed=2 * moved, transcendentals=0),
    )(scalars, *sources)


ALL = slice(None)


def everything(s):
    return (ALL,)


def gather_xyz(g, scal, shard, widths):
    kinds, rows, _ = shard.shape
    other = g.over_x(shard)
    (pair,) = place(
        scal,
        [shard, other],
        [(2,) + shard.shape],
        [
            (0, everything, 0, lambda s: (s[0],)),
            (1, everything, 0, lambda s: (1 - s[0],)),
        ],
    )
    bufs = []
    for dy, block in ((0, pair), (1, g.over_y(pair))):
        low, high = g.over_z(block, 1), g.over_z(block, -1)
        far = g.over_z(low, 1) if dy == 0 else g.over_z(high, -1)
        bufs += [(block, 0, dy), (high, 1, dy), (far, 2, dy), (low, 3, dy)]
    shapes = [(2, kinds, 4, 2, rows, width) for width in widths]
    copies = []
    for i, (_, dz, dy) in enumerate(bufs):
        start = 0
        for o, width in enumerate(widths):
            copies.append(
                (
                    i,
                    lambda s, start=start, width=width: (ALL, ALL, ALL, pl.ds(start, width)),
                    o,
                    lambda s, dz=dz, dy=dy: (ALL, ALL, (s[2] + dz) & 3, s[3] ^ dy),
                )
            )
            start += width
    return place(scal, [b[0] for b in bufs], shapes, copies)


def gather_yxz(g, scal, shard, sections):
    _, rows, _ = shard.shape
    other = g.over_y(shard)
    (pair,) = place(
        scal,
        [shard, other],
        [(2,) + shard.shape],
        [
            (0, everything, 0, lambda s: (s[3],)),
            (1, everything, 0, lambda s: (1 - s[3],)),
        ],
    )
    bufs = []
    for dx, block in ((0, pair), (1, g.over_x(pair))):
        low, high = g.over_z(block, 1), g.over_z(block, -1)
        far = g.over_z(low, 1) if dx == 0 else g.over_z(high, -1)
        bufs += [(block, 0, dx), (high, 1, dx), (far, 2, dx), (low, 3, dx)]
    shapes = [(2, kinds, 4, 2, rows, width) for width, kinds in sections]
    copies = []
    for i, (_, dz, dx) in enumerate(bufs):
        start = 0
        for o, (width, kinds) in enumerate(sections):
            for kind in range(kinds):
                copies.append(
                    (
                        i,
                        lambda s, start=start, width=width: (ALL, 0, ALL, pl.ds(start, width)),
                        o,
                        lambda s, dz=dz, dx=dx, kind=kind: (s[0] ^ dx, kind, (s[2] + dz) & 3),
                    )
                )
                start += width
    return place(scal, [b[0] for b in bufs], shapes, copies)


def gather_z_first(g, scal, shard, order, step):
    kinds, rows, width = shard.shape
    low, high = g.over_z(shard, 1), g.over_z(shard, -1)
    far = g.over_z(low, 1) if step == 1 else g.over_z(high, -1)
    (line,) = place(
        scal,
        [shard, high, far, low],
        [(4,) + shard.shape],
        [(i, everything, 0, lambda s, i=i: ((s[2] + i) & 3,)) for i in range(4)],
    )
    bufs = []
    if order == "zxy":
        for dx, block in ((0, line), (1, g.over_x(line))):
            bufs += [(block, dx, 0), (g.over_y(block), dx, 1)]
    else:
        for dy, block in ((0, line), (1, g.over_y(line))):
            bufs += [(block, 0, dy), (g.over_x(block), 1, dy)]
    copies = []
    for i, (_, dx, dy) in enumerate(bufs):
        for kind in range(kinds):
            copies.append(
                (
                    i,
                    lambda s, kind=kind: (ALL, kind),
                    0,
                    lambda s, dx=dx, dy=dy, kind=kind: (s[0] ^ dx, kind, ALL, s[3] ^ dy),
                )
            )
    return place(scal, [b[0] for b in bufs], [(2, kinds, 4, 2, rows, width)], copies)[0]


def plus(*terms):
    total = terms[0].astype(F32)
    for term in terms[1:]:
        total = total + term.astype(F32)
    return total.astype(BF)


def reduce_z(g, part, dim, step):
    ahead = g.over_z(part((g.z + 2) & 3), step)
    near = g.over_z(plus(part((g.z + step) & 3), ahead), step)
    back = g.over_z(part((g.z - step) & 3), -step)
    return near, back


def reduce_pair(g, terms, dim, mine, over):
    gone = plus(*[pick(term, dim, 1 - mine) for term in terms])
    return [pick(term, dim, mine) for term in terms] + [over(gone)]


def scatter(g, grad, order, step):
    terms = [grad]
    dims = ["x", "k", "z", "y"]
    for axis in order:
        dim = dims.index(axis)
        if axis == "z":
            if len(terms) > 1:
                terms = [plus(*terms)]
            whole = terms[0]
            near, back = reduce_z(g, lambda i: pick(whole, dim, i), dim, step)
            terms = [pick(whole, dim, g.z), near, back]
        elif axis == "x":
            terms = reduce_pair(g, terms, dim, g.x, g.over_x)
        else:
            terms = reduce_pair(g, terms, dim, g.y, g.over_y)
        dims.pop(dim)
    return terms


def attn_fwd_kernel(z_ref, q_ref, k_ref, v_ref, o_ref, *, scale):
    z = z_ref[0]
    size = q_ref.shape[0] // 4
    starts = [pl.multiple_of(((z - h) & 3) * size, size) for h in range(4)]
    keys = jnp.concatenate([k_ref[pl.ds(s, size), :] for s in starts], 0)
    values = jnp.concatenate([v_ref[pl.ds(s, size), :] for s in starts], 0)
    first = lax.broadcasted_iota(jnp.int32, (size, 128), 1) < 64
    for j in range(4):
        span = (j + 1) * size
        q = q_ref[pl.ds(starts[j], size), :]
        row = lax.broadcasted_iota(jnp.int32, (size, span), 0) + j * size
        seen = lax.broadcasted_iota(jnp.int32, (size, span), 1) <= row
        outs = []
        for head in range(2):
            lanes = first if head == 0 else ~first
            qh = jnp.where(lanes, q, jnp.zeros_like(q))
            s = mm_cols(qh, keys[:span]) * scale
            s = jnp.where(seen, s, NEG)
            p = jnp.exp(s - jnp.max(s, -1, keepdims=True))
            total = jnp.sum(p, -1, keepdims=True)
            outs.append(mm(p.astype(BF), values[:span]) / total)
        o_ref[pl.ds(starts[j], size), :] = jnp.where(first, outs[0], outs[1]).astype(BF)


def attn_fwd(z, qkv, scale):
    rows, width = qkv.shape
    pairs = width // 3 // 128
    return pl.pallas_call(
        functools.partial(attn_fwd_kernel, scale=scale),
        grid=(pairs,),
        out_shape=jax.ShapeDtypeStruct((rows, width // 3), BF),
        in_specs=[
            pl.BlockSpec(memory_space=pltpu.SMEM),
            pl.BlockSpec((rows, 128), lambda i: (0, i)),
            pl.BlockSpec((rows, 128), lambda i: (0, pairs + i)),
            pl.BlockSpec((rows, 128), lambda i: (0, 2 * pairs + i)),
        ],
        out_specs=pl.BlockSpec((rows, 128), lambda i: (0, i)),
        compiler_params=pltpu.CompilerParams(vmem_limit_bytes=32 * 2**20),
        cost_estimate=pl.CostEstimate(
            flops=4 * rows * rows * width // 3,
            bytes_accessed=rows * width * 3,
            transcendentals=rows * rows * pairs * 2,
        ),
    )(z, qkv, qkv, qkv)


def attn_bwd_kernel(z_ref, q_ref, k_ref, v_ref, g_ref, d_ref, dk_ref, dv_ref, *, scale, pairs):
    z = z_ref[0]
    at = pl.program_id(0)
    size = q_ref.shape[0] // 4
    starts = [pl.multiple_of(((z - h) & 3) * size, size) for h in range(4)]
    keys = jnp.concatenate([k_ref[pl.ds(s, size), :] for s in starts], 0)
    values = jnp.concatenate([v_ref[pl.ds(s, size), :] for s in starts], 0)
    first = lax.broadcasted_iota(jnp.int32, (size, 128), 1) < 64
    dk_ref[...] = jnp.zeros_like(dk_ref)
    dv_ref[...] = jnp.zeros_like(dv_ref)
    for j in range(4):
        span = (j + 1) * size
        q = q_ref[pl.ds(starts[j], size), :]
        grad = g_ref[pl.ds(starts[j], size), :]
        row = lax.broadcasted_iota(jnp.int32, (size, span), 0) + j * size
        seen = lax.broadcasted_iota(jnp.int32, (size, span), 1) <= row
        outs = []
        for head in range(2):
            lanes = first if head == 0 else ~first
            qh = jnp.where(lanes, q, jnp.zeros_like(q))
            gh = jnp.where(lanes, grad, jnp.zeros_like(grad))
            s = mm_cols(qh, keys[:span]) * scale
            s = jnp.where(seen, s, NEG)
            p = jnp.exp(s - jnp.max(s, -1, keepdims=True))
            p = p / jnp.sum(p, -1, keepdims=True)
            dp = mm_cols(gh, values[:span])
            ds = (p * (dp - jnp.sum(p * dp, -1, keepdims=True))).astype(BF)
            dv_ref[0:span, :] += mm_rows(p.astype(BF), gh)
            dk_ref[0:span, :] += mm_rows(ds, qh)
            outs.append(mm(ds, keys[:span]))
        dq = jnp.where(first, outs[0], outs[1]) * scale
        d_ref[pl.ds(starts[j], size), pl.ds(pl.multiple_of(at * 128, 128), 128)] = dq.astype(BF)
    for j in range(4):
        rows = slice(j * size, (j + 1) * size)
        d_ref[pl.ds(starts[j], size), pl.ds(pl.multiple_of((at + pairs) * 128, 128), 128)] = (
            dk_ref[rows, :] * scale
        ).astype(BF)
        d_ref[pl.ds(starts[j], size), pl.ds(pl.multiple_of((at + 2 * pairs) * 128, 128), 128)] = (
            dv_ref[rows, :].astype(BF)
        )


def attn_bwd(z, qkv, grad, scale):
    rows, width = qkv.shape
    pairs = width // 3 // 128
    return pl.pallas_call(
        functools.partial(attn_bwd_kernel, scale=scale, pairs=pairs),
        grid=(pairs,),
        out_shape=jax.ShapeDtypeStruct((rows, width), BF),
        in_specs=[
            pl.BlockSpec(memory_space=pltpu.SMEM),
            pl.BlockSpec((rows, 128), lambda i: (0, i)),
            pl.BlockSpec((rows, 128), lambda i: (0, pairs + i)),
            pl.BlockSpec((rows, 128), lambda i: (0, 2 * pairs + i)),
            pl.BlockSpec((rows, 128), lambda i: (0, i)),
        ],
        out_specs=pl.BlockSpec((rows, width), lambda i: (0, 0)),
        scratch_shapes=[pltpu.VMEM((rows, 128), F32), pltpu.VMEM((rows, 128), F32)],
        compiler_params=pltpu.CompilerParams(vmem_limit_bytes=32 * 2**20),
        cost_estimate=pl.CostEstimate(
            flops=10 * rows * rows * width // 3,
            bytes_accessed=rows * width * 5,
            transcendentals=rows * rows * pairs * 2,
        ),
    )(z, qkv, qkv, qkv, grad)


def cross_probs(q, keys, lanes, seen, scale):
    qh = jnp.where(lanes, q, jnp.zeros_like(q))
    s = jnp.where(seen, mm_cols(qh, keys) * scale, NEG)
    p = jnp.where(seen, jnp.exp(s - jnp.max(s, -1, keepdims=True)), 0.0)
    return qh, p / jnp.sum(p, -1, keepdims=True)


def cross_fwd_kernel(cap_ref, seg_ref, q_ref, k_ref, v_ref, o_ref, *, scale):
    seen = seg_ref[...] == cap_ref[0]
    q, keys, values = q_ref[...], k_ref[...], v_ref[...]
    first = lax.broadcasted_iota(jnp.int32, q.shape, 1) < 64
    outs = []
    for head in range(2):
        _, p = cross_probs(q, keys, first if head == 0 else ~first, seen, scale)
        outs.append(mm(p.astype(BF), values))
    o_ref[...] = jnp.where(first, outs[0], outs[1]).astype(BF)


def cross_fwd(cap, seg, cq, ckv, scale):
    rows, width = cq.shape
    text = ckv.shape[0]
    pairs = width // 128
    return pl.pallas_call(
        functools.partial(cross_fwd_kernel, scale=scale),
        grid=(pairs,),
        out_shape=jax.ShapeDtypeStruct((rows, width), BF),
        in_specs=[
            pl.BlockSpec(memory_space=pltpu.SMEM),
            pl.BlockSpec((1, text), lambda i: (0, 0)),
            pl.BlockSpec((rows, 128), lambda i: (0, i)),
            pl.BlockSpec((text, 128), lambda i: (0, i)),
            pl.BlockSpec((text, 128), lambda i: (0, pairs + i)),
        ],
        out_specs=pl.BlockSpec((rows, 128), lambda i: (0, i)),
        compiler_params=pltpu.CompilerParams(vmem_limit_bytes=32 * 2**20),
        cost_estimate=pl.CostEstimate(
            flops=4 * rows * text * width,
            bytes_accessed=rows * width * 4,
            transcendentals=rows * text * pairs * 2,
        ),
    )(cap, seg, cq, ckv, ckv)


def cross_bwd_kernel(cap_ref, seg_ref, q_ref, k_ref, v_ref, g_ref, dq_ref, dk_ref, dv_ref, *, scale):
    seen = seg_ref[...] == cap_ref[0]
    q, keys, values, grad = q_ref[...], k_ref[...], v_ref[...], g_ref[...]
    first = lax.broadcasted_iota(jnp.int32, q.shape, 1) < 64
    outs = []
    for head in range(2):
        lanes = first if head == 0 else ~first
        qh, p = cross_probs(q, keys, lanes, seen, scale)
        gh = jnp.where(lanes, grad, jnp.zeros_like(grad))
        dp = mm_cols(gh, values)
        ds = (p * (dp - jnp.sum(p * dp, -1, keepdims=True))).astype(BF)
        dv = mm_rows(p.astype(BF), gh)
        dk = mm_rows(ds, qh) * scale
        if head == 0:
            dv_ref[...] = dv
            dk_ref[...] = dk
        else:
            dv_ref[...] += dv
            dk_ref[...] += dk
        outs.append(mm(ds, keys))
    dq_ref[...] = (jnp.where(first, outs[0], outs[1]) * scale).astype(BF)


def cross_bwd(cap, seg, cq, ckv, grad, scale):
    rows, width = cq.shape
    text = ckv.shape[0]
    pairs = width // 128
    return pl.pallas_call(
        functools.partial(cross_bwd_kernel, scale=scale),
        grid=(pairs,),
        out_shape=[
            jax.ShapeDtypeStruct((rows, width), BF),
            jax.ShapeDtypeStruct((text, width), F32),
            jax.ShapeDtypeStruct((text, width), F32),
        ],
        in_specs=[
            pl.BlockSpec(memory_space=pltpu.SMEM),
            pl.BlockSpec((1, text), lambda i: (0, 0)),
            pl.BlockSpec((rows, 128), lambda i: (0, i)),
            pl.BlockSpec((text, 128), lambda i: (0, i)),
            pl.BlockSpec((text, 128), lambda i: (0, pairs + i)),
            pl.BlockSpec((rows, 128), lambda i: (0, i)),
        ],
        out_specs=[
            pl.BlockSpec((rows, 128), lambda i: (0, i)),
            pl.BlockSpec((text, 128), lambda i: (0, i)),
            pl.BlockSpec((text, 128), lambda i: (0, i)),
        ],
        compiler_params=pltpu.CompilerParams(vmem_limit_bytes=32 * 2**20),
        cost_estimate=pl.CostEstimate(
            flops=10 * rows * text * width,
            bytes_accessed=rows * width * 6,
            transcendentals=rows * text * pairs * 2,
        ),
    )(cap, seg, cq, ckv, ckv, grad)


def long_masks(g, rows):
    slot = jnp.arange(rows, dtype=jnp.int32) // (2 * STRIPE)
    rest = jnp.arange(rows, dtype=jnp.int32) % (2 * STRIPE)

    def positions(r):
        return (((g.z - slot) % 4) * g.t + r) * (2 * STRIPE) + rest

    key_pos = jnp.concatenate([positions((g.r - q) % g.t) for q in range(g.t)])
    return key_pos[None, :] <= positions(g.r)[:, None]


def long_gather(g, value):
    return jnp.concatenate([value] + [g.over_r(value, q) for q in range(1, g.t)], 0)


def long_fwd(g, qkv, scale):
    rows, width = qkv.shape
    head = 64
    heads = width // 3 // head
    keyval = long_gather(g, qkv[:, width // 3 :])
    q = qkv[:, : width // 3].reshape(rows, heads, head)
    k = keyval[:, : width // 3].reshape(-1, heads, head)
    v = keyval[:, width // 3 :].reshape(-1, heads, head)
    seen = long_masks(g, rows)[None]
    s = jnp.einsum("qhd,khd->hqk", q, k, preferred_element_type=F32) * scale
    s = jnp.where(seen, s, NEG)
    p = jnp.exp(s - jnp.max(s, -1, keepdims=True))
    p = p / jnp.sum(p, -1, keepdims=True)
    out = jnp.einsum("hqk,khd->qhd", p.astype(BF), v, preferred_element_type=F32)
    return out.reshape(rows, width // 3).astype(BF), (q, k, v, p)


def long_bwd(g, saved, grad, scale):
    q, k, v, p = saved
    rows, heads, head = q.shape
    width = heads * head
    grad = grad.reshape(rows, heads, head)
    dv = jnp.einsum("hqk,qhd->khd", p.astype(BF), grad, preferred_element_type=F32)
    dp = jnp.einsum("qhd,khd->hqk", grad, v, preferred_element_type=F32)
    ds = (p * (dp - jnp.sum(p * dp, -1, keepdims=True))).astype(BF)
    dq = jnp.einsum("hqk,khd->qhd", ds, k, preferred_element_type=F32) * scale
    dk = jnp.einsum("hqk,qhd->khd", ds, q, preferred_element_type=F32) * scale
    both = jnp.concatenate([dk.reshape(-1, width), dv.reshape(-1, width)], 1)
    both = both.reshape(g.t, rows, 2 * width)
    total = both[0]
    for step in range(1, g.t):
        total = total + g.over_r(both[step], -step)
    return jnp.concatenate([dq.reshape(rows, width).astype(BF), total.astype(BF)], 1)


def normed(values):
    center = values - jnp.mean(values, -1, keepdims=True)
    spread = lax.rsqrt(jnp.mean(center * center, -1, keepdims=True) + EPS)
    return center * spread, spread


def norm_back(unit, spread, gain, grad):
    f = grad * gain
    added = spread * (
        f - jnp.mean(f, -1, keepdims=True) - unit * jnp.mean(f * unit, -1, keepdims=True)
    )
    return added, jnp.sum(grad * unit, 0), jnp.sum(grad, 0)


def column_halves(weight, groups, mine):
    rows, width = weight.shape
    parts = weight.reshape(rows, groups, 2, width // groups // 2)
    return (
        pick(parts, 2, mine).reshape(rows, width // 2),
        pick(parts, 2, 1 - mine).reshape(rows, width // 2),
    )


def two(g, mine, other, axis):
    first = jnp.where(g.c == 0, mine, other)
    second = jnp.where(g.c == 0, other, mine)
    return jnp.stack([first, second], axis)


def gather_fast(g, weights):
    gains, shifts, w_qkv, w_out, w_cq, w_ckv, w_co, w_up, w_down = weights
    scal = jnp.stack([g.x, g.c, g.z, g.y]).astype(jnp.int32)
    small = jnp.concatenate([gains, shifts], 0).T
    small = jnp.pad(small, ((0, 0), (0, 128 - small.shape[1])))
    mine, other = column_halves(w_qkv, 6, g.c)
    got = g.over_c(jnp.concatenate([other, small], 1))
    qkv = two(g, jnp.concatenate([mine, small], 1), got, 0)
    cq_mine, cq_other = column_halves(w_cq, 2, g.c)
    ckv_mine, ckv_other = column_halves(w_ckv, 4, g.c)
    up_mine, up_other = column_halves(w_up, 2, g.c)
    n_cq, n_ckv = cq_mine.shape[1], ckv_mine.shape[1]
    got = g.over_c(jnp.concatenate([cq_other, ckv_other, up_other], 1))
    cq = two(g, cq_mine, got[:, :n_cq], 0)
    ckv = two(g, ckv_mine, got[:, n_cq : n_cq + n_ckv], 0)
    up = two(g, up_mine, got[:, n_cq + n_ckv :], 0)
    misc = jnp.concatenate([w_out, w_co, cq[0], cq[1], ckv[0], ckv[1]], 1)[None]
    depth = w_out.shape[1]
    qkv_all, small_all = gather_xyz(g, scal, qkv, [mine.shape[1], 128])
    out_all, co_all, cq_all, ckv_all = gather_yxz(
        g, scal, misc, [(depth, 1), (depth, 1), (n_cq, 2), (n_ckv, 2)]
    )
    up_all = gather_z_first(g, scal, up, "zxy", 1)
    down_all = gather_z_first(g, scal, w_down[None], "zyx", -1)
    small_all = small_all.reshape(-1, 128)[:, :6].astype(F32).T

    def flat(array):
        return array.reshape(-1, array.shape[-1])

    return (small_all,) + tuple(
        flat(a) for a in (qkv_all, out_all, cq_all, ckv_all, co_all, up_all, down_all)
    )


def gather_plain(g, weights):
    gains, shifts, w_qkv, w_out, w_cq, w_ckv, w_co, w_up, w_down = weights
    small = lax.all_gather(jnp.concatenate([gains, shifts], 0), AXES, axis=1, tiled=True)

    def columns(weight, groups):
        whole = lax.all_gather(weight, AXES, axis=0, tiled=True)
        return column_halves(whole, groups, g.c)[0]

    def rows(weight):
        whole = lax.all_gather(weight, AXES, axis=0, tiled=True)
        parts = whole.reshape(2, 2, whole.shape[0] // 4, whole.shape[1])
        return pick(parts, 1, g.c).reshape(whole.shape[0] // 2, whole.shape[1])

    return (
        small.astype(F32),
        columns(w_qkv, 6),
        rows(w_out),
        columns(w_cq, 2),
        columns(w_ckv, 4),
        rows(w_co),
        columns(w_up, 2),
        rows(w_down),
    )


def join_columns(g, keep, got, groups):
    rows, width = keep.shape
    block = width // groups
    parts = two(g, keep.reshape(rows, groups, block), got.reshape(rows, groups, block), 2)
    return parts.reshape(rows, 2 * width)


def scatter_columns_plain(g, grad, groups):
    rows, width = grad.shape
    whole = join_columns(g, grad, jnp.zeros_like(grad), groups)
    return lax.psum_scatter(whole, AXES, scatter_dimension=0, tiled=True)


def scatter_rows_plain(g, grad):
    rows, width = grad.shape
    parts = grad.reshape(2, rows // 2, width)
    whole = two(g, parts, jnp.zeros_like(parts), 1).reshape(2 * rows, width)
    return lax.psum_scatter(whole, AXES, scatter_dimension=0, tiled=True)


def scatter_columns_fast(g, grad, rows, groups, order, step):
    width = grad.shape[1]
    terms = scatter(g, grad.astype(BF).reshape(2, 2, 4, 2, rows, width), order, step)
    gone = plus(*[pick(term, 0, 1 - g.c) for term in terms])
    got = g.over_c(gone)
    keep = sum(pick(term, 0, g.c).astype(F32) for term in terms)
    return join_columns(g, keep, got.astype(F32), groups)


def scatter_rows_fast(g, grad, rows, order, step):
    width = grad.shape[1]
    terms = scatter(g, grad.astype(BF).reshape(2, 1, 4, 2, rows, width), order, step)
    return sum(term[0].astype(F32) for term in terms)


def chip_sum(g, value):
    value = plus32(value, g.xor_z(value, 1))
    value = plus32(value, g.xor_z(value, 2))
    value = plus32(value, g.over_x(value))
    return plus32(value, g.over_y(value))


def plus32(a, b):
    return (a.astype(F32) + b.astype(F32)).astype(a.dtype)


def both_cores(g, part):
    low = part.astype(BF)
    return low.astype(F32) + g.over_c(low).astype(F32)


def local(
    tokens,
    text_states,
    image_ids,
    text_segments,
    image_caption,
    norm_gains,
    norm_shifts,
    self_qkv,
    self_out,
    cross_query,
    cross_keyval,
    cross_out,
    mlp_up,
    mlp_down,
    cotangent,
    *,
    dp,
    seq,
):
    g = Grid(dp, seq)
    fast = g.t == 1
    depth = tokens.shape[-1]
    scale = (depth // H) ** (-0.5)
    weights = (
        norm_gains,
        norm_shifts,
        self_qkv,
        self_out,
        cross_query,
        cross_keyval,
        cross_out,
        mlp_up,
        mlp_down,
    )

    start = image_ids[:, 0] & 1
    both = jnp.stack([tokens, cotangent], 2).reshape(4, STRIPE, 2 * depth)
    received = []
    for step in range(4):
        j = (g.z + step) & 3
        half = (j & 1) ^ start[j >> 1]
        received.append(g.regroup(pick(both, 0, (j >> 1) * 2 + half), step))
    mine = jnp.stack(received)
    held = two(g, mine, g.over_c(mine), 1).reshape(8 * STRIPE, 2, depth)
    resid = held[:, 0].astype(F32)
    cot = held[:, 1]

    (small, w_qkv, w_out, w_cq, w_ckv, w_co, w_up, w_down) = (
        gather_fast(g, weights) if fast else gather_plain(g, weights)
    )
    gain, shift = small[:3], small[3:]

    image = (g.x * 2 + g.y) * 2 + (g.z & 1)
    cap = image_caption[g.z >> 1, image].reshape(1)
    seg = text_segments.reshape(1, -1)
    slot = g.z.reshape(1).astype(jnp.int32)

    unit_one, spread_one = normed(resid)
    n_one = (unit_one * gain[0] + shift[0]).astype(BF)
    qkv = mm(n_one, w_qkv).astype(BF)
    if fast:
        attended = attn_fwd(slot, qkv, scale)
    else:
        attended, saved = long_fwd(g, qkv, scale)
    hidden_one = resid + both_cores(g, mm(attended, w_out))
    unit_two, spread_two = normed(hidden_one)
    n_two = (unit_two * gain[1] + shift[1]).astype(BF)
    cq = mm(n_two, w_cq).astype(BF)
    ckv = mm(text_states, w_ckv).astype(BF)
    crossed = cross_fwd(cap, seg, cq, ckv, scale)
    hidden_two = hidden_one + both_cores(g, mm(crossed, w_co))
    unit_three, spread_three = normed(hidden_two)
    n_three = (unit_three * gain[2] + shift[2]).astype(BF)
    up = mm(n_three, w_up)
    inner = jnp.tanh(GELU_C * (up + 0.044715 * up * up * up))
    act = (0.5 * up * (1.0 + inner)).astype(BF)

    def halves(value):
        parts = value.reshape(4, 2, STRIPE, value.shape[-1])
        return pick(parts, 1, g.c), pick(parts, 1, 1 - g.c)

    down = mm(act, w_down)
    keep, gone = halves(down)
    out = (halves(hidden_two)[0] + keep + g.over_c(gone.astype(BF)).astype(F32)).astype(BF)

    grad_down = mm_rows(act, cot)
    slope = 0.5 * (1.0 + inner) + 0.5 * up * (1.0 - inner * inner) * GELU_C * (
        1.0 + 3 * 0.044715 * up * up
    )
    d_up = (mm_cols(cot, w_down) * slope).astype(BF)
    grad_up = mm_rows(n_three, d_up)
    added, gain_three, shift_three = norm_back(
        unit_three, spread_three, gain[2], both_cores(g, mm_cols(d_up, w_up))
    )
    g_two = cot.astype(F32) + added
    d_cross = g_two.astype(BF)
    grad_co = mm_rows(crossed, d_cross)
    d_crossed = mm_cols(d_cross, w_co).astype(BF)
    d_cq, d_ck, d_cv = cross_bwd(cap, seg, cq, ckv, d_crossed, scale)
    grad_cq = mm_rows(n_two, d_cq)
    added, gain_two, shift_two = norm_back(
        unit_two, spread_two, gain[1], both_cores(g, mm_cols(d_cq, w_cq))
    )
    g_one = g_two + added
    d_self = g_one.astype(BF)
    grad_out = mm_rows(attended, d_self)
    d_att = mm_cols(d_self, w_out).astype(BF)
    d_qkv = attn_bwd(slot, qkv, d_att, scale) if fast else long_bwd(g, saved, d_att, scale)
    grad_qkv = mm_rows(n_one, d_qkv)
    added, gain_one, shift_one = norm_back(
        unit_one, spread_one, gain[0], both_cores(g, mm_cols(d_qkv, w_qkv))
    )
    grad_in = (g_one + added).astype(BF)

    def home(mine):
        back = jnp.stack([g.regroup(mine[step], -step) for step in range(4)])
        order = []
        for block in range(4):
            j = (block & 2) + ((block & 1) ^ start[block >> 1])
            order.append(pick(back, 0, (j - g.z) & 3))
        return jnp.stack(order).reshape(2, 2 * STRIPE, depth)

    output = home(out)
    grad_tokens = home(halves(grad_in)[0]).astype(F32)

    d_ckv = jnp.concatenate([d_ck, d_cv], 1)
    norms = jnp.stack([gain_one, gain_two, gain_three, shift_one, shift_two, shift_three])
    if fast:
        d_ckv = chip_sum(g, d_ckv.astype(BF))
        norms = chip_sum(g, norms)
        d_ckv_whole = join_columns(g, d_ckv, g.over_c(d_ckv), 4)
    else:
        whole = join_columns(g, d_ckv, jnp.zeros_like(d_ckv), 4)
        d_ckv_whole = lax.psum(whole, AXES).astype(BF)
        d_ckv = column_halves(d_ckv_whole, 4, g.c)[0]
        norms = lax.psum(norms, AXES) * 0.5
    part = mm_cols(d_ckv, w_ckv)
    grad_text = part + g.over_c(part)
    share = depth // g.count
    text_cols = lax.dynamic_slice_in_dim(text_states, g.me * share, share, 1)
    grad_ckv = mm_rows(text_cols, d_ckv_whole)
    norms = lax.dynamic_slice_in_dim(norms, g.me * share, share, 1)

    if fast:
        grad_down = scatter_rows_fast(g, grad_down, mlp_down.shape[0], "yxz", 1)
        grad_up = scatter_columns_fast(g, grad_up, share, 2, "xyz", -1)
        grad_co = scatter_rows_fast(g, grad_co, share, "zxy", 1)
        grad_cq = scatter_columns_fast(g, grad_cq, share, 2, "zxy", -1)
        grad_out = scatter_rows_fast(g, grad_out, share, "zxy", 1)
        grad_qkv = scatter_columns_fast(g, grad_qkv, share, 6, "zyx", -1)
    else:
        grad_down = scatter_rows_plain(g, grad_down)
        grad_up = scatter_columns_plain(g, grad_up, 2)
        grad_co = scatter_rows_plain(g, grad_co)
        grad_cq = scatter_columns_plain(g, grad_cq, 2)
        grad_out = scatter_rows_plain(g, grad_out)
        grad_qkv = scatter_columns_plain(g, grad_qkv, 6)
    return (
        output,
        grad_tokens,
        grad_text,
        norms[:3],
        norms[3:5],
        grad_qkv,
        grad_out,
        grad_cq,
        grad_ckv,
        grad_co,
        grad_up,
        grad_down,
        norms[5],
    )


def solution(mesh):
    both = ("dp", "seq")
    rows = P(both, None)
    in_specs = (
        P(None, both, None),
        P(),
        P(None, both),
        P(),
        P(),
        P(None, both),
        P(None, both),
        rows,
        rows,
        rows,
        rows,
        rows,
        rows,
        rows,
        P(None, both, None),
    )
    out_specs = (
        P(None, both, None),
        P(None, both, None),
        P(),
        P(None, both),
        P(None, both),
        rows,
        rows,
        rows,
        rows,
        rows,
        rows,
        rows,
        P(both),
    )
    body = functools.partial(local, dp=mesh.shape["dp"], seq=mesh.shape["seq"])
    return jax.shard_map(body, mesh=mesh, in_specs=in_specs, out_specs=out_specs, check_vma=False)
```

time: 2550 us -> 1180 us (0.46)
  waiting for transfers between devices: 2000 us -> 166 us
  Pallas kernels: 0 us -> 665 us
  blocking collectives: 220 us -> 0 us
  starting transfers between devices: 1.42 us -> 135 us
  matrix products: 168 us -> 42.2 us
  other arithmetic: 22.7 us -> 94.8 us
  local copies, waits for them, and re-layouts: 92.6 us -> 55.1 us
    reduce_scatter x8 -> x0, waiting for transfers between devices: 1450 us -> none  [the longest x1 360 us: local(): lax.psum_scatter(grads[7], ('dp', 'seq'), scatter_dimension=0, tiled=True)]
    pallas_call x0 -> x12, Pallas kernels: none -> 665 us  [the longest x8 627 us: place(): pl.pallas_call(kernel, out_shape=[jax.ShapeDtypeStruct(shape, BF) for sha...]
    all_gather x11 -> x0, waiting for transfers between devices: 408 us -> none  [the longest x2 91 us: self_forward(): value_piece = lax.all_gather(values, 'seq', axis=0, tiled=True)]
    all_gather x4 -> x0, blocking collectives: 169 us -> none  [the longest x1 70.2 us: local(): lax.all_gather(local_weights[1], ('dp', 'seq'), axis=1, tiled=True)]
    ppermute x0 -> x92, waiting for transfers between devices: none -> 166 us  [send(): return lax.ppermute(value, AXES, perm)]
    unnamed x23 -> x0, waiting for transfers between devices: 143 us -> none
    ppermute x0 -> x92, starting transfers between devices: none -> 135 us  [send(): return lax.ppermute(value, AXES, perm)]
    dot_general x63 -> x21, matrix products: 165 us -> 42.2 us  [the longest x7 17 us: mm(): return jnp.dot(left, right, preferred_element_type=F32)]
  transfers between devices with their start and end apart: 21 -> 92, of which waited for: 18 -> 30; matrix products, arithmetic and copies ran while one was open for 8% -> 14% of each run, Pallas kernels for 0% -> 57%
where the time goes in v1:
time: 1180 us; the launch traced here: 1170 us
  Pallas kernels  665 us (56%)
  waiting for transfers between devices  166 us (14%)
  starting transfers between devices  135 us (11%)
  other arithmetic  94.8 us (8%)
  local copies, waits for them, and re-layouts  55.1 us (5%)
  matrix products  42.2 us (4%)
    pallas_call x8, Pallas kernels, place(): pl.pallas_call(kernel, out_shape=[jax.ShapeDtypeStruct(shape, BF) for sha...  627 us
    ppermute x92, waiting for transfers between devices, send(): return lax.ppermute(value, AXES, perm)  166 us
    ppermute x92, starting transfers between devices, send(): return lax.ppermute(value, AXES, perm)  135 us
    convert_element_type x21, other arithmetic, plus(): return total.astype(BF)  32.7 us
  transfers between devices with their start and end apart: 92, of which 30 were waited for; matrix products, arithmetic and copies ran while one was open for 14% of the time, Pallas kernels for 57%

profile of v1, /device:TPU:0, one launch (start us, length us, event | category | flops | bytes accessed | tf_op | source)
XLA Modules:
  0.0 1165.7 jit_solution(1527804984737646674)
XLA Ops:
  32.9 15.3 %collective-permute-done.2 = bf16[64,2048]{1,0:T(8,128)(2,1)S(1)} collective-permute-done((bf16[64,2048]{1,0:T(8,128)(2,1)S(1)}, bf16[64,2048]{1,0:T(8,128)(2,1)S(1)}, u32[]{:S(2)}, u32[]{:S(2)}) %collective-permute-start.2) | collective-permute-done | bytes 262176 | tf_op jit(solution)/shard_map/ppermute | solution.py:64
  49.2 6.4 collective-permute-start.4
  58.0 3.5 collective-permute-start.32
  61.5 14.7 %shard_map.246.refs_0_ = bf16[2,2,32,1664]{3,2,1,0:T(8,128)(2,1)} custom-call(s32[4]{0:T(128)} %pad_add_fusion.s_ref, bf16[2,32,1664]{2,1,0:T(8,128)(2,1)} %copy-done.36, bf16[2,32,1664]{2,1,0:T(8,128)(2,1)} %collective-permute-done.6.refs_1_), custom_call_target="tpu_custom_call" | custom-call | bytes 851968 | tf_op jit(solution)/shard_map/pallas_call | solution.py:104
  81.3 33.6 %shard_map.254.refs_0_ = bf16[4,1,128,1024]{3,2,1,0:T(8,128)(2,1)} custom-call(s32[4]{0:T(128)} %pad_add_fusion.s_ref, bf16[1,128,1024]{2,1,0:T(8,128)(2,1)} %bitcast.48.refs_0_, bf16[1,128,1024]{2,1,0:T(8,128)(2,1)} %collective-permute-done.31.refs_1_, bf16[1,128,1024]{2,1,0:T(8,128)(2,1)} %collective-permute-done.32.refs_2_, ...), custom_call_target="tpu_custom_call" | custom-call | bytes 2097152 | tf_op jit(solution)/shard_map/pallas_call | solution.py:104
  115.0 21.6 %shard_map.249.refs_0_ = bf16[2,1,32,5120]{3,2,1,0:T(8,128)(2,1)} custom-call(s32[4]{0:T(128)} %pad_add_fusion.s_ref, bf16[1,32,5120]{2,1,0:T(8,128)(2,1)} %bitcast.583, bf16[1,32,5120]{2,1,0:T(8,128)(2,1)} %collective-permute-done.15.refs_1_), custom_call_target="tpu_custom_call" | custom-call | bytes 1310720 | tf_op jit(solution)/shard_map/pallas_call | solution.py:104
  136.6 3.9 collective-permute-start.7
  142.0 33.6 %shard_map.252.refs_0_ = bf16[4,2,32,2048]{3,2,1,0:T(8,128)(2,1)} custom-call(s32[4]{0:T(128)} %pad_add_fusion.s_ref, bf16[2,32,2048]{2,1,0:T(8,128)(2,1)} %copy-done.30, bf16[2,32,2048]{2,1,0:T(8,128)(2,1)} %collective-permute-done.25.refs_1_, bf16[2,32,2048]{2,1,0:T(8,128)(2,1)} %collective-permute-done.27.refs_2_, ...), custom_call_target="tpu_custom_call" | custom-call | bytes 2097152 | tf_op jit(solution)/shard_map/pallas_call | solution.py:104
  175.6 3.8 collective-permute-start.11
  182.2 3.3 reshape.1219
  185.5 3.8 fusion.91
  190.3 11.2 collective-permute-done.11.refs_5_
  207.4 6.1 collective-permute-done.13.refs_7_
  213.6 8.9 collective-permute-done.9.refs_2_
  224.5 4.1 collective-permute-done.12.refs_6_
  229.4 105.1 %shard_map.247 = (bf16[2,2,4,2,32,1536]{5,4,3,2,1,0:T(8,128)(2,1)}, bf16[2,2,4,2,32,128]{5,4,3,2,1,0:T(8,128)(2,1)}) custom-call(s32[4]{0:T(128)} %pad_add_fusion.s_ref, bf16[2,2,32,1664]{3,2,1,0:T(8,128)(2,1)} %shard_map.246.refs_0_, bf16[2,2,32,1664]{3,2,1,0:T(8,128)(2,1)} %collective-permute-done.7.refs_1_, bf16[2,2,32,1664]{3,2,1,0:T(8,128)(2,1)} %copy-done.41, ...), custom_call_target="tpu_custom_call" | custom-call | bytes 6815744 | tf_op jit(solution)/shard_map/pallas_call | solution.py:104
  340.1 3.8 convolution_convert_fusion.3.q_ref.k_ref.v_ref
  343.9 9.1 shard_map.248
  353.6 161.0 %shard_map.250 = (bf16[2,1,4,2,32,1024]{5,4,3,2,1,0:T(8,128)(2,1)}, bf16[2,1,4,2,32,1024]{5,4,3,2,1,0:T(8,128)(2,1)}, bf16[2,2,4,2,32,512]{5,4,3,2,1,0:T(8,128)(2,1)}, bf16[2,2,4,2,32,1024]{5,4,3,2,1,0:T(8,128)(2,1)}) custom-call(s32[4]{0:T(128)} %pad_add_fusion.s_ref, bf16[2,1,32,5120]{3,2,1,0:T(8,128)(2,1)} %shard_map.249.refs_0_, ...), custom_call_target="tpu_custom_call" | custom-call | bytes 10485760 | tf_op jit(solution)/shard_map/pallas_call | solution.py:104
  529.5 4.6 shard_map.251
  538.4 6.0 collective-permute-done.34.refs_1_
  544.5 22.1 %collective-permute-done.36.refs_3_ = bf16[4,1,128,1024]{3,2,1,0:T(8,128)(2,1)} collective-permute-done((bf16[4,1,128,1024]{3,2,1,0:T(8,128)(2,1)}, bf16[4,1,128,1024]{3,2,1,0:T(8,128)(2,1)}, u32[]{:S(2)}, u32[]{:S(2)}) %collective-permute-start.36) | collective-permute-done | bytes 1048608 | tf_op jit(solution)/shard_map/ppermute | solution.py:64
  566.6 128.9 %shard_map.255 = bf16[2,1,4,2,128,1024]{5,4,3,2,1,0:T(8,128)(2,1)} custom-call(s32[4]{0:T(128)} %pad_add_fusion.s_ref, bf16[4,1,128,1024]{3,2,1,0:T(8,128)(2,1)} %shard_map.254.refs_0_, bf16[4,1,128,1024]{3,2,1,0:T(8,128)(2,1)} %collective-permute-done.34.refs_1_, bf16[4,1,128,1024]{3,2,1,0:T(8,128)(2,1)} %collective-permute-done.35.refs_2_, ...), custom_call_target="tpu_custom_call" | custom-call | bytes 8388608 | tf_op jit(solution)/shard_map/pallas_call | solution.py:104
  695.5 128.9 %shard_map.253 = bf16[2,2,4,2,32,2048]{5,4,3,2,1,0:T(8,128)(2,1)} custom-call(s32[4]{0:T(128)} %pad_add_fusion.s_ref, bf16[4,2,32,2048]{3,2,1,0:T(8,128)(2,1)} %shard_map.252.refs_0_, bf16[4,2,32,2048]{3,2,1,0:T(8,128)(2,1)} %collective-permute-done.28.refs_1_, bf16[4,2,32,2048]{3,2,1,0:T(8,128)(2,1)} %collective-permute-done.29.refs_2_, ...), custom_call_target="tpu_custom_call" | custom-call | bytes 8388608 | tf_op jit(solution)/shard_map/pallas_call | solution.py:104
  831.3 4.9 fusion.6
  857.4 3.6 collective-permute-start.87
  867.4 6.7 shard_map.256
  874.9 3.9 collective-permute-start.49
  882.2 3.8 collective-permute-start.69
  890.0 6.3 collective-permute-done.69
  903.6 3.7 collective-permute-done.71
  907.3 7.6 collective-permute-start.70
  920.1 11.9 %collective-permute-start.77 = (bf16[2,1,2,32,1024]{4,3,2,1,0:T(8,128)(2,1)}, bf16[2,1,2,32,1024]{4,3,2,1,0:T(8,128)(2,1)}, u32[]{:S(2)}, u32[]{:S(2)}) collective-permute-start(bf16[2,1,2,32,1024]{4,3,2,1,0:T(8,128)(2,1)} %fusion.63), channel_id=1, source_target_pairs={{0,2},{1,3},{2,4},{3,5},{4,6},{5,7},{6,0},{7,1},{8,10},{9,11},{10,... | collective-permute-start | bytes 786440 | tf_op jit(solution)/shard_map/ppermute | solution.py:64
  944.9 5.6 collective-permute-done.79
  951.4 3.3 collective-permute-done.73
  966.1 8.1 collective-permute-done.52
  975.9 3.3 fusion.95
  988.4 17.4 %shard_map.257 = bf16[512,1536]{1,0:T(8,128)(2,1)S(1)} custom-call(s32[1]{0:T(128)} %bitcast.18.z_ref, bf16[512,1536]{1,0:T(8,128)(2,1)S(1)} %convolution_convert_fusion.3.q_ref.k_ref.v_ref, bf16[512,1536]{1,0:T(8,128)(2,1)S(1)} %convolution_convert_fusion.3.q_ref.k_ref.v_ref, bf16[512,1536]{1,0:T(8,128)(2,1)S(1)} %convolution_convert_fusion.3.q_ref.k_ref.v_ref, ...), custom_call_target="tpu_custom_call" | custom-call | flops 1342177280 | bytes 3932160 | tf_op jit(solution)/shard_map/pallas_call | solution.py:352
  1011.1 3.9 collective-permute-start.66
  1022.2 4.2 collective-permute-start.58
  1026.4 3.4 collective-permute-done.65
  1051.5 12.1 %collective-permute-done.60 = bf16[2,2,2,32,1536]{4,3,2,1,0:T(8,128)(2,1)} collective-permute-done((bf16[2,2,2,32,1536]{4,3,2,1,0:T(8,128)(2,1)}, bf16[2,2,2,32,1536]{4,3,2,1,0:T(8,128)(2,1)}, u32[]{:S(2)}, u32[]{:S(2)}) %collective-permute-start.60) | collective-permute-done | bytes 786464 | tf_op jit(solution)/shard_map/ppermute | solution.py:64
  1073.8 6.1 collective-permute-done.54
  1099.6 3.8 collective-permute-start.83
  1115.5 6.8 collective-permute-done.89
  1126.1 7.9 collective-permute-done.84
  1146.2 7.6 collective-permute-done.61
  1156.8 4.5 collective-permute-done.62
  (483 shorter events, 264.3 us)
Async XLA Ops:
  11.0 66.2 %collective-permute-start.33 = (bf16[1,128,1024]{2,1,0:T(8,128)(2,1)}, bf16[1,128,1024]{2,1,0:T(8,128)(2,1)}, u32[]{:S(2)}, u32[]{:S(2)}) collective-permute-start(bf16[1,128,1024]{2,1,0:T(8,128)(2,1)} %bitcast.48.refs_0_), channel_id=1, source_target_pairs={{0,2},{1,3},{2,4},{3,5},{4,6},{5,7},{6,0},{7,1},{8,10},{9,11},{10,... | collective-permute-start | bytes 786440 | tf_op jit(solution)/shard_map/ppermute | solution.py:64
  24.5 23.8 %collective-permute-start.2 = (bf16[64,2048]{1,0:T(8,128)(2,1)S(1)}, bf16[64,2048]{1,0:T(8,128)(2,1)S(1)}, u32[]{:S(2)}, u32[]{:S(2)}) collective-permute-start(bf16[64,2048]{1,0:T(8,128)(2,1)S(1)} %get-tuple-element.86), channel_id=1, source_target_pairs={{0,4},{1,12},{2,6},{3,14},{4,0},{5,8},{6,2},{7,10},{8,5},{9,13},{1... | collective-permute-start | bytes 786440 | tf_op jit(solution)/shard_map/ppermute | solution.py:64
  26.5 21.8 %collective-permute-start.1 = (bf16[64,2048]{1,0:T(8,128)(2,1)S(1)}, bf16[64,2048]{1,0:T(8,128)(2,1)S(1)}, u32[]{:S(2)}, u32[]{:S(2)}) collective-permute-start(bf16[64,2048]{1,0:T(8,128)(2,1)S(1)} %get-tuple-element.87), channel_id=1, source_target_pairs={{0,2},{1,10},{2,4},{3,12},{4,6},{5,14},{6,0},{7,8},{8,3},{9,11},{1... | collective-permute-start | bytes 786440 | tf_op jit(solution)/shard_map/ppermute | solution.py:64
  29.1 28.8 %collective-permute-start.31 = (bf16[1,128,1024]{2,1,0:T(8,128)(2,1)}, bf16[1,128,1024]{2,1,0:T(8,128)(2,1)}, u32[]{:S(2)}, u32[]{:S(2)}) collective-permute-start(bf16[1,128,1024]{2,1,0:T(8,128)(2,1)} %bitcast.48.refs_0_), channel_id=1, source_target_pairs={{0,6},{1,7},{2,0},{3,1},{4,2},{5,3},{6,4},{7,5},{8,14},{9,15},{10,... | collective-permute-start | bytes 786440 | tf_op jit(solution)/shard_map/ppermute | solution.py:64
  31.5 30.1 %collective-permute-start.6 = (bf16[2,32,1664]{2,1,0:T(8,128)(2,1)S(1)}, bf16[2,32,1664]{2,1,0:T(8,128)(2,1)}, u32[]{:S(2)}, u32[]{:S(2)}) collective-permute-start(bf16[2,32,1664]{2,1,0:T(8,128)(2,1)S(1)} %pad_maximum_fusion.13.refs_0_), channel_id=1, source_target_pairs={{0,16},{1,17},{2,18},{3,19},{4,20},{5,21},{6,22},{7,23},{8,24},{9,... | collective-permute-start | bytes 638984 | tf_op jit(solution)/shard_map/ppermute | solution.py:64
  48.3 31.0 %collective-permute-start.26 = (bf16[2,32,2048]{2,1,0:T(8,128)(2,1)S(1)}, bf16[2,32,2048]{2,1,0:T(8,128)(2,1)}, u32[]{:S(2)}, u32[]{:S(2)}) collective-permute-start(bf16[2,32,2048]{2,1,0:T(8,128)(2,1)S(1)} %pad_maximum_fusion.10.refs_0_), channel_id=1, source_target_pairs={{0,2},{1,3},{2,4},{3,5},{4,6},{5,7},{6,0},{7,1},{8,10},{9,11},{10,... | collective-permute-start | bytes 786440 | tf_op jit(solution)/shard_map/ppermute | solution.py:64
  49.2 126.4 %collective-permute-start.4 = (bf16[4,64,2048]{2,1,0:T(8,128)(2,1)S(1)}, bf16[4,64,2048]{2,1,0:T(8,128)(2,1)S(1)}, u32[]{:S(2)}, u32[]{:S(2)}) collective-permute-start(bf16[4,64,2048]{2,1,0:T(8,128)(2,1)S(1)} %pad_maximum_fusion.2), channel_id=1, source_target_pairs={{0,8},{1,9},{2,10},{3,11},{4,12},{5,13},{6,14},{7,15},{8,0},{9,1},... | collective-permute-start | bytes 3145736 | tf_op jit(solution)/shard_map/ppermute | solution.py:64
  76.2 99.3 %collective-permute-start.10 = (bf16[2,2,32,1664]{3,2,1,0:T(8,128)(2,1)}, bf16[2,2,32,1664]{3,2,1,0:T(8,128)(2,1)}, u32[]{:S(2)}, u32[]{:S(2)}) collective-permute-start(bf16[2,2,32,1664]{3,2,1,0:T(8,128)(2,1)} %shard_map.246.refs_0_), channel_id=1, source_target_pairs={{0,1},{1,0},{2,3},{3,2},{4,5},{5,4},{6,7},{7,6},{8,9},{9,8},{10,11... | collective-permute-start | bytes 1277960 | tf_op jit(solution)/shard_map/ppermute | solution.py:64
  77.2 37.7 %collective-permute-start.15 = (bf16[1,32,5120]{2,1,0:T(8,128)(2,1)S(1)}, bf16[1,32,5120]{2,1,0:T(8,128)(2,1)}, u32[]{:S(2)}, u32[]{:S(2)}) collective-permute-start(bf16[1,32,5120]{2,1,0:T(8,128)(2,1)S(1)} %bitcast.582), channel_id=1, source_target_pairs={{0,1},{1,0},{2,3},{3,2},{4,5},{5,4},{6,7},{7,6},{8,9},{9,8},{10,11... | collective-permute-start | bytes 983048 | tf_op jit(solution)/shard_map/ppermute | solution.py:64
  79.3 57.4 %collective-permute-start.25 = (bf16[2,32,2048]{2,1,0:T(8,128)(2,1)S(1)}, bf16[2,32,2048]{2,1,0:T(8,128)(2,1)}, u32[]{:S(2)}, u32[]{:S(2)}) collective-permute-start(bf16[2,32,2048]{2,1,0:T(8,128)(2,1)S(1)} %pad_maximum_fusion.10.refs_0_), channel_id=1, source_target_pairs={{0,6},{1,7},{2,0},{3,1},{4,2},{5,3},{6,4},{7,5},{8,14},{9,15},{10,... | collective-permute-start | bytes 786440 | tf_op jit(solution)/shard_map/ppermute | solution.py:64
  79.3 61.2 %collective-permute-start.27 = (bf16[2,32,2048]{2,1,0:T(8,128)(2,1)}, bf16[2,32,2048]{2,1,0:T(8,128)(2,1)}, u32[]{:S(2)}, u32[]{:S(2)}) collective-permute-start(bf16[2,32,2048]{2,1,0:T(8,128)(2,1)} %collective-permute-done.26.refs_3_), channel_id=1, source_target_pairs={{0,2},{1,3},{2,4},{3,5},{4,6},{5,7},{6,0},{7,1},{8,10},{9,11},{10,... | collective-permute-start | bytes 786440 | tf_op jit(solution)/shard_map/ppermute | solution.py:64
  114.9 74.9 %collective-permute-start.8 = (bf16[2,2,32,1664]{3,2,1,0:T(8,128)(2,1)}, bf16[2,2,32,1664]{3,2,1,0:T(8,128)(2,1)}, u32[]{:S(2)}, u32[]{:S(2)}) collective-permute-start(bf16[2,2,32,1664]{3,2,1,0:T(8,128)(2,1)} %shard_map.246.refs_0_), channel_id=1, source_target_pairs={{0,2},{1,3},{2,4},{3,5},{4,6},{5,7},{6,0},{7,1},{8,10},{9,11},{10,... | collective-permute-start | bytes 1277960 | tf_op jit(solution)/shard_map/ppermute | solution.py:64
  136.6 53.2 %collective-permute-start.7 = (bf16[2,2,32,1664]{3,2,1,0:T(8,128)(2,1)}, bf16[2,2,32,1664]{3,2,1,0:T(8,128)(2,1)}, u32[]{:S(2)}, u32[]{:S(2)}) collective-permute-start(bf16[2,2,32,1664]{3,2,1,0:T(8,128)(2,1)} %shard_map.246.refs_0_), channel_id=1, source_target_pairs={{0,6},{1,7},{2,0},{3,1},{4,2},{5,3},{6,4},{7,5},{8,14},{9,15},{10,... | collective-permute-start | bytes 1277960 | tf_op jit(solution)/shard_map/ppermute | solution.py:64
  140.5 63.9 %collective-permute-start.19 = (bf16[2,1,32,5120]{3,2,1,0:T(8,128)(2,1)}, bf16[2,1,32,5120]{3,2,1,0:T(8,128)(2,1)}, u32[]{:S(2)}, u32[]{:S(2)}) collective-permute-start(bf16[2,1,32,5120]{3,2,1,0:T(8,128)(2,1)} %shard_map.249.refs_0_), channel_id=1, source_target_pairs={{0,16},{1,17},{2,18},{3,19},{4,20},{5,21},{6,22},{7,23},{8,24},{9,... | collective-permute-start | bytes 1966088 | tf_op jit(solution)/shard_map/ppermute | solution.py:64
  175.6 47.0 %collective-permute-start.17 = (bf16[2,1,32,5120]{3,2,1,0:T(8,128)(2,1)S(1)}, bf16[2,1,32,5120]{3,2,1,0:T(8,128)(2,1)}, u32[]{:S(2)}, u32[]{:S(2)}) collective-permute-start(bf16[2,1,32,5120]{3,2,1,0:T(8,128)(2,1)S(1)} %copy-done.23), channel_id=1, source_target_pairs={{0,2},{1,3},{2,4},{3,5},{4,6},{5,7},{6,0},{7,1},{8,10},{9,11},{10,... | collective-permute-start | bytes 1966088 | tf_op jit(solution)/shard_map/ppermute | solution.py:64
  175.6 25.8 %collective-permute-start.11 = (bf16[2,2,32,1664]{3,2,1,0:T(8,128)(2,1)}, bf16[2,2,32,1664]{3,2,1,0:T(8,128)(2,1)}, u32[]{:S(2)}, u32[]{:S(2)}) collective-permute-start(bf16[2,2,32,1664]{3,2,1,0:T(8,128)(2,1)} %collective-permute-done.10.refs_4_), channel_id=1, source_target_pairs={{0,6},{1,7},{2,0},{3,1},{4,2},{5,3},{6,4},{7,5},{8,14},{9,15},{10,... | collective-permute-start | bytes 1277960 | tf_op jit(solution)/shard_map/ppermute | solution.py:64
  189.8 23.7 %collective-permute-start.13 = (bf16[2,2,32,1664]{3,2,1,0:T(8,128)(2,1)}, bf16[2,2,32,1664]{3,2,1,0:T(8,128)(2,1)S(1)}, u32[]{:S(2)}, u32[]{:S(2)}) collective-permute-start(bf16[2,2,32,1664]{3,2,1,0:T(8,128)(2,1)} %collective-permute-done.10.refs_4_), channel_id=1, source_target_pairs={{0,2},{1,3},{2,4},{3,5},{4,6},{5,7},{6,0},{7,1},{8,10},{9,11},{10,... | collective-permute-start | bytes 1277960 | tf_op jit(solution)/shard_map/ppermute | solution.py:64
  189.9 32.7 %collective-permute-start.9 = (bf16[2,2,32,1664]{3,2,1,0:T(8,128)(2,1)}, bf16[2,2,32,1664]{3,2,1,0:T(8,128)(2,1)S(1)}, u32[]{:S(2)}, u32[]{:S(2)}) collective-permute-start(bf16[2,2,32,1664]{3,2,1,0:T(8,128)(2,1)} %collective-permute-done.8.refs_3_), channel_id=1, source_target_pairs={{0,2},{1,3},{2,4},{3,5},{4,6},{5,7},{6,0},{7,1},{8,10},{9,11},{10,... | collective-permute-start | bytes 1277960 | tf_op jit(solution)/shard_map/ppermute | solution.py:64
  201.4 27.2 %collective-permute-start.12 = (bf16[2,2,32,1664]{3,2,1,0:T(8,128)(2,1)}, bf16[2,2,32,1664]{3,2,1,0:T(8,128)(2,1)S(1)}, u32[]{:S(2)}, u32[]{:S(2)}) collective-permute-start(bf16[2,2,32,1664]{3,2,1,0:T(8,128)(2,1)} %collective-permute-done.11.refs_5_), channel_id=1, source_target_pairs={{0,6},{1,7},{2,0},{3,1},{4,2},{5,3},{6,4},{7,5},{8,14},{9,15},{10,... | collective-permute-start | bytes 1277960 | tf_op jit(solution)/shard_map/ppermute | solution.py:64
  204.4 131.2 %collective-permute-start.20 = (bf16[2,1,32,5120]{3,2,1,0:T(8,128)(2,1)}, bf16[2,1,32,5120]{3,2,1,0:T(8,128)(2,1)}, u32[]{:S(2)}, u32[]{:S(2)}) collective-permute-start(bf16[2,1,32,5120]{3,2,1,0:T(8,128)(2,1)} %collective-permute-done.19.refs_4_), channel_id=1, source_target_pairs={{0,6},{1,7},{2,0},{3,1},{4,2},{5,3},{6,4},{7,5},{8,14},{9,15},{10,... | collective-permute-start | bytes 1966088 | tf_op jit(solution)/shard_map/ppermute | solution.py:64
  213.5 306.6 %collective-permute-start.35 = (bf16[4,1,128,1024]{3,2,1,0:T(8,128)(2,1)}, bf16[4,1,128,1024]{3,2,1,0:T(8,128)(2,1)}, u32[]{:S(2)}, u32[]{:S(2)}) collective-permute-start(bf16[4,1,128,1024]{3,2,1,0:T(8,128)(2,1)} %shard_map.254.refs_0_), channel_id=1, source_target_pairs={{0,1},{1,0},{2,3},{3,2},{4,5},{5,4},{6,7},{7,6},{8,9},{9,8},{10,11... | collective-permute-start | bytes 3145736 | tf_op jit(solution)/shard_map/ppermute | solution.py:64
  222.5 130.5 %collective-permute-start.16 = (bf16[2,1,32,5120]{3,2,1,0:T(8,128)(2,1)S(1)}, bf16[2,1,32,5120]{3,2,1,0:T(8,128)(2,1)}, u32[]{:S(2)}, u32[]{:S(2)}) collective-permute-start(bf16[2,1,32,5120]{3,2,1,0:T(8,128)(2,1)S(1)} %copy-done.23), channel_id=1, source_target_pairs={{0,6},{1,7},{2,0},{3,1},{4,2},{5,3},{6,4},{7,5},{8,14},{9,15},{10,... | collective-permute-start | bytes 1966088 | tf_op jit(solution)/shard_map/ppermute | solution.py:64
  222.5 131.1 %collective-permute-start.22 = (bf16[2,1,32,5120]{3,2,1,0:T(8,128)(2,1)}, bf16[2,1,32,5120]{3,2,1,0:T(8,128)(2,1)}, u32[]{:S(2)}, u32[]{:S(2)}) collective-permute-start(bf16[2,1,32,5120]{3,2,1,0:T(8,128)(2,1)} %collective-permute-done.19.refs_4_), channel_id=1, source_target_pairs={{0,2},{1,3},{2,4},{3,5},{4,6},{5,7},{6,0},{7,1},{8,10},{9,11},{10,... | collective-permute-start | bytes 1966088 | tf_op jit(solution)/shard_map/ppermute | solution.py:64
  228.6 125.0 %collective-permute-start.18 = (bf16[2,1,32,5120]{3,2,1,0:T(8,128)(2,1)}, bf16[2,1,32,5120]{3,2,1,0:T(8,128)(2,1)}, u32[]{:S(2)}, u32[]{:S(2)}) collective-permute-start(bf16[2,1,32,5120]{3,2,1,0:T(8,128)(2,1)} %collective-permute-done.17.refs_3_), channel_id=1, source_target_pairs={{0,2},{1,3},{2,4},{3,5},{4,6},{5,7},{6,0},{7,1},{8,10},{9,11},{10,... | collective-permute-start | bytes 1966088 | tf_op jit(solution)/shard_map/ppermute | solution.py:64
  353.0 167.5 %collective-permute-start.29 = (bf16[4,2,32,2048]{3,2,1,0:T(8,128)(2,1)}, bf16[4,2,32,2048]{3,2,1,0:T(8,128)(2,1)}, u32[]{:S(2)}, u32[]{:S(2)}) collective-permute-start(bf16[4,2,32,2048]{3,2,1,0:T(8,128)(2,1)} %shard_map.252.refs_0_), channel_id=1, source_target_pairs={{0,16},{1,17},{2,18},{3,19},{4,20},{5,21},{6,22},{7,23},{8,24},{9,... | collective-permute-start | bytes 3145736 | tf_op jit(solution)/shard_map/ppermute | solution.py:64
  518.2 26.3 %collective-permute-start.34 = (bf16[4,1,128,1024]{3,2,1,0:T(8,128)(2,1)}, bf16[4,1,128,1024]{3,2,1,0:T(8,128)(2,1)}, u32[]{:S(2)}, u32[]{:S(2)}) collective-permute-start(bf16[4,1,128,1024]{3,2,1,0:T(8,128)(2,1)} %shard_map.254.refs_0_), channel_id=1, source_target_pairs={{0,16},{1,17},{2,18},{3,19},{4,20},{5,21},{6,22},{7,23},{8,24},{9,... | collective-permute-start | bytes 3145736 | tf_op jit(solution)/shard_map/ppermute | solution.py:64
  519.7 175.7 %collective-permute-start.28 = (bf16[4,2,32,2048]{3,2,1,0:T(8,128)(2,1)}, bf16[4,2,32,2048]{3,2,1,0:T(8,128)(2,1)}, u32[]{:S(2)}, u32[]{:S(2)}) collective-permute-start(bf16[4,2,32,2048]{3,2,1,0:T(8,128)(2,1)} %shard_map.252.refs_0_), channel_id=1, source_target_pairs={{0,1},{1,0},{2,3},{3,2},{4,5},{5,4},{6,7},{7,6},{8,9},{9,8},{10,11... | collective-permute-start | bytes 3145736 | tf_op jit(solution)/shard_map/ppermute | solution.py:64
  520.1 46.5 %collective-permute-start.36 = (bf16[4,1,128,1024]{3,2,1,0:T(8,128)(2,1)}, bf16[4,1,128,1024]{3,2,1,0:T(8,128)(2,1)}, u32[]{:S(2)}, u32[]{:S(2)}) collective-permute-start(bf16[4,1,128,1024]{3,2,1,0:T(8,128)(2,1)} %collective-permute-done.35.refs_2_), channel_id=1, source_target_pairs={{0,16},{1,17},{2,18},{3,19},{4,20},{5,21},{6,22},{7,23},{8,24},{9,... | collective-permute-start | bytes 3145736 | tf_op jit(solution)/shard_map/ppermute | solution.py:64
  520.5 175.0 %collective-permute-start.30 = (bf16[4,2,32,2048]{3,2,1,0:T(8,128)(2,1)}, bf16[4,2,32,2048]{3,2,1,0:T(8,128)(2,1)}, u32[]{:S(2)}, u32[]{:S(2)}) collective-permute-start(bf16[4,2,32,2048]{3,2,1,0:T(8,128)(2,1)} %collective-permute-done.29.refs_2_), channel_id=1, source_target_pairs={{0,1},{1,0},{2,3},{3,2},{4,5},{5,4},{6,7},{7,6},{8,9},{9,8},{10,11... | collective-permute-start | bytes 3145736 | tf_op jit(solution)/shard_map/ppermute | solution.py:64
  535.9 288.5 %collective-permute-start.24 = (bf16[512,1024]{1,0:T(8,128)(2,1)}, bf16[512,1024]{1,0:T(8,128)(2,1)}, u32[]{:S(2)}, u32[]{:S(2)}) collective-permute-start(bf16[512,1024]{1,0:T(8,128)(2,1)} %convolution_convert_fusion.9), channel_id=1, source_target_pairs={{0,8},{1,9},{2,10},{3,11},{4,12},{5,13},{6,14},{7,15},{8,0},{9,1},... | collective-permute-start | bytes 3145736 | tf_op jit(solution)/shard_map/ppermute | solution.py:64
  855.9 155.2 %collective-permute-start.81 = (bf16[2,4,2,32,2048]{4,3,1,0,2:T(8,128)(2,1)}, bf16[2,4,2,32,2048]{4,3,1,0,2:T(8,128)(2,1)}, u32[]{:S(2)}, u32[]{:S(2)}) collective-permute-start(bf16[2,4,2,32,2048]{4,3,1,0,2:T(8,128)(2,1)} %copy_bitcast_fusion), channel_id=1, source_target_pairs={{0,16},{1,17},{2,18},{3,19},{4,20},{5,21},{6,22},{7,23},{8,24},{9,... | collective-permute-start | bytes 6291464 | tf_op jit(solution)/shard_map/ppermute | solution.py:64
  857.4 161.4 %collective-permute-start.87 = (bf16[2,1,4,128,1024]{4,3,2,1,0:T(8,128)(2,1)}, bf16[2,1,4,128,1024]{4,3,2,1,0:T(8,128)(2,1)}, u32[]{:S(2)}, u32[]{:S(2)}) collective-permute-start(bf16[2,1,4,128,1024]{4,3,2,1,0:T(8,128)(2,1)} %dynamic-slice_bitcast_fusion), channel_id=1, source_target_pairs={{0,1},{1,0},{2,3},{3,2},{4,5},{5,4},{6,7},{7,6},{8,9},{9,8},{10,11... | collective-permute-start | bytes 6291464 | tf_op jit(solution)/shard_map/ppermute | solution.py:64
  874.9 23.7 %collective-permute-start.49 = (bf16[128,1024]{1,0:T(8,128)(2,1)}, bf16[128,1024]{1,0:T(8,128)(2,1)}, u32[]{:S(2)}, u32[]{:S(2)}) collective-permute-start(bf16[128,1024]{1,0:T(8,128)(2,1)} %pad_maximum_fusion.11), channel_id=1, source_target_pairs={{0,2},{1,3},{2,0},{3,1},{4,6},{5,7},{6,4},{7,5},{8,10},{9,11},{10,... | collective-permute-start | bytes 786440 | tf_op jit(solution)/shard_map/ppermute | solution.py:64
  879.7 36.0 %collective-permute-start.76 = (bf16[2,1,2,32,1024]{4,3,2,1,0:T(8,128)(2,1)}, bf16[2,1,2,32,1024]{4,3,2,1,0:T(8,128)(2,1)}, u32[]{:S(2)}, u32[]{:S(2)}) collective-permute-start(bf16[2,1,2,32,1024]{4,3,2,1,0:T(8,128)(2,1)} %get-tuple-element.73), channel_id=1, source_target_pairs={{0,2},{1,3},{2,4},{3,5},{4,6},{5,7},{6,0},{7,1},{8,10},{9,11},{10,... | collective-permute-start | bytes 786440 | tf_op jit(solution)/shard_map/ppermute | solution.py:64
  898.6 40.0 %collective-permute-start.78 = (bf16[2,1,2,32,1024]{4,3,2,1,0:T(8,128)(2,1)}, bf16[2,1,2,32,1024]{4,3,2,1,0:T(8,128)(2,1)}, u32[]{:S(2)}, u32[]{:S(2)}) collective-permute-start(bf16[2,1,2,32,1024]{4,3,2,1,0:T(8,128)(2,1)} %get-tuple-element.74), channel_id=1, source_target_pairs={{0,6},{1,7},{2,0},{3,1},{4,2},{5,3},{6,4},{7,5},{8,14},{9,15},{10,... | collective-permute-start | bytes 786440 | tf_op jit(solution)/shard_map/ppermute | solution.py:64
  938.6 41.2 %collective-permute-start.43 = (bf16[512,1024]{1,0:T(8,128)(2,1)S(1)}, bf16[512,1024]{1,0:T(8,128)(2,1)}, u32[]{:S(2)}, u32[]{:S(2)}) collective-permute-start(bf16[512,1024]{1,0:T(8,128)(2,1)S(1)} %convolution_convert_fusion.8), channel_id=1, source_target_pairs={{0,8},{1,9},{2,10},{3,11},{4,12},{5,13},{6,14},{7,15},{8,0},{9,1},... | collective-permute-start | bytes 3145736 | tf_op jit(solution)/shard_map/ppermute | solution.py:64
  938.6 24.7 %collective-permute-start.51 = (bf16[128,1024]{1,0:T(8,128)(2,1)}, bf16[128,1024]{1,0:T(8,128)(2,1)}, u32[]{:S(2)}, u32[]{:S(2)}) collective-permute-start(bf16[128,1024]{1,0:T(8,128)(2,1)} %add_convert_fusion.4), channel_id=1, source_target_pairs={{0,16},{1,17},{2,18},{3,19},{4,20},{5,21},{6,22},{7,23},{8,24},{9,... | collective-permute-start | bytes 786440 | tf_op jit(solution)/shard_map/ppermute | solution.py:64
  975.9 55.5 %collective-permute-start.75 = (bf16[128,1024]{1,0:T(8,128)(2,1)}, bf16[128,1024]{1,0:T(8,128)(2,1)}, u32[]{:S(2)}, u32[]{:S(2)}) collective-permute-start(bf16[128,1024]{1,0:T(8,128)(2,1)} %add_convert_fusion.2), channel_id=1, source_target_pairs={{0,8},{1,9},{2,10},{3,11},{4,12},{5,13},{6,14},{7,15},{8,0},{9,1},... | collective-permute-start | bytes 786440 | tf_op jit(solution)/shard_map/ppermute | solution.py:64
  979.3 59.7 %collective-permute-start.53 = (f32[128,1024]{1,0:T(8,128)}, f32[128,1024]{1,0:T(8,128)}, u32[]{:S(2)}, u32[]{:S(2)}) collective-permute-start(f32[128,1024]{1,0:T(8,128)} %fusion.95), channel_id=1, source_target_pairs={{0,8},{1,9},{2,10},{3,11},{4,12},{5,13},{6,14},{7,15},{8,0},{9,1},... | collective-permute-start | bytes 1572872 | tf_op jit(solution)/shard_map/ppermute | solution.py:64
  988.3 29.7 %collective-permute-start.64 = (bf16[2,1,2,32,1024]{4,3,2,1,0:T(8,128)(2,1)S(1)}, bf16[2,1,2,32,1024]{4,3,2,1,0:T(8,128)(2,1)S(1)}, u32[]{:S(2)}, u32[]{:S(2)}) collective-permute-start(bf16[2,1,2,32,1024]{4,3,2,1,0:T(8,128)(2,1)S(1)} %get-tuple-element.78), channel_id=1, source_target_pairs={{0,2},{1,3},{2,4},{3,5},{4,6},{5,7},{6,0},{7,1},{8,10},{9,11},{10,... | collective-permute-start | bytes 786440 | tf_op jit(solution)/shard_map/ppermute | solution.py:64
  1018.9 45.7 %collective-permute-start.44 = (bf16[512,1024]{1,0:T(8,128)(2,1)S(1)}, bf16[512,1024]{1,0:T(8,128)(2,1)}, u32[]{:S(2)}, u32[]{:S(2)}) collective-permute-start(bf16[512,1024]{1,0:T(8,128)(2,1)S(1)} %convolution_convert_fusion.4), channel_id=1, source_target_pairs={{0,8},{1,9},{2,10},{3,11},{4,12},{5,13},{6,14},{7,15},{8,0},{9,1},... | collective-permute-start | bytes 3145736 | tf_op jit(solution)/shard_map/ppermute | solution.py:64
  1022.2 24.6 %collective-permute-start.58 = (bf16[2,2,2,32,1536]{4,3,2,1,0:T(8,128)(2,1)}, bf16[2,2,2,32,1536]{4,3,2,1,0:T(8,128)(2,1)}, u32[]{:S(2)}, u32[]{:S(2)}) collective-permute-start(bf16[2,2,2,32,1536]{4,3,2,1,0:T(8,128)(2,1)} %get-tuple-element.61), channel_id=1, source_target_pairs={{0,6},{1,7},{2,0},{3,1},{4,2},{5,3},{6,4},{7,5},{8,14},{9,15},{10,... | collective-permute-start | bytes 2359304 | tf_op jit(solution)/shard_map/ppermute | solution.py:64
  1029.7 33.9 %collective-permute-start.60 = (bf16[2,2,2,32,1536]{4,3,2,1,0:T(8,128)(2,1)}, bf16[2,2,2,32,1536]{4,3,2,1,0:T(8,128)(2,1)}, u32[]{:S(2)}, u32[]{:S(2)}) collective-permute-start(bf16[2,2,2,32,1536]{4,3,2,1,0:T(8,128)(2,1)} %get-tuple-element.62), channel_id=1, source_target_pairs={{0,2},{1,3},{2,4},{3,5},{4,6},{5,7},{6,0},{7,1},{8,10},{9,11},{10,... | collective-permute-start | bytes 2359304 | tf_op jit(solution)/shard_map/ppermute | solution.py:64
  1039.0 28.5 %collective-permute-start.82 = (bf16[2,4,32,2048]{3,2,1,0:T(8,128)(2,1)}, bf16[2,4,32,2048]{3,2,1,0:T(8,128)(2,1)}, u32[]{:S(2)}, u32[]{:S(2)}) collective-permute-start(bf16[2,4,32,2048]{3,2,1,0:T(8,128)(2,1)} %fusion.31), channel_id=1, source_target_pairs={{0,1},{1,0},{2,3},{3,2},{4,5},{5,4},{6,7},{7,6},{8,9},{9,8},{10,11... | collective-permute-start | bytes 3145736 | tf_op jit(solution)/shard_map/ppermute | solution.py:64
  1042.8 44.6 %collective-permute-start.88 = (bf16[1,4,128,1024]{3,2,1,0:T(8,128)(2,1)}, bf16[1,4,128,1024]{3,2,1,0:T(8,128)(2,1)}, u32[]{:S(2)}, u32[]{:S(2)}) collective-permute-start(bf16[1,4,128,1024]{3,2,1,0:T(8,128)(2,1)} %fusion.28), channel_id=1, source_target_pairs={{0,16},{1,17},{2,18},{3,19},{4,20},{5,21},{6,22},{7,23},{8,24},{9,... | collective-permute-start | bytes 3145736 | tf_op jit(solution)/shard_map/ppermute | solution.py:64
  1049.3 91.8 %collective-permute-start.59 = (bf16[2,2,2,32,1536]{4,3,1,2,0:T(8,128)(2,1)}, bf16[2,2,2,32,1536]{4,3,1,2,0:T(8,128)(2,1)}, u32[]{:S(2)}, u32[]{:S(2)}) collective-permute-start(bf16[2,2,2,32,1536]{4,3,1,2,0:T(8,128)(2,1)} %copy.207), channel_id=1, source_target_pairs={{0,6},{1,7},{2,0},{3,1},{4,2},{5,3},{6,4},{7,5},{8,14},{9,15},{10,... | collective-permute-start | bytes 2359304 | tf_op jit(solution)/shard_map/ppermute | solution.py:64
  1105.4 31.8 %collective-permute-start.91 = (bf16[1,128,1024]{2,1,0:T(8,128)(2,1)}, bf16[1,128,1024]{2,1,0:T(8,128)(2,1)}, u32[]{:S(2)}, u32[]{:S(2)}) collective-permute-start(bf16[1,128,1024]{2,1,0:T(8,128)(2,1)} %get-tuple-element.68), channel_id=1, source_target_pairs={{0,6},{1,7},{2,0},{3,1},{4,2},{5,3},{6,4},{7,5},{8,14},{9,15},{10,... | collective-permute-start | bytes 786440 | tf_op jit(solution)/shard_map/ppermute | solution.py:64
  1112.3 21.7 %collective-permute-start.84 = (bf16[2,32,2048]{2,1,0:T(8,128)(2,1)}, bf16[2,32,2048]{2,1,0:T(8,128)(2,1)}, u32[]{:S(2)}, u32[]{:S(2)}) collective-permute-start(bf16[2,32,2048]{2,1,0:T(8,128)(2,1)} %fusion.62), channel_id=1, source_target_pairs={{0,6},{1,7},{2,0},{3,1},{4,2},{5,3},{6,4},{7,5},{8,14},{9,15},{10,... | collective-permute-start | bytes 786440 | tf_op jit(solution)/shard_map/ppermute | solution.py:64
  (113 other events, 2413.0 us)

commit v2 on v1

--- a/solution.py
+++ b/solution.py
@@ -72,17 +72,18 @@
     def over_y(self, value):
         return self.send(value, lambda x, c, z, r, y: (x, c, z, r, 1 - y))
 
-    def over_z(self, value, step):
-        return self.send(value, lambda x, c, z, r, y: (x, c, (z + step) % 4, r, y))
-
-    def xor_z(self, value, bit):
-        return self.send(value, lambda x, c, z, r, y: (x, c, z ^ bit, r, y))
+    def xor_z(self, value, bits):
+        return self.send(value, lambda x, c, z, r, y: (x, c, z ^ bits, r, y))
 
     def over_r(self, value, step):
         return self.send(value, lambda x, c, z, r, y: (x, c, z, (r + step) % self.t, y))
 
-    def regroup(self, value, step):
-        return self.send(value, lambda x, c, z, r, y: (x, y, (z + step) % 4, r, c))
+    def regroup(self, value, bits):
+        return self.send(value, lambda x, c, z, r, y: (x, y, z ^ bits, r, c))
+
+
+def after(value, *others):
+    return lax.optimization_barrier((value, others))[0]
 
 
 def place(scalars, sources, shapes, copies):
@@ -106,8 +107,9 @@
         out_shape=[jax.ShapeDtypeStruct(shape, BF) for shape in shapes],
         in_specs=[pl.BlockSpec(memory_space=pltpu.SMEM)]
         + [pl.BlockSpec(memory_space=pl.ANY)] * len(sources),
-        out_specs=[pl.BlockSpec(memory_space=pl.ANY)] * len(shapes),
+        out_specs=[pl.BlockSpec(memory_space=pltpu.VMEM)] * len(shapes),
         scratch_shapes=[pltpu.SemaphoreType.DMA((len(copies),))],
+        compiler_params=pltpu.CompilerParams(vmem_limit_bytes=32 * 2**20),
         cost_estimate=pl.CostEstimate(flops=0, bytes_accessed=2 * moved, transcendentals=0),
     )(scalars, *sources)
 
@@ -115,108 +117,50 @@
 ALL = slice(None)
 
 
-def everything(s):
-    return (ALL,)
-
-
-def gather_xyz(g, scal, shard, widths):
-    kinds, rows, _ = shard.shape
-    other = g.over_x(shard)
-    (pair,) = place(
+def gather_line(scal, got):
+    _, rows, width = got[0].shape
+    return place(
         scal,
-        [shard, other],
-        [(2,) + shard.shape],
+        got,
+        [(4, rows, width)] * 2,
         [
-            (0, everything, 0, lambda s: (s[0],)),
-            (1, everything, 0, lambda s: (1 - s[0],)),
+            (k, lambda s, h=h: (h,), h, lambda s, k=k: (s[2] ^ k,))
+            for k in range(4)
+            for h in range(2)
         ],
     )
-    bufs = []
-    for dy, block in ((0, pair), (1, g.over_y(pair))):
-        low, high = g.over_z(block, 1), g.over_z(block, -1)
-        far = g.over_z(low, 1) if dy == 0 else g.over_z(high, -1)
-        bufs += [(block, 0, dy), (high, 1, dy), (far, 2, dy), (low, 3, dy)]
-    shapes = [(2, kinds, 4, 2, rows, width) for width in widths]
+
+
+def gather_place(scal, pair_a, far_a, pair_b, far_b, shapes, targets):
+    rows = pair_a.shape[2]
     copies = []
-    for i, (_, dz, dy) in enumerate(bufs):
-        start = 0
-        for o, width in enumerate(widths):
-            copies.append(
-                (
-                    i,
-                    lambda s, start=start, width=width: (ALL, ALL, ALL, pl.ds(start, width)),
-                    o,
-                    lambda s, dz=dz, dy=dy: (ALL, ALL, (s[2] + dz) & 3, s[3] ^ dy),
-                )
-            )
-            start += width
-    return place(scal, [b[0] for b in bufs], shapes, copies)
-
-
-def gather_yxz(g, scal, shard, sections):
-    _, rows, _ = shard.shape
-    other = g.over_y(shard)
-    (pair,) = place(
-        scal,
-        [shard, other],
-        [(2,) + shard.shape],
-        [
-            (0, everything, 0, lambda s: (s[3],)),
-            (1, everything, 0, lambda s: (1 - s[3],)),
-        ],
-    )
-    bufs = []
-    for dx, block in ((0, pair), (1, g.over_x(pair))):
-        low, high = g.over_z(block, 1), g.over_z(block, -1)
-        far = g.over_z(low, 1) if dx == 0 else g.over_z(high, -1)
-        bufs += [(block, 0, dx), (high, 1, dx), (far, 2, dx), (low, 3, dx)]
-    shapes = [(2, kinds, 4, 2, rows, width) for width, kinds in sections]
-    copies = []
-    for i, (_, dz, dx) in enumerate(bufs):
-        start = 0
-        for o, (width, kinds) in enumerate(sections):
-            for kind in range(kinds):
+    for i, half in enumerate((0, 0, 1, 1)):
+        far = i % 2
+        for near in range(2):
+            dx, dy = (near, far) if half == 0 else (far, near)
+            start = 0
+            for wide, out, kind, row in targets[half]:
                 copies.append(
                     (
                         i,
-                        lambda s, start=start, width=width: (ALL, 0, ALL, pl.ds(start, width)),
-                        o,
-                        lambda s, dz=dz, dx=dx, kind=kind: (s[0] ^ dx, kind, (s[2] + dz) & 3),
+                        lambda s, near=near, start=start, wide=wide: (
+                            near,
+                            ALL,
+                            ALL,
+                            pl.ds(start, wide),
+                        ),
+                        out,
+                        lambda s, dx=dx, dy=dy, kind=kind, row=row, half=half: (
+                            s[0] ^ dx,
+                            s[1] ^ half if kind is None else kind,
+                            ALL,
+                            s[3] ^ dy,
+                            pl.ds(row, rows),
+                        ),
                     )
                 )
-                start += width
-    return place(scal, [b[0] for b in bufs], shapes, copies)
-
-
-def gather_z_first(g, scal, shard, order, step):
-    kinds, rows, width = shard.shape
-    low, high = g.over_z(shard, 1), g.over_z(shard, -1)
-    far = g.over_z(low, 1) if step == 1 else g.over_z(high, -1)
-    (line,) = place(
-        scal,
-        [shard, high, far, low],
-        [(4,) + shard.shape],
-        [(i, everything, 0, lambda s, i=i: ((s[2] + i) & 3,)) for i in range(4)],
-    )
-    bufs = []
-    if order == "zxy":
-        for dx, block in ((0, line), (1, g.over_x(line))):
-            bufs += [(block, dx, 0), (g.over_y(block), dx, 1)]
-    else:
-        for dy, block in ((0, line), (1, g.over_y(line))):
-            bufs += [(block, 0, dy), (g.over_x(block), 1, dy)]
-    copies = []
-    for i, (_, dx, dy) in enumerate(bufs):
-        for kind in range(kinds):
-            copies.append(
-                (
-                    i,
-                    lambda s, kind=kind: (ALL, kind),
-                    0,
-                    lambda s, dx=dx, dy=dy, kind=kind: (s[0] ^ dx, kind, ALL, s[3] ^ dy),
-                )
-            )
-    return place(scal, [b[0] for b in bufs], [(2, kinds, 4, 2, rows, width)], copies)[0]
+                start += wide
+    return place(scal, [pair_a, far_a, pair_b, far_b], shapes, copies)
 
 
 def plus(*terms):
@@ -226,41 +170,272 @@
     return total.astype(BF)
 
 
-def reduce_z(g, part, dim, step):
-    ahead = g.over_z(part((g.z + 2) & 3), step)
-    near = g.over_z(plus(part((g.z + step) & 3), ahead), step)
-    back = g.over_z(part((g.z - step) & 3), -step)
-    return near, back
-
-
-def reduce_pair(g, terms, dim, mine, over):
-    gone = plus(*[pick(term, dim, 1 - mine) for term in terms])
-    return [pick(term, dim, mine) for term in terms] + [over(gone)]
-
-
-def scatter(g, grad, order, step):
-    terms = [grad]
-    dims = ["x", "k", "z", "y"]
-    for axis in order:
-        dim = dims.index(axis)
-        if axis == "z":
-            if len(terms) > 1:
-                terms = [plus(*terms)]
-            whole = terms[0]
-            near, back = reduce_z(g, lambda i: pick(whole, dim, i), dim, step)
-            terms = [pick(whole, dim, g.z), near, back]
-        elif axis == "x":
-            terms = reduce_pair(g, terms, dim, g.x, g.over_x)
-        else:
-            terms = reduce_pair(g, terms, dim, g.y, g.over_y)
-        dims.pop(dim)
-    return terms
+def by_columns(array, share):
+    view = array.reshape(2, 2, 4, 2, share, array.shape[1])
+    block = (None, None, None, None, share, array.shape[1])
+    return [(view, block, lambda x, z, y, h: (x, h, z, y, 0, 0))]
+
+
+def by_rows(array, share):
+    groups, width = array.shape[0] // (16 * share), array.shape[1]
+    if groups == 1:
+        view = array.reshape(2, 4, 2, share, width)
+        block = (None, None, None, share, width // 2)
+        return [(view, block, lambda x, z, y, h: (x, z, y, 0, h))]
+    view = array.reshape(2, 4, 2, groups, share, width)
+    block = (None, None, None, None, share, width)
+    return [
+        (view, block, lambda x, z, y, h, i=i: (x, z, y, h * (groups // 2) + i, 0, 0))
+        for i in range(groups // 2)
+    ]
+
+
+def fold(scal, slots, steps, share, places, received, outs):
+    width = sum(block[-1] for _, block, _ in slots)
+    arrays, specs = [], []
+    for h in range(2):
+        for view, block, index in slots:
+            arrays.append(view)
+            specs.append(
+                pl.BlockSpec(
+                    block, lambda i, s, h=h, index=index: index(*places[h](i, s), h)
+                )
+            )
+        for array, at in received[h]:
+            arrays.append(array)
+            specs.append(
+                pl.BlockSpec((None, share, width), lambda i, s, at=at: (at(i, s), 0, 0))
+            )
+    each = len(slots), len(received[0])
+
+    def kernel(s_ref, *refs):
+        step = pl.program_id(0)
+        ins, targets = refs[: len(arrays)], refs[len(arrays) :]
+        for h in range(2):
+            mine = ins[h * sum(each) : (h + 1) * sum(each)]
+            start = 0
+            for part in mine[: each[0]]:
+                wide = part.shape[-1]
+                at = pl.ds(start, wide)
+                value = part[...]
+                if each[1]:
+                    value = value.astype(F32)
+                    for extra in mine[each[0] :]:
+                        value = value + extra[:, at].astype(F32)
+                    value = value.astype(BF)
+                if outs is None:
+                    targets[h][:, at] = value
+                else:
+                    for j in range(steps):
+
+                        @pl.when(step == j)
+                        def _():
+                            targets[j][h, :, at] = value
+
+                start += wide
+
+    if outs is None:
+        out_shape = [jax.ShapeDtypeStruct((steps, share, width), BF)] * 2
+        out_specs = [pl.BlockSpec((None, share, width), lambda i, s: (i, 0, 0))] * 2
+    else:
+        out_shape = [jax.ShapeDtypeStruct((2, share, width), BF)] * steps
+        out_specs = [pl.BlockSpec((2, share, width), lambda i, s: (0, 0, 0))] * steps
+    return pl.pallas_call(
+        kernel,
+        grid_spec=pltpu.PrefetchScalarGridSpec(
+            num_scalar_prefetch=1, grid=(steps,), in_specs=specs, out_specs=out_specs
+        ),
+        out_shape=out_shape,
+        compiler_params=pltpu.CompilerParams(vmem_limit_bytes=32 * 2**20),
+        cost_estimate=pl.CostEstimate(
+            flops=0, bytes_accessed=2 * steps * share * width * 6, transcendentals=0
+        ),
+    )(scal, *arrays)
+
+
+def spread(g, line):
+    return [line[0]] + [g.xor_z(line[k], k) for k in (1, 2, 3)]
+
+
+class Scatter:
+    def __init__(self, g, scal, share, slots):
+        self.g, self.scal, self.share, self.slots = g, scal, share, slots
+
+    def fold(self, *rest):
+        return fold(self.scal, self.slots, *rest)
+
+    def width(self):
+        return sum(block[-1] for _, block, _ in self.slots)
+
+    def far(self, *others):
+        far_a, far_b = self.fold(
+            8,
+            self.share,
+            [
+                lambda i, s: (i // 4, lax.rem(i, 4), 1 - s[3]),
+                lambda i, s: (1 - s[0], i // 2, lax.rem(i, 2)),
+            ],
+            [[], []],
+            None,
+        )
+        self.folded = far_a, far_b
+        if others:
+            far_a, far_b = after(self.folded, others)
+        self.far_a, self.far_b = self.g.over_y(far_a), self.g.over_x(far_b)
+        return self
+
+    def near(self):
+        near_a, near_b = self.fold(
+            4,
+            self.share,
+            [lambda i, s: (1 - s[0], i, s[3]), lambda i, s: (s[0], i, 1 - s[3])],
+            [
+                [(self.far_a, lambda i, s: (1 - s[0]) * 4 + i)],
+                [(self.far_b, lambda i, s: i * 2 + 1 - s[3])],
+            ],
+            None,
+        )
+        self.folded = near_a, near_b
+        self.near_a, self.near_b = self.g.over_x(near_a), self.g.over_y(near_b)
+        return self
+
+    def line(self):
+        line = self.fold(
+            4,
+            self.share,
+            [lambda i, s: (s[0], s[2] ^ i, s[3])] * 2,
+            [
+                [
+                    (self.far_a, lambda i, s: s[0] * 4 + (s[2] ^ i)),
+                    (self.near_a, lambda i, s: s[2] ^ i),
+                ],
+                [
+                    (self.far_b, lambda i, s: (s[2] ^ i) * 2 + s[3]),
+                    (self.near_b, lambda i, s: s[2] ^ i),
+                ],
+            ],
+            True,
+        )
+        return line
+
+
+def summed(terms, *at):
+    return sum(term[at].astype(F32) for term in terms)
+
+
+def prep_weights(scal, sources, whole=None):
+    share = sources[0][0].shape[0]
+    more = 0 if whole is None else whole.shape[1]
+    width = sum(array.shape[1] // (2 if groups else 1) for array, groups in sources)
+
+    def kernel(s_ref, *refs):
+        low = s_ref[1] == 0
+        keep, send = refs[-2:]
+        start = 0
+        for ref, (_, groups) in zip(refs, sources):
+            if groups == 0:
+                keep[:, pl.ds(start, ref.shape[1])] = ref[...]
+                send[:, pl.ds(start, ref.shape[1])] = ref[...]
+                start += ref.shape[1]
+                continue
+            block = ref.shape[1] // groups // 2
+            for i in range(groups):
+                a = ref[:, pl.ds(2 * i * block, block)]
+                b = ref[:, pl.ds((2 * i + 1) * block, block)]
+                keep[:, pl.ds(start, block)] = jnp.where(low, a, b)
+                send[:, pl.ds(start, block)] = jnp.where(low, b, a)
+                start += block
+        if whole is not None:
+            keep[:, pl.ds(start, more)] = refs[len(sources)][...]
+
+    vmem = pl.BlockSpec(memory_space=pltpu.VMEM)
+    smem = pl.BlockSpec(memory_space=pltpu.SMEM)
+    arrays = [array for array, _ in sources] + ([] if whole is None else [whole])
+    return pl.pallas_call(
+        kernel,
+        in_specs=[smem] + [vmem] * len(arrays),
+        out_specs=[vmem] * 2,
+        out_shape=[
+            jax.ShapeDtypeStruct((share, width + more), BF),
+            jax.ShapeDtypeStruct((share, width), BF),
+        ],
+        compiler_params=pltpu.CompilerParams(vmem_limit_bytes=32 * 2**20),
+    )(scal, *arrays)
+
+
+def prep_tokens(scal, ids, tokens, cotangent):
+    depth = tokens.shape[2]
+
+    def kernel(s_ref, ids_ref, tok, cot, *blocks):
+        for step in range(4):
+            j = s_ref[2] ^ step
+            b = j >> 1
+            half = (j & 1) ^ (ids_ref[b, 0] & 1)
+            rows = pl.ds(pl.multiple_of(half * STRIPE, STRIPE), STRIPE)
+            blocks[step][...] = tok[b, rows, :]
+            blocks[4 + step][...] = cot[b, rows, :]
+
+    vmem = pl.BlockSpec(memory_space=pltpu.VMEM)
+    smem = pl.BlockSpec(memory_space=pltpu.SMEM)
+    return pl.pallas_call(
+        kernel,
+        in_specs=[smem, smem, vmem, vmem],
+        out_specs=[vmem] * 8,
+        out_shape=[jax.ShapeDtypeStruct((STRIPE, depth), BF)] * 8,
+        compiler_params=pltpu.CompilerParams(vmem_limit_bytes=32 * 2**20),
+    )(scal, ids, tokens, cotangent)
+
+
+def join_tokens(scal, mine, other):
+    _, rows, depth = other.shape
+
+    def kernel(s_ref, a0, a1, a2, a3, o_ref, out):
+        for step, ref in enumerate((a0, a1, a2, a3)):
+            for part, core in ((ref, s_ref[1]), (o_ref.at[step], 1 - s_ref[1])):
+                at = pl.ds(pl.multiple_of((2 * step + core) * rows, rows), rows)
+                out[at, :] = part[...]
+
+    vmem = pl.BlockSpec(memory_space=pltpu.VMEM)
+    return pl.pallas_call(
+        kernel,
+        in_specs=[pl.BlockSpec(memory_space=pltpu.SMEM)] + [vmem] * 5,
+        out_specs=vmem,
+        out_shape=jax.ShapeDtypeStruct((8 * rows, depth), BF),
+        compiler_params=pltpu.CompilerParams(vmem_limit_bytes=32 * 2**20),
+    )(scal, *mine, other)
+
+
+def place_home(scal, ids, blocks):
+    rows, width = blocks[0].shape
+    depth = width // 2
+
+    def kernel(s_ref, ids_ref, a0, a1, a2, a3, out, grad):
+        for step, ref in enumerate((a0, a1, a2, a3)):
+            j = s_ref[2] ^ step
+            b = j >> 1
+            half = (j & 1) ^ (ids_ref[b, 0] & 1)
+            at = pl.ds(pl.multiple_of(half * rows, rows), rows)
+            out[b, at, :] = ref[:, pl.ds(0, depth)]
+            grad[b, at, :] = ref[:, pl.ds(depth, depth)].astype(F32)
+
+    vmem = pl.BlockSpec(memory_space=pltpu.VMEM)
+    smem = pl.BlockSpec(memory_space=pltpu.SMEM)
+    return pl.pallas_call(
+        kernel,
+        in_specs=[smem, smem] + [vmem] * 4,
+        out_specs=[vmem] * 2,
+        out_shape=[
+            jax.ShapeDtypeStruct((2, 2 * rows, depth), BF),
+            jax.ShapeDtypeStruct((2, 2 * rows, depth), F32),
+        ],
+        compiler_params=pltpu.CompilerParams(vmem_limit_bytes=32 * 2**20),
+    )(scal, ids, *blocks)
 
 
 def attn_fwd_kernel(z_ref, q_ref, k_ref, v_ref, o_ref, *, scale):
     z = z_ref[0]
     size = q_ref.shape[0] // 4
-    starts = [pl.multiple_of(((z - h) & 3) * size, size) for h in range(4)]
+    starts = [pl.multiple_of((z ^ h) * size, size) for h in range(4)]
     keys = jnp.concatenate([k_ref[pl.ds(s, size), :] for s in starts], 0)
     values = jnp.concatenate([v_ref[pl.ds(s, size), :] for s in starts], 0)
     first = lax.broadcasted_iota(jnp.int32, (size, 128), 1) < 64
@@ -308,7 +483,7 @@
     z = z_ref[0]
     at = pl.program_id(0)
     size = q_ref.shape[0] // 4
-    starts = [pl.multiple_of(((z - h) & 3) * size, size) for h in range(4)]
+    starts = [pl.multiple_of((z ^ h) * size, size) for h in range(4)]
     keys = jnp.concatenate([k_ref[pl.ds(s, size), :] for s in starts], 0)
     values = jnp.concatenate([v_ref[pl.ds(s, size), :] for s in starts], 0)
     first = lax.broadcasted_iota(jnp.int32, (size, 128), 1) < 64
@@ -476,7 +651,7 @@
     rest = jnp.arange(rows, dtype=jnp.int32) % (2 * STRIPE)
 
     def positions(r):
-        return (((g.z - slot) % 4) * g.t + r) * (2 * STRIPE) + rest
+        return ((g.z ^ slot) * g.t + r) * (2 * STRIPE) + rest
 
     key_pos = jnp.concatenate([positions((g.r - q) % g.t) for q in range(g.t)])
     return key_pos[None, :] <= positions(g.r)[:, None]
@@ -550,38 +725,98 @@
     return jnp.stack([first, second], axis)
 
 
-def gather_fast(g, weights):
+def gather_fast(g, scal, weights, ids, tokens, cotangent):
     gains, shifts, w_qkv, w_out, w_cq, w_ckv, w_co, w_up, w_down = weights
-    scal = jnp.stack([g.x, g.c, g.z, g.y]).astype(jnp.int32)
+    share, depth = w_co.shape
+    tall = w_down.shape[0]
     small = jnp.concatenate([gains, shifts], 0).T
     small = jnp.pad(small, ((0, 0), (0, 128 - small.shape[1])))
-    mine, other = column_halves(w_qkv, 6, g.c)
-    got = g.over_c(jnp.concatenate([other, small], 1))
-    qkv = two(g, jnp.concatenate([mine, small], 1), got, 0)
-    cq_mine, cq_other = column_halves(w_cq, 2, g.c)
-    ckv_mine, ckv_other = column_halves(w_ckv, 4, g.c)
-    up_mine, up_other = column_halves(w_up, 2, g.c)
-    n_cq, n_ckv = cq_mine.shape[1], ckv_mine.shape[1]
-    got = g.over_c(jnp.concatenate([cq_other, ckv_other, up_other], 1))
-    cq = two(g, cq_mine, got[:, :n_cq], 0)
-    ckv = two(g, ckv_mine, got[:, n_cq : n_cq + n_ckv], 0)
-    up = two(g, up_mine, got[:, n_cq + n_ckv :], 0)
-    misc = jnp.concatenate([w_out, w_co, cq[0], cq[1], ckv[0], ckv[1]], 1)[None]
-    depth = w_out.shape[1]
-    qkv_all, small_all = gather_xyz(g, scal, qkv, [mine.shape[1], 128])
-    out_all, co_all, cq_all, ckv_all = gather_yxz(
-        g, scal, misc, [(depth, 1), (depth, 1), (n_cq, 2), (n_ckv, 2)]
-    )
-    up_all = gather_z_first(g, scal, up, "zxy", 1)
-    down_all = gather_z_first(g, scal, w_down[None], "zyx", -1)
-    small_all = small_all.reshape(-1, 128)[:, :6].astype(F32).T
+    keep1, send1 = prep_weights(scal, [(w_qkv, 6), (small, 0), (w_cq, 2)])
+    keep2, send2 = prep_weights(scal, [(w_ckv, 4)], w_out)
+    keep3, send3 = prep_weights(scal, [(w_up, 2)])
+    blocks = prep_tokens(scal, ids, tokens, cotangent)
+    got1 = g.over_c(send1)
+    got2 = g.over_c(jnp.concatenate([send2, send3], 1))
+
+    def shape(kinds, rows, width):
+        return (2, kinds, 4, 2, rows, width)
+
+    n_qkv, n_cq, n_ckv, n_up = (w.shape[1] // 2 for w in (w_qkv, w_cq, w_ckv, w_up))
+    groups = tall // share // 2
+    low, high = (
+        list(half.reshape(groups, share, depth))
+        for half in (w_down[: tall // 2], w_down[tall // 2 :])
+    )
+    second = jnp.stack([keep2, jnp.concatenate([got2[:, :n_ckv], w_co], 1)])
+    third = jnp.stack(
+        [jnp.concatenate([keep3] + low, 1), jnp.concatenate([got2[:, n_ckv:]] + high, 1)]
+    )
+    first = after(jnp.stack([keep1, got1]), second, third)
+    tok, cot = list(blocks[:4]), list(blocks[4:])
+
+    def near(lines):
+        return g.over_x(lines[0]), g.over_y(lines[1])
+
+    def far(lines, got):
+        pair_a, pair_b = jnp.stack([lines[0], got[0]]), jnp.stack([lines[1], got[1]])
+        return pair_a, g.over_y(pair_a), pair_b, g.over_x(pair_b)
+
+    got_a = [first] + [g.xor_z(first, k) for k in (1, 2, 3)]
+    tok = [g.regroup(tok[0], 0)] + tok[1:]
+    line_a = gather_line(scal, got_a)
+    near_a = near(line_a)
+    tok[1:] = after(tok[1:], got_a)
+    tok[1:] = [g.regroup(tok[k], k) for k in (1, 2, 3)]
+    second = after(second, near_a, tok)
+    far_a = far(line_a, after(near_a, tok))
+    got_b = [second] + [g.xor_z(second, k) for k in (1, 2, 3)]
+    tok = after(tok, near_a)
+    resid = join_tokens(scal, tok, g.over_c(jnp.stack(tok)))
+    line_b = gather_line(scal, after(got_b, far_a))
+    near_b = near(line_b)
+    third = after(third, got_b, far_a)
+    got_c1 = g.xor_z(third, 1)
+    far_b = far(line_b, after(near_b, got_c1))
+    third_late = after(third, near_b, got_c1)
+    got_c = [third, got_c1] + [g.xor_z(third_late, k) for k in (2, 3)]
+    line_c = gather_line(scal, after(got_c, far_b))
+    near_c = near(line_c)
+    cot = [g.regroup(block, k) for k, block in enumerate(after(cot, got_c, far_b))]
+    far_c = far(line_c, after(near_c, cot))
+    cot = after(cot, near_c)
+    cot = join_tokens(scal, cot, g.over_c(jnp.stack(cot)))
+
+    qkv, small, cq = gather_place(
+        scal,
+        *far_a,
+        [shape(2, share, n_qkv), shape(2, share, 128), shape(2, share, n_cq)],
+        [[(n_qkv, 0, None, 0), (128, 1, None, 0), (n_cq, 2, None, 0)]] * 2,
+    )
+    ckv, out, co = gather_place(
+        scal,
+        *far_b,
+        [shape(2, share, n_ckv), shape(1, share, depth), shape(1, share, depth)],
+        [[(n_ckv, 0, None, 0), (depth, 1 + half, 0, 0)] for half in range(2)],
+    )
+    up, down = gather_place(
+        scal,
+        *far_c,
+        [shape(2, share, n_up), shape(1, tall, depth)],
+        [
+            [(n_up, 0, None, 0)]
+            + [(depth, 1, 0, (half * groups + i) * share) for i in range(groups)]
+            for half in range(2)
+        ],
+    )
 
     def flat(array):
         return array.reshape(-1, array.shape[-1])
 
-    return (small_all,) + tuple(
-        flat(a) for a in (qkv_all, out_all, cq_all, ckv_all, co_all, up_all, down_all)
-    )
+    return (
+        resid,
+        cot,
+        flat(small)[:, :6].astype(F32).T,
+    ) + tuple(flat(array) for array in (qkv, out, cq, ckv, co, up, down))
 
 
 def gather_plain(g, weights):
@@ -627,32 +862,6 @@
     parts = grad.reshape(2, rows // 2, width)
     whole = two(g, parts, jnp.zeros_like(parts), 1).reshape(2 * rows, width)
     return lax.psum_scatter(whole, AXES, scatter_dimension=0, tiled=True)
-
-
-def scatter_columns_fast(g, grad, rows, groups, order, step):
-    width = grad.shape[1]
-    terms = scatter(g, grad.astype(BF).reshape(2, 2, 4, 2, rows, width), order, step)
-    gone = plus(*[pick(term, 0, 1 - g.c) for term in terms])
-    got = g.over_c(gone)
-    keep = sum(pick(term, 0, g.c).astype(F32) for term in terms)
-    return join_columns(g, keep, got.astype(F32), groups)
-
-
-def scatter_rows_fast(g, grad, rows, order, step):
-    width = grad.shape[1]
-    terms = scatter(g, grad.astype(BF).reshape(2, 1, 4, 2, rows, width), order, step)
-    return sum(term[0].astype(F32) for term in terms)
-
-
-def chip_sum(g, value):
-    value = plus32(value, g.xor_z(value, 1))
-    value = plus32(value, g.xor_z(value, 2))
-    value = plus32(value, g.over_x(value))
-    return plus32(value, g.over_y(value))
-
-
-def plus32(a, b):
-    return (a.astype(F32) + b.astype(F32)).astype(a.dtype)
 
 
 def both_cores(g, part):
@@ -696,21 +905,24 @@
         mlp_down,
     )
 
+    scal = jnp.stack([g.x, g.c, g.z, g.y]).astype(jnp.int32)
     start = image_ids[:, 0] & 1
-    both = jnp.stack([tokens, cotangent], 2).reshape(4, STRIPE, 2 * depth)
-    received = []
-    for step in range(4):
-        j = (g.z + step) & 3
-        half = (j & 1) ^ start[j >> 1]
-        received.append(g.regroup(pick(both, 0, (j >> 1) * 2 + half), step))
-    mine = jnp.stack(received)
-    held = two(g, mine, g.over_c(mine), 1).reshape(8 * STRIPE, 2, depth)
-    resid = held[:, 0].astype(F32)
-    cot = held[:, 1]
-
-    (small, w_qkv, w_out, w_cq, w_ckv, w_co, w_up, w_down) = (
-        gather_fast(g, weights) if fast else gather_plain(g, weights)
-    )
+    if fast:
+        (resid, cot, small, w_qkv, w_out, w_cq, w_ckv, w_co, w_up, w_down) = gather_fast(
+            g, scal, weights, image_ids, tokens, cotangent
+        )
+    else:
+        (small, w_qkv, w_out, w_cq, w_ckv, w_co, w_up, w_down) = gather_plain(g, weights)
+        both = jnp.stack([tokens, cotangent], 2).reshape(4, STRIPE, 2 * depth)
+        received = []
+        for step in range(4):
+            j = g.z ^ step
+            half = (j & 1) ^ start[j >> 1]
+            received.append(g.regroup(pick(both, 0, (j >> 1) * 2 + half), step))
+        mine = jnp.stack(received)
+        held = two(g, mine, g.over_c(mine), 1).reshape(8 * STRIPE, 2, depth)
+        resid, cot = held[:, 0], held[:, 1]
+    resid = resid.astype(F32)
     gain, shift = small[:3], small[3:]
 
     image = (g.x * 2 + g.y) * 2 + (g.z & 1)
@@ -752,6 +964,10 @@
     )
     d_up = (mm_cols(cot, w_down) * slope).astype(BF)
     grad_up = mm_rows(n_three, d_up)
+    share = depth // g.count
+    if fast:
+        grad_down, grad_up = grad_down.astype(BF), grad_up.astype(BF)
+        mlp = Scatter(g, scal, share, by_rows(grad_down, share) + by_columns(grad_up, share)).far()
     added, gain_three, shift_three = norm_back(
         unit_three, spread_three, gain[2], both_cores(g, mm_cols(d_up, w_up))
     )
@@ -768,49 +984,100 @@
     d_self = g_one.astype(BF)
     grad_out = mm_rows(attended, d_self)
     d_att = mm_cols(d_self, w_out).astype(BF)
-    d_qkv = attn_bwd(slot, qkv, d_att, scale) if fast else long_bwd(g, saved, d_att, scale)
+    if fast:
+        grad_co, grad_cq = grad_co.astype(BF), grad_cq.astype(BF)
+        cross = Scatter(g, scal, share, by_rows(grad_co, share) + by_columns(grad_cq, share))
+        d_ckv = jnp.concatenate([d_ck, d_cv], 1).astype(BF)
+        swapped = g.xor_z(d_ckv, 1)
+        mlp.near()
+        d_att, swapped = after((d_att, swapped), mlp.folded)
+        d_ckv = plus(d_ckv, swapped)
+        swapped = g.xor_z(d_ckv, 2)
+        d_qkv = attn_bwd(slot, qkv, d_att, scale)
+        mlp_line = mlp.line()
+        cross.far()
+        d_qkv, swapped = after((d_qkv, swapped), mlp_line, cross.folded)
+        mlp_terms = spread(g, mlp_line)
+        d_ckv = plus(d_ckv, swapped)
+    else:
+        d_qkv = long_bwd(g, saved, d_att, scale)
     grad_qkv = mm_rows(n_one, d_qkv)
     added, gain_one, shift_one = norm_back(
         unit_one, spread_one, gain[0], both_cores(g, mm_cols(d_qkv, w_qkv))
     )
     grad_in = (g_one + added).astype(BF)
 
-    def home(mine):
-        back = jnp.stack([g.regroup(mine[step], -step) for step in range(4)])
+    norms = jnp.stack([gain_one, gain_two, gain_three, shift_one, shift_two, shift_three])
+    back = jnp.concatenate([out, halves(grad_in)[0]], 2)
+    if fast:
+        grad_out, grad_qkv = grad_out.astype(BF), grad_qkv.astype(BF)
+        cross.near()
+        last = Scatter(
+            g, scal, share, by_rows(grad_out, share) + by_columns(grad_qkv, share)
+        )
+        last.far(cross.near_a, cross.near_b)
+        back, mlp_terms = after((back, mlp_terms), last.folded, last.far_a, last.far_b)
+        last.near()
+        back = [g.regroup(back[step], step) for step in range(4)]
+        mlp_terms = after(mlp_terms, last.folded)
+        lines = [jnp.concatenate(pair, 2) for pair in zip(cross.line(), last.line())]
+        last_terms = spread(g, after(lines, back))
+        d_ckv, norms, mlp_terms = after(
+            (d_ckv, norms, mlp_terms), lines, last.near_a, last.near_b
+        )
+        d_ckv = plus(d_ckv, g.over_x(d_ckv))
+        norms = norms + g.over_y(norms)
+        d_ckv = plus(d_ckv, g.over_y(d_ckv))
+        norms = norms + g.over_x(norms)
+        norms = norms + g.xor_z(norms, 1)
+        norms = norms + g.xor_z(norms, 2)
+        norms = lax.dynamic_slice_in_dim(norms, g.me * share, share, 1)
+        output, grad_tokens = place_home(scal, image_ids, back)
+        n_cross = cross.width()
+        cross_terms = [term[:, :, : n_cross] for term in last_terms]
+        last_terms = [term[:, :, n_cross:] for term in last_terms]
+        d_ckv_whole = join_columns(g, d_ckv, g.over_c(d_ckv), 4)
+    else:
+        back = jnp.stack([g.regroup(back[step], step) for step in range(4)])
         order = []
         for block in range(4):
             j = (block & 2) + ((block & 1) ^ start[block >> 1])
-            order.append(pick(back, 0, (j - g.z) & 3))
-        return jnp.stack(order).reshape(2, 2 * STRIPE, depth)
-
-    output = home(out)
-    grad_tokens = home(halves(grad_in)[0]).astype(F32)
-
-    d_ckv = jnp.concatenate([d_ck, d_cv], 1)
-    norms = jnp.stack([gain_one, gain_two, gain_three, shift_one, shift_two, shift_three])
-    if fast:
-        d_ckv = chip_sum(g, d_ckv.astype(BF))
-        norms = chip_sum(g, norms)
-        d_ckv_whole = join_columns(g, d_ckv, g.over_c(d_ckv), 4)
-    else:
+            order.append(pick(back, 0, j ^ g.z))
+        back = jnp.stack(order).reshape(2, 2 * STRIPE, 2 * depth)
+        output, grad_tokens = back[:, :, :depth], back[:, :, depth:].astype(F32)
+        d_ckv = jnp.concatenate([d_ck, d_cv], 1)
         whole = join_columns(g, d_ckv, jnp.zeros_like(d_ckv), 4)
         d_ckv_whole = lax.psum(whole, AXES).astype(BF)
         d_ckv = column_halves(d_ckv_whole, 4, g.c)[0]
         norms = lax.psum(norms, AXES) * 0.5
+        norms = lax.dynamic_slice_in_dim(norms, g.me * (depth // g.count), depth // g.count, 1)
     part = mm_cols(d_ckv, w_ckv)
     grad_text = part + g.over_c(part)
-    share = depth // g.count
     text_cols = lax.dynamic_slice_in_dim(text_states, g.me * share, share, 1)
     grad_ckv = mm_rows(text_cols, d_ckv_whole)
-    norms = lax.dynamic_slice_in_dim(norms, g.me * share, share, 1)
-
     if fast:
-        grad_down = scatter_rows_fast(g, grad_down, mlp_down.shape[0], "yxz", 1)
-        grad_up = scatter_columns_fast(g, grad_up, share, 2, "xyz", -1)
-        grad_co = scatter_rows_fast(g, grad_co, share, "zxy", 1)
-        grad_cq = scatter_columns_fast(g, grad_cq, share, 2, "zxy", -1)
-        grad_out = scatter_rows_fast(g, grad_out, share, "zxy", 1)
-        grad_qkv = scatter_columns_fast(g, grad_qkv, share, 6, "zyx", -1)
+        tall = mlp_down.shape[0]
+
+        def columns(terms, low, high, groups):
+            got = g.over_c(plus(*[pick(term, 0, 1 - g.c)[:, low:high] for term in terms]))
+            keep = sum(pick(term, 0, g.c)[:, low:high].astype(F32) for term in terms)
+            return join_columns(g, keep, got.astype(F32), groups)
+
+        terms = mlp_terms
+        n_down = tall // share // 2 * depth
+        grad_down = summed(terms, ALL, ALL, slice(0, n_down))
+        grad_down = grad_down.reshape(2, share, tall // share // 2, depth)
+        grad_down = grad_down.transpose(0, 2, 1, 3).reshape(tall, depth)
+        grad_up = columns(terms, n_down, None, 2)
+        terms = cross_terms
+        half = depth // 2
+        co = summed(terms, ALL, ALL, slice(0, half))
+        grad_co = jnp.concatenate([co[0], co[1]], 1)
+        grad_cq = columns(terms, half, None, 2)
+        terms = last_terms
+        out_sum = summed(terms, ALL, ALL, slice(0, half))
+        grad_out = jnp.concatenate([out_sum[0], out_sum[1]], 1)
+        grad_qkv = columns(terms, half, None, 6)
     else:
         grad_down = scatter_rows_plain(g, grad_down)
         grad_up = scatter_columns_plain(g, grad_up, 2)

time: 1180 us -> 529 us (0.45)
  Pallas kernels: 665 us -> 76.9 us
  other arithmetic: 94.8 us -> 39.9 us
  waiting for transfers between devices: 166 us -> 203 us
  starting transfers between devices: 135 us -> 113 us
    pallas_call x8 -> x6, Pallas kernels: 627 us -> 15.4 us  [place(): pl.pallas_call(kernel, out_shape=[jax.ShapeDtypeStruct(shape, BF) for sha...]
    ppermute x92 -> x74, waiting for transfers between devices: 166 us -> 203 us  [send(): return lax.ppermute(value, AXES, perm)]
    convert_element_type x21 -> x7, other arithmetic: 32.7 us -> 4.31 us  [plus(): return total.astype(BF)]
    pallas_call x0 -> x16, Pallas kernels: none -> 23.6 us  [the longest x9 17.2 us: fold(): pl.pallas_call(kernel, grid_spec=pltpu.PrefetchScalarGridSpec(num_scalar_...]
    unnamed x149 -> x251, local copies, waits for them, and re-layouts: 8.15 us -> 30.6 us
    ppermute x92 -> x74, starting transfers between devices: 135 us -> 113 us  [send(): return lax.ppermute(value, AXES, perm)]
    convert_element_type x18 -> x0, other arithmetic: 14.8 us -> none  [the longest x4 7.07 us: plus32(): return (a.astype(F32) + b.astype(F32)).astype(a.dtype)]
  transfers between devices with their start and end apart: 92 -> 74, of which waited for: 30 -> 33; matrix products, arithmetic and copies ran while one was open for 14% -> 15% of each run, Pallas kernels for 57% -> 12%
where the time goes in v2:
time: 529 us; the launch traced here: 521 us
  waiting for transfers between devices  203 us (38%)
  starting transfers between devices  113 us (21%)
  Pallas kernels  76.9 us (15%)
  local copies, waits for them, and re-layouts  48.8 us (9%)
  other arithmetic  39.9 us (8%)
  matrix products  36.8 us (7%)
    ppermute x74, waiting for transfers between devices, send(): return lax.ppermute(value, AXES, perm)  203 us
    ppermute x74, starting transfers between devices, send(): return lax.ppermute(value, AXES, perm)  113 us
    unnamed x251, local copies, waits for them, and re-layouts  30.6 us
    pallas_call x1, Pallas kernels, attn_bwd(): pl.pallas_call(functools.partial(attn_bwd_kernel, scale=scale, pairs=pair...  17.4 us
    pallas_call x9, Pallas kernels, fold(): pl.pallas_call(kernel, grid_spec=pltpu.PrefetchScalarGridSpec(num_scalar_...  17.2 us
    pallas_call x6, Pallas kernels, place(): pl.pallas_call(kernel, out_shape=[jax.ShapeDtypeStruct(shape, BF) for sha...  15.4 us
    dot_general x7, matrix products, mm(): return jnp.dot(left, right, preferred_element_type=F32)  13.1 us
    dot_general x7, matrix products, mm_cols(): lax.dot_general(left, right, (((1,), (1,)), ((), ())), preferred_element_...  13 us
  transfers between devices with their start and end apart: 74, of which 33 were waited for; matrix products, arithmetic and copies ran while one was open for 15% of the time, Pallas kernels for 12%

profile of v2, /device:TPU:0, one launch (start us, length us, event | category | flops | bytes accessed | tf_op | source)
XLA Modules:
  0.0 521.4 jit_solution(16174671924977421744)
XLA Ops:
  10.0 4.8 collective-permute-start.5
  15.5 6.9 %collective-permute-done.5.refs_3_ = bf16[2,32,2176]{2,1,0:T(8,128)(2,1)S(1)} collective-permute-done((bf16[2,32,2176]{2,1,0:T(8,128)(2,1)S(1)}, bf16[2,32,2176]{2,1,0:T(8,128)(2,1)S(1)}, u32[]{:S(2)}, u32[]{:S(2)}) %collective-permute-start.5) | collective-permute-done | bytes 278560 | tf_op jit(solution)/shard_map/ppermute | solution.py:64
  22.4 16.6 %collective-permute-done.4.refs_2_ = bf16[2,32,2176]{2,1,0:T(8,128)(2,1)S(1)} collective-permute-done((bf16[2,32,2176]{2,1,0:T(8,128)(2,1)S(1)}, bf16[2,32,2176]{2,1,0:T(8,128)(2,1)S(1)}, u32[]{:S(2)}, u32[]{:S(2)}) %collective-permute-start.4) | collective-permute-done | bytes 278560 | tf_op jit(solution)/shard_map/ppermute | solution.py:64
  45.7 3.0 collective-permute-start.7
  50.1 3.1 collective-permute-done.6.a1
  53.2 3.6 collective-permute-done.8.a3
  56.7 3.0 collective-permute-done.10
  59.9 9.3 %collective-permute-start.12 = (bf16[2,4,32,2176]{3,2,1,0:T(8,128)(2,1)S(1)}, bf16[2,4,32,2176]{3,2,1,0:T(8,128)(2,1)S(1)}, u32[]{:S(2)}, u32[]{:S(2)}) collective-permute-start(bf16[2,4,32,2176]{3,2,1,0:T(8,128)(2,1)S(1)} %pad_maximum_fusion.2.refs_0_), channel_id=1, source_target_pairs={{0,1},{1,0},{2,3},{3,2},{4,5},{5,4},{6,7},{7,6},{8,9},{9,8},{10,11... | collective-permute-start | bytes 3342344 | tf_op jit(solution)/shard_map/ppermute | solution.py:64
  76.1 5.9 %collective-permute-done.16.refs_3_ = bf16[2,32,2048]{2,1,0:T(8,128)(2,1)S(1)} collective-permute-done((bf16[2,32,2048]{2,1,0:T(8,128)(2,1)S(1)}, bf16[2,32,2048]{2,1,0:T(8,128)(2,1)S(1)}, u32[]{:S(2)}, u32[]{:S(2)}) %collective-permute-start.16) | collective-permute-done | bytes 262176 | tf_op jit(solution)/shard_map/ppermute | solution.py:64
  82.0 9.7 %collective-permute-done.15.refs_2_ = bf16[2,32,2048]{2,1,0:T(8,128)(2,1)S(1)} collective-permute-done((bf16[2,32,2048]{2,1,0:T(8,128)(2,1)S(1)}, bf16[2,32,2048]{2,1,0:T(8,128)(2,1)S(1)}, u32[]{:S(2)}, u32[]{:S(2)}) %collective-permute-start.15) | collective-permute-done | bytes 262176 | tf_op jit(solution)/shard_map/ppermute | solution.py:64
  91.7 2.6 collective-permute-done.12.refs_1_
  96.3 3.0 shard_map.254
  105.5 4.5 collective-permute-done.19.refs_1_
  110.1 3.3 collective-permute-done.17
  121.0 2.5 collective-permute-start.25
  129.0 8.8 %collective-permute-done.25.refs_3_ = bf16[2,32,4096]{2,1,0:T(8,128)(2,1)} collective-permute-done((bf16[2,32,4096]{2,1,0:T(8,128)(2,1)S(1)}, bf16[2,32,4096]{2,1,0:T(8,128)(2,1)}, u32[]{:S(2)}, u32[]{:S(2)}) %collective-permute-start.25) | collective-permute-done | bytes 524320 | tf_op jit(solution)/shard_map/ppermute | solution.py:64
  137.8 29.6 %collective-permute-done.24.refs_2_ = bf16[2,32,4096]{2,1,0:T(8,128)(2,1)} collective-permute-done((bf16[2,32,4096]{2,1,0:T(8,128)(2,1)S(1)}, bf16[2,32,4096]{2,1,0:T(8,128)(2,1)}, u32[]{:S(2)}, u32[]{:S(2)}) %collective-permute-start.24) | collective-permute-done | bytes 524320 | tf_op jit(solution)/shard_map/ppermute | solution.py:64
  171.7 3.8 convolution_convert_fusion.3.q_ref.k_ref.v_ref
  175.6 9.1 %shard_map.253 = bf16[512,512]{1,0:T(8,128)(2,1)S(1)} custom-call(s32[1]{0:T(128)} %bitcast.2.z_ref, bf16[512,1536]{1,0:T(8,128)(2,1)S(1)} %convolution_convert_fusion.3.q_ref.k_ref.v_ref, bf16[512,1536]{1,0:T(8,128)(2,1)S(1)} %convolution_convert_fusion.3.q_ref.k_ref.v_ref, bf16[512,1536]{1,0:T(8,128)(2,1)S(1)} %convolution_convert_fusion.3.q_ref.k_ref.v_ref), custom_call_target="tpu_custom_call" | custom-call | flops 536870912 | bytes 2359296 | tf_op jit(solution)/shard_map/pallas_call | solution.py:462
  186.0 3.0 collective-permute-start.30
  189.0 2.9 shard_map.255
  194.3 6.5 %collective-permute-start.22 = (bf16[512,1024]{1,0:T(8,128)(2,1)S(1)}, bf16[512,1024]{1,0:T(8,128)(2,1)S(1)}, u32[]{:S(2)}, u32[]{:S(2)}) collective-permute-start(bf16[512,1024]{1,0:T(8,128)(2,1)S(1)} %convolution_convert_fusion.10), channel_id=1, source_target_pairs={{0,8},{1,9},{2,10},{3,11},{4,12},{5,13},{6,14},{7,15},{8,0},{9,1},... | collective-permute-start | bytes 3145736 | tf_op jit(solution)/shard_map/ppermute | solution.py:64
  205.7 4.5 collective-permute-start.32
  213.6 4.6 shard_map.256
  230.3 18.5 %collective-permute-done.33.refs_3_ = bf16[2,4,32,4096]{3,2,1,0:T(8,128)(2,1)} collective-permute-done((bf16[2,4,32,4096]{3,2,1,0:T(8,128)(2,1)}, bf16[2,4,32,4096]{3,2,1,0:T(8,128)(2,1)}, u32[]{:S(2)}, u32[]{:S(2)}) %collective-permute-start.33) | collective-permute-done | bytes 2097184 | tf_op jit(solution)/shard_map/ppermute | solution.py:64
  248.8 8.2 %collective-permute-done.32.refs_1_ = bf16[2,4,32,4096]{3,2,1,0:T(8,128)(2,1)} collective-permute-done((bf16[2,4,32,4096]{3,2,1,0:T(8,128)(2,1)}, bf16[2,4,32,4096]{3,2,1,0:T(8,128)(2,1)}, u32[]{:S(2)}, u32[]{:S(2)}) %collective-permute-start.32) | collective-permute-done | bytes 2097184 | tf_op jit(solution)/shard_map/ppermute | solution.py:64
  257.0 4.2 shard_map.258
  261.2 3.3 multiply_convert_fusion
  264.5 4.7 fusion.6
  274.2 2.7 convolution_convert_fusion.1
  283.8 6.7 %shard_map.260 = (bf16[512,512]{1,0:T(8,128)(2,1)S(1)}, f32[128,512]{1,0:T(8,128)S(1)}, f32[128,512]{1,0:T(8,128)S(1)}) custom-call(s32[1]{0:T(128)} %bitcast.29.cap_ref, s32[1,128]{1,0:T(1,128)S(1)} %bitcast.257, bf16[512,512]{1,0:T(8,128)(2,1)S(1)} %copy-done.20, bf16[128,1024]{1,0:T(8,128)(2,1)S(1)} %fusion.33.k_ref.v_ref, ...), custom_call_target="tpu_custom_call" | custom-call | flops 335544320 | bytes 1572864 | tf_op jit(solution)/shard_map/pallas_call | solution.py:619
  298.4 27.5 %collective-permute-done.39.refs_3_ = bf16[8,32,4096]{2,1,0:T(8,128)(2,1)S(1)} collective-permute-done((bf16[8,32,4096]{2,1,0:T(8,128)(2,1)S(1)}, bf16[8,32,4096]{2,1,0:T(8,128)(2,1)S(1)}, u32[]{:S(2)}, u32[]{:S(2)}) %collective-permute-start.39) | collective-permute-done | bytes 2097184 | tf_op jit(solution)/shard_map/ppermute | solution.py:64
  335.5 17.4 %shard_map.263 = bf16[512,1536]{1,0:T(8,128)(2,1)S(1)} custom-call(s32[1]{0:T(128)} %bitcast.2.z_ref, bf16[512,1536]{1,0:T(8,128)(2,1)S(1)} %convolution_convert_fusion.3.q_ref.k_ref.v_ref, bf16[512,1536]{1,0:T(8,128)(2,1)S(1)} %convolution_convert_fusion.3.q_ref.k_ref.v_ref, bf16[512,1536]{1,0:T(8,128)(2,1)S(1)} %convolution_convert_fusion.3.q_ref.k_ref.v_ref, ...), custom_call_target="tpu_custom_call" | custom-call | flops 1342177280 | bytes 3932160 | tf_op jit(solution)/shard_map/pallas_call | solution.py:527
  355.9 2.8 convolution_convert_fusion.4
  358.8 4.5 collective-permute-done.48.refs_2_
  374.1 2.8 shard_map.270
  377.9 3.0 collective-permute-start.46
  387.6 3.3 fusion.20
  393.4 5.5 %collective-permute-done.45 = bf16[2,32,4096]{2,1,0:T(8,128)(2,1)S(1)} collective-permute-done((bf16[2,32,4096]{2,1,0:T(8,128)(2,1)S(1)}, bf16[2,32,4096]{2,1,0:T(8,128)(2,1)S(1)}, u32[]{:S(2)}, u32[]{:S(2)}) %collective-permute-start.45) | collective-permute-done | bytes 524320 | tf_op jit(solution)/shard_map/ppermute | solution.py:64
  398.9 17.4 %collective-permute-done.46 = bf16[2,32,4096]{2,1,0:T(8,128)(2,1)S(1)} collective-permute-done((bf16[2,32,4096]{2,1,0:T(8,128)(2,1)S(1)}, bf16[2,32,4096]{2,1,0:T(8,128)(2,1)S(1)}, u32[]{:S(2)}, u32[]{:S(2)}) %collective-permute-start.46) | collective-permute-done | bytes 524320 | tf_op jit(solution)/shard_map/ppermute | solution.py:64
  417.3 2.5 collective-permute-start.57
  426.1 13.1 %collective-permute-start.56 = (bf16[64,2048]{1,0:T(8,128)(2,1)}, bf16[64,2048]{1,0:T(8,128)(2,1)}, u32[]{:S(2)}, u32[]{:S(2)}) collective-permute-start(bf16[64,2048]{1,0:T(8,128)(2,1)} %get-tuple-element.264), channel_id=1, source_target_pairs={{0,4},{1,12},{2,6},{3,14},{4,0},{5,8},{6,2},{7,10},{8,5},{9,13},{1... | collective-permute-start | bytes 786440 | tf_op jit(solution)/shard_map/ppermute | solution.py:64
  440.0 3.6 collective-permute-start.54
  446.3 5.6 %collective-permute-done.56.a2 = bf16[64,2048]{1,0:T(8,128)(2,1)} collective-permute-done((bf16[64,2048]{1,0:T(8,128)(2,1)}, bf16[64,2048]{1,0:T(8,128)(2,1)}, u32[]{:S(2)}, u32[]{:S(2)}) %collective-permute-start.56) | collective-permute-done | bytes 262176 | tf_op jit(solution)/shard_map/ppermute | solution.py:64
  459.0 3.4 shard_map.271
  473.6 7.2 %collective-permute-start.65 = (f32[6,1024]{1,0:T(8,128)S(1)}, f32[6,1024]{1,0:T(8,128)S(1)}, u32[]{:S(2)}, u32[]{:S(2)}) collective-permute-start(f32[6,1024]{1,0:T(8,128)S(1)} %add.318), channel_id=1, source_target_pairs={{0,2},{1,3},{2,0},{3,1},{4,6},{5,7},{6,4},{7,5},{8,10},{9,11},{10,... | collective-permute-start | bytes 73736 | tf_op jit(solution)/shard_map/ppermute | solution.py:64
  483.4 2.7 collective-permute-start.66
  502.2 5.5 %collective-permute-done.68 = bf16[2,32,3072]{2,1,0:T(8,128)(2,1)S(1)} collective-permute-done((bf16[2,32,3072]{2,1,0:T(8,128)(2,1)}, bf16[2,32,3072]{2,1,0:T(8,128)(2,1)S(1)}, u32[]{:S(2)}, u32[]{:S(2)}) %collective-permute-start.68) | collective-permute-done | bytes 393248 | tf_op jit(solution)/shard_map/ppermute | solution.py:64
  (521 shorter events, 187.9 us)
Async XLA Ops:
  10.0 12.4 %collective-permute-start.5 = (bf16[2,32,2176]{2,1,0:T(8,128)(2,1)S(1)}, bf16[2,32,2176]{2,1,0:T(8,128)(2,1)S(1)}, u32[]{:S(2)}, u32[]{:S(2)}) collective-permute-start(bf16[2,32,2176]{2,1,0:T(8,128)(2,1)S(1)} %pad_maximum_fusion.13.refs_0_), channel_id=1, source_target_pairs={{0,6},{1,7},{2,4},{3,5},{4,2},{5,3},{6,0},{7,1},{8,14},{9,15},{10,... | collective-permute-start | bytes 835592 | tf_op jit(solution)/shard_map/ppermute | solution.py:64
  14.8 24.2 %collective-permute-start.4 = (bf16[2,32,2176]{2,1,0:T(8,128)(2,1)S(1)}, bf16[2,32,2176]{2,1,0:T(8,128)(2,1)S(1)}, u32[]{:S(2)}, u32[]{:S(2)}) collective-permute-start(bf16[2,32,2176]{2,1,0:T(8,128)(2,1)S(1)} %pad_maximum_fusion.13.refs_0_), channel_id=1, source_target_pairs={{0,4},{1,5},{2,6},{3,7},{4,0},{5,1},{6,2},{7,3},{8,12},{9,13},{10,... | collective-permute-start | bytes 835592 | tf_op jit(solution)/shard_map/ppermute | solution.py:64
  14.8 24.2 %collective-permute-start.3 = (bf16[2,32,2176]{2,1,0:T(8,128)(2,1)S(1)}, bf16[2,32,2176]{2,1,0:T(8,128)(2,1)S(1)}, u32[]{:S(2)}, u32[]{:S(2)}) collective-permute-start(bf16[2,32,2176]{2,1,0:T(8,128)(2,1)S(1)} %pad_maximum_fusion.13.refs_0_), channel_id=1, source_target_pairs={{0,2},{1,3},{2,0},{3,1},{4,6},{5,7},{6,4},{7,5},{8,10},{9,11},{10,... | collective-permute-start | bytes 835592 | tf_op jit(solution)/shard_map/ppermute | solution.py:64
  41.2 15.6 %collective-permute-start.9 = (bf16[4,32,2176]{2,1,0:T(8,128)(2,1)S(1)}, bf16[4,32,2176]{2,1,0:T(8,128)(2,1)S(1)}, u32[]{:S(2)}, u32[]{:S(2)}) collective-permute-start(bf16[4,32,2176]{2,1,0:T(8,128)(2,1)S(1)} %get-tuple-element.142), channel_id=1, source_target_pairs={{0,16},{1,17},{2,18},{3,19},{4,20},{5,21},{6,22},{7,23},{8,24},{9,... | collective-permute-start | bytes 1671176 | tf_op jit(solution)/shard_map/ppermute | solution.py:64
  42.7 17.0 %collective-permute-start.10 = (bf16[4,32,2176]{2,1,0:T(8,128)(2,1)S(1)}, bf16[4,32,2176]{2,1,0:T(8,128)(2,1)S(1)}, u32[]{:S(2)}, u32[]{:S(2)}) collective-permute-start(bf16[4,32,2176]{2,1,0:T(8,128)(2,1)S(1)} %get-tuple-element.143), channel_id=1, source_target_pairs={{0,1},{1,0},{2,3},{3,2},{4,5},{5,4},{6,7},{7,6},{8,9},{9,8},{10,11... | collective-permute-start | bytes 1671176 | tf_op jit(solution)/shard_map/ppermute | solution.py:64
  59.9 34.4 %collective-permute-start.12 = (bf16[2,4,32,2176]{3,2,1,0:T(8,128)(2,1)S(1)}, bf16[2,4,32,2176]{3,2,1,0:T(8,128)(2,1)S(1)}, u32[]{:S(2)}, u32[]{:S(2)}) collective-permute-start(bf16[2,4,32,2176]{3,2,1,0:T(8,128)(2,1)S(1)} %pad_maximum_fusion.2.refs_0_), channel_id=1, source_target_pairs={{0,1},{1,0},{2,3},{3,2},{4,5},{5,4},{6,7},{7,6},{8,9},{9,8},{10,11... | collective-permute-start | bytes 3342344 | tf_op jit(solution)/shard_map/ppermute | solution.py:64
  69.3 26.0 %collective-permute-start.13 = (bf16[2,4,32,2176]{3,2,1,0:T(8,128)(2,1)S(1)}, bf16[2,4,32,2176]{3,2,1,0:T(8,128)(2,1)S(1)}, u32[]{:S(2)}, u32[]{:S(2)}) collective-permute-start(bf16[2,4,32,2176]{3,2,1,0:T(8,128)(2,1)S(1)} %pad_maximum_fusion.3.refs_2_), channel_id=1, source_target_pairs={{0,16},{1,17},{2,18},{3,19},{4,20},{5,21},{6,22},{7,23},{8,24},{9,... | collective-permute-start | bytes 3342344 | tf_op jit(solution)/shard_map/ppermute | solution.py:64
  73.4 18.3 %collective-permute-start.15 = (bf16[2,32,2048]{2,1,0:T(8,128)(2,1)S(1)}, bf16[2,32,2048]{2,1,0:T(8,128)(2,1)S(1)}, u32[]{:S(2)}, u32[]{:S(2)}) collective-permute-start(bf16[2,32,2048]{2,1,0:T(8,128)(2,1)S(1)} %pad_maximum_fusion.14.refs_0_), channel_id=1, source_target_pairs={{0,4},{1,5},{2,6},{3,7},{4,0},{5,1},{6,2},{7,3},{8,12},{9,13},{10,... | collective-permute-start | bytes 786440 | tf_op jit(solution)/shard_map/ppermute | solution.py:64
  73.4 18.3 %collective-permute-start.14 = (bf16[2,32,2048]{2,1,0:T(8,128)(2,1)S(1)}, bf16[2,32,2048]{2,1,0:T(8,128)(2,1)S(1)}, u32[]{:S(2)}, u32[]{:S(2)}) collective-permute-start(bf16[2,32,2048]{2,1,0:T(8,128)(2,1)S(1)} %pad_maximum_fusion.14.refs_0_), channel_id=1, source_target_pairs={{0,2},{1,3},{2,0},{3,1},{4,6},{5,7},{6,4},{7,5},{8,10},{9,11},{10,... | collective-permute-start | bytes 786440 | tf_op jit(solution)/shard_map/ppermute | solution.py:64
  82.0 19.4 %collective-permute-start.11 = (bf16[4,64,1024]{2,1,0:T(8,128)(2,1)}, bf16[4,64,1024]{2,1,0:T(8,128)(2,1)}, u32[]{:S(2)}, u32[]{:S(2)}) collective-permute-start(bf16[4,64,1024]{2,1,0:T(8,128)(2,1)} %pad_maximum_fusion.8), channel_id=1, source_target_pairs={{0,8},{1,9},{2,10},{3,11},{4,12},{5,13},{6,14},{7,15},{8,0},{9,1},... | collective-permute-start | bytes 1572872 | tf_op jit(solution)/shard_map/ppermute | solution.py:64
  96.3 13.8 %collective-permute-start.19 = (bf16[2,32,4096]{2,1,0:T(8,128)(2,1)S(1)}, bf16[2,32,4096]{2,1,0:T(8,128)(2,1)}, u32[]{:S(2)}, u32[]{:S(2)}) collective-permute-start(bf16[2,32,4096]{2,1,0:T(8,128)(2,1)S(1)} %pad_maximum_fusion.7.refs_0_), channel_id=1, source_target_pairs={{0,2},{1,3},{2,0},{3,1},{4,6},{5,7},{6,4},{7,5},{8,10},{9,11},{10,... | collective-permute-start | bytes 1572872 | tf_op jit(solution)/shard_map/ppermute | solution.py:64
  99.3 14.1 %collective-permute-start.17 = (bf16[4,32,2048]{2,1,0:T(8,128)(2,1)}, bf16[4,32,2048]{2,1,0:T(8,128)(2,1)}, u32[]{:S(2)}, u32[]{:S(2)}) collective-permute-start(bf16[4,32,2048]{2,1,0:T(8,128)(2,1)} %get-tuple-element.157), channel_id=1, source_target_pairs={{0,16},{1,17},{2,18},{3,19},{4,20},{5,21},{6,22},{7,23},{8,24},{9,... | collective-permute-start | bytes 1572872 | tf_op jit(solution)/shard_map/ppermute | solution.py:64
  99.9 13.7 %collective-permute-start.18 = (bf16[4,32,2048]{2,1,0:T(8,128)(2,1)}, bf16[4,32,2048]{2,1,0:T(8,128)(2,1)}, u32[]{:S(2)}, u32[]{:S(2)}) collective-permute-start(bf16[4,32,2048]{2,1,0:T(8,128)(2,1)} %get-tuple-element.158), channel_id=1, source_target_pairs={{0,1},{1,0},{2,3},{3,2},{4,5},{5,4},{6,7},{7,6},{8,9},{9,8},{10,11... | collective-permute-start | bytes 1572872 | tf_op jit(solution)/shard_map/ppermute | solution.py:64
  116.0 51.5 %collective-permute-start.21 = (bf16[2,4,32,2048]{3,2,1,0:T(8,128)(2,1)}, bf16[2,4,32,2048]{3,2,1,0:T(8,128)(2,1)}, u32[]{:S(2)}, u32[]{:S(2)}) collective-permute-start(bf16[2,4,32,2048]{3,2,1,0:T(8,128)(2,1)} %pad_maximum_fusion.5.refs_2_), channel_id=1, source_target_pairs={{0,16},{1,17},{2,18},{3,19},{4,20},{5,21},{6,22},{7,23},{8,24},{9,... | collective-permute-start | bytes 3145736 | tf_op jit(solution)/shard_map/ppermute | solution.py:64
  119.7 47.7 %collective-permute-start.20 = (bf16[2,4,32,2048]{3,2,1,0:T(8,128)(2,1)}, bf16[2,4,32,2048]{3,2,1,0:T(8,128)(2,1)}, u32[]{:S(2)}, u32[]{:S(2)}) collective-permute-start(bf16[2,4,32,2048]{3,2,1,0:T(8,128)(2,1)} %pad_maximum_fusion.4.refs_0_), channel_id=1, source_target_pairs={{0,1},{1,0},{2,3},{3,2},{4,5},{5,4},{6,7},{7,6},{8,9},{9,8},{10,11... | collective-permute-start | bytes 3145736 | tf_op jit(solution)/shard_map/ppermute | solution.py:64
  121.0 16.9 %collective-permute-start.25 = (bf16[2,32,4096]{2,1,0:T(8,128)(2,1)S(1)}, bf16[2,32,4096]{2,1,0:T(8,128)(2,1)}, u32[]{:S(2)}, u32[]{:S(2)}) collective-permute-start(bf16[2,32,4096]{2,1,0:T(8,128)(2,1)S(1)} %pad_maximum_fusion.7.refs_0_), channel_id=1, source_target_pairs={{0,6},{1,7},{2,4},{3,5},{4,2},{5,3},{6,0},{7,1},{8,14},{9,15},{10,... | collective-permute-start | bytes 1572872 | tf_op jit(solution)/shard_map/ppermute | solution.py:64
  123.5 43.9 %collective-permute-start.24 = (bf16[2,32,4096]{2,1,0:T(8,128)(2,1)S(1)}, bf16[2,32,4096]{2,1,0:T(8,128)(2,1)}, u32[]{:S(2)}, u32[]{:S(2)}) collective-permute-start(bf16[2,32,4096]{2,1,0:T(8,128)(2,1)S(1)} %pad_maximum_fusion.7.refs_0_), channel_id=1, source_target_pairs={{0,4},{1,5},{2,6},{3,7},{4,0},{5,1},{6,2},{7,3},{8,12},{9,13},{10,... | collective-permute-start | bytes 1572872 | tf_op jit(solution)/shard_map/ppermute | solution.py:64
  169.5 31.9 %collective-permute-start.26 = (bf16[4,32,4096]{2,1,0:T(8,128)(2,1)S(1)}, bf16[4,32,4096]{2,1,0:T(8,128)(2,1)S(1)}, u32[]{:S(2)}, u32[]{:S(2)}) collective-permute-start(bf16[4,32,4096]{2,1,0:T(8,128)(2,1)S(1)} %get-tuple-element.171), channel_id=1, source_target_pairs={{0,16},{1,17},{2,18},{3,19},{4,20},{5,21},{6,22},{7,23},{8,24},{9,... | collective-permute-start | bytes 3145736 | tf_op jit(solution)/shard_map/ppermute | solution.py:64
  170.2 31.1 %collective-permute-start.27 = (bf16[4,32,4096]{2,1,0:T(8,128)(2,1)S(1)}, bf16[4,32,4096]{2,1,0:T(8,128)(2,1)S(1)}, u32[]{:S(2)}, u32[]{:S(2)}) collective-permute-start(bf16[4,32,4096]{2,1,0:T(8,128)(2,1)S(1)} %get-tuple-element.172), channel_id=1, source_target_pairs={{0,1},{1,0},{2,3},{3,2},{4,5},{5,4},{6,7},{7,6},{8,9},{9,8},{10,11... | collective-permute-start | bytes 3145736 | tf_op jit(solution)/shard_map/ppermute | solution.py:64
  186.0 15.3 %collective-permute-start.30 = (bf16[64,1024]{1,0:T(8,128)(2,1)S(1)}, bf16[64,1024]{1,0:T(8,128)(2,1)S(1)}, u32[]{:S(2)}, u32[]{:S(2)}) collective-permute-start(bf16[64,1024]{1,0:T(8,128)(2,1)S(1)} %copy-done.70), channel_id=1, source_target_pairs={{0,4},{1,12},{2,6},{3,14},{4,0},{5,8},{6,2},{7,10},{8,5},{9,13},{1... | collective-permute-start | bytes 393224 | tf_op jit(solution)/shard_map/ppermute | solution.py:64
  194.3 15.9 %collective-permute-start.22 = (bf16[512,1024]{1,0:T(8,128)(2,1)S(1)}, bf16[512,1024]{1,0:T(8,128)(2,1)S(1)}, u32[]{:S(2)}, u32[]{:S(2)}) collective-permute-start(bf16[512,1024]{1,0:T(8,128)(2,1)S(1)} %convolution_convert_fusion.10), channel_id=1, source_target_pairs={{0,8},{1,9},{2,10},{3,11},{4,12},{5,13},{6,14},{7,15},{8,0},{9,1},... | collective-permute-start | bytes 3145736 | tf_op jit(solution)/shard_map/ppermute | solution.py:64
  202.8 45.9 %collective-permute-start.33 = (bf16[2,4,32,4096]{3,2,1,0:T(8,128)(2,1)}, bf16[2,4,32,4096]{3,2,1,0:T(8,128)(2,1)}, u32[]{:S(2)}, u32[]{:S(2)}) collective-permute-start(bf16[2,4,32,4096]{3,2,1,0:T(8,128)(2,1)} %pad_maximum_fusion.1.refs_2_), channel_id=1, source_target_pairs={{0,16},{1,17},{2,18},{3,19},{4,20},{5,21},{6,22},{7,23},{8,24},{9,... | collective-permute-start | bytes 6291464 | tf_op jit(solution)/shard_map/ppermute | solution.py:64
  205.7 51.3 %collective-permute-start.32 = (bf16[2,4,32,4096]{3,2,1,0:T(8,128)(2,1)}, bf16[2,4,32,4096]{3,2,1,0:T(8,128)(2,1)}, u32[]{:S(2)}, u32[]{:S(2)}) collective-permute-start(bf16[2,4,32,4096]{3,2,1,0:T(8,128)(2,1)} %pad_maximum_fusion.refs_0_), channel_id=1, source_target_pairs={{0,1},{1,0},{2,3},{3,2},{4,5},{5,4},{6,7},{7,6},{8,9},{9,8},{10,11... | collective-permute-start | bytes 6291464 | tf_op jit(solution)/shard_map/ppermute | solution.py:64
  277.9 48.0 %collective-permute-start.39 = (bf16[8,32,4096]{2,1,0:T(8,128)(2,1)S(1)}, bf16[8,32,4096]{2,1,0:T(8,128)(2,1)S(1)}, u32[]{:S(2)}, u32[]{:S(2)}) collective-permute-start(bf16[8,32,4096]{2,1,0:T(8,128)(2,1)S(1)} %get-tuple-element.192), channel_id=1, source_target_pairs={{0,1},{1,0},{2,3},{3,2},{4,5},{5,4},{6,7},{7,6},{8,9},{9,8},{10,11... | collective-permute-start | bytes 6291464 | tf_op jit(solution)/shard_map/ppermute | solution.py:64
  278.2 47.7 %collective-permute-start.40 = (bf16[8,32,4096]{2,1,0:T(8,128)(2,1)S(1)}, bf16[8,32,4096]{2,1,0:T(8,128)(2,1)S(1)}, u32[]{:S(2)}, u32[]{:S(2)}) collective-permute-start(bf16[8,32,4096]{2,1,0:T(8,128)(2,1)S(1)} %get-tuple-element.193), channel_id=1, source_target_pairs={{0,16},{1,17},{2,18},{3,19},{4,20},{5,21},{6,22},{7,23},{8,24},{9,... | collective-permute-start | bytes 6291464 | tf_op jit(solution)/shard_map/ppermute | solution.py:64
  295.7 35.5 %collective-permute-start.38 = (bf16[128,1024]{1,0:T(8,128)(2,1)S(1)}, bf16[128,1024]{1,0:T(8,128)(2,1)S(1)}, u32[]{:S(2)}, u32[]{:S(2)}) collective-permute-start(bf16[128,1024]{1,0:T(8,128)(2,1)S(1)} %pad_maximum_fusion.15), channel_id=1, source_target_pairs={{0,2},{1,3},{2,0},{3,1},{4,6},{5,7},{6,4},{7,5},{8,10},{9,11},{10,... | collective-permute-start | bytes 786440 | tf_op jit(solution)/shard_map/ppermute | solution.py:64
  327.1 26.2 %collective-permute-start.42 = (bf16[4,32,4096]{2,1,0:T(8,128)(2,1)S(1)}, bf16[4,32,4096]{2,1,0:T(8,128)(2,1)S(1)}, u32[]{:S(2)}, u32[]{:S(2)}) collective-permute-start(bf16[4,32,4096]{2,1,0:T(8,128)(2,1)S(1)} %get-tuple-element.194), channel_id=1, source_target_pairs={{0,16},{1,17},{2,18},{3,19},{4,20},{5,21},{6,22},{7,23},{8,24},{9,... | collective-permute-start | bytes 3145736 | tf_op jit(solution)/shard_map/ppermute | solution.py:64
  327.8 26.1 %collective-permute-start.43 = (bf16[4,32,4096]{2,1,0:T(8,128)(2,1)S(1)}, bf16[4,32,4096]{2,1,0:T(8,128)(2,1)S(1)}, u32[]{:S(2)}, u32[]{:S(2)}) collective-permute-start(bf16[4,32,4096]{2,1,0:T(8,128)(2,1)S(1)} %get-tuple-element.195), channel_id=1, source_target_pairs={{0,1},{1,0},{2,3},{3,2},{4,5},{5,4},{6,7},{7,6},{8,9},{9,8},{10,11... | collective-permute-start | bytes 3145736 | tf_op jit(solution)/shard_map/ppermute | solution.py:64
  331.7 24.1 %collective-permute-start.41 = (bf16[128,1024]{1,0:T(8,128)(2,1)S(1)}, bf16[128,1024]{1,0:T(8,128)(2,1)S(1)}, u32[]{:S(2)}, u32[]{:S(2)}) collective-permute-start(bf16[128,1024]{1,0:T(8,128)(2,1)S(1)} %add_convert_fusion.5), channel_id=1, source_target_pairs={{0,4},{1,5},{2,6},{3,7},{4,0},{5,1},{6,2},{7,3},{8,12},{9,13},{10,... | collective-permute-start | bytes 786440 | tf_op jit(solution)/shard_map/ppermute | solution.py:64
  333.7 29.6 %collective-permute-start.48 = (bf16[8,32,1024]{2,1,0:T(8,128)(2,1)S(1)}, bf16[8,32,1024]{2,1,0:T(8,128)(2,1)S(1)}, u32[]{:S(2)}, u32[]{:S(2)}) collective-permute-start(bf16[8,32,1024]{2,1,0:T(8,128)(2,1)S(1)} %get-tuple-element.202), channel_id=1, source_target_pairs={{0,1},{1,0},{2,3},{3,2},{4,5},{5,4},{6,7},{7,6},{8,9},{9,8},{10,11... | collective-permute-start | bytes 1572872 | tf_op jit(solution)/shard_map/ppermute | solution.py:64
  334.1 29.2 %collective-permute-start.49 = (bf16[8,32,1024]{2,1,0:T(8,128)(2,1)S(1)}, bf16[8,32,1024]{2,1,0:T(8,128)(2,1)S(1)}, u32[]{:S(2)}, u32[]{:S(2)}) collective-permute-start(bf16[8,32,1024]{2,1,0:T(8,128)(2,1)S(1)} %get-tuple-element.203), channel_id=1, source_target_pairs={{0,16},{1,17},{2,18},{3,19},{4,20},{5,21},{6,22},{7,23},{8,24},{9,... | collective-permute-start | bytes 1572872 | tf_op jit(solution)/shard_map/ppermute | solution.py:64
  353.3 15.5 %collective-permute-start.34 = (bf16[4,64,1024]{2,1,0:T(8,128)(2,1)}, bf16[4,64,1024]{2,1,0:T(8,128)(2,1)S(1)}, u32[]{:S(2)}, u32[]{:S(2)}) collective-permute-start(bf16[4,64,1024]{2,1,0:T(8,128)(2,1)} %fusion.37), channel_id=1, source_target_pairs={{0,8},{1,9},{2,10},{3,11},{4,12},{5,13},{6,14},{7,15},{8,0},{9,1},... | collective-permute-start | bytes 1572872 | tf_op jit(solution)/shard_map/ppermute | solution.py:64
  358.7 28.3 %collective-permute-start.44 = (bf16[512,1024]{1,0:T(8,128)(2,1)}, bf16[512,1024]{1,0:T(8,128)(2,1)}, u32[]{:S(2)}, u32[]{:S(2)}) collective-permute-start(bf16[512,1024]{1,0:T(8,128)(2,1)} %convolution_convert_fusion.4), channel_id=1, source_target_pairs={{0,8},{1,9},{2,10},{3,11},{4,12},{5,13},{6,14},{7,15},{8,0},{9,1},... | collective-permute-start | bytes 3145736 | tf_op jit(solution)/shard_map/ppermute | solution.py:64
  377.7 21.2 %collective-permute-start.45 = (bf16[2,32,4096]{2,1,0:T(8,128)(2,1)S(1)}, bf16[2,32,4096]{2,1,0:T(8,128)(2,1)S(1)}, u32[]{:S(2)}, u32[]{:S(2)}) collective-permute-start(bf16[2,32,4096]{2,1,0:T(8,128)(2,1)S(1)} %copy-done.66), channel_id=1, source_target_pairs={{0,2},{1,3},{2,0},{3,1},{4,6},{5,7},{6,4},{7,5},{8,10},{9,11},{10,... | collective-permute-start | bytes 1572872 | tf_op jit(solution)/shard_map/ppermute | solution.py:64
  377.9 38.3 %collective-permute-start.46 = (bf16[2,32,4096]{2,1,0:T(8,128)(2,1)S(1)}, bf16[2,32,4096]{2,1,0:T(8,128)(2,1)S(1)}, u32[]{:S(2)}, u32[]{:S(2)}) collective-permute-start(bf16[2,32,4096]{2,1,0:T(8,128)(2,1)S(1)} %copy-done.64), channel_id=1, source_target_pairs={{0,4},{1,5},{2,6},{3,7},{4,0},{5,1},{6,2},{7,3},{8,12},{9,13},{10,... | collective-permute-start | bytes 1572872 | tf_op jit(solution)/shard_map/ppermute | solution.py:64
  380.9 35.3 %collective-permute-start.47 = (bf16[2,32,4096]{2,1,0:T(8,128)(2,1)S(1)}, bf16[2,32,4096]{2,1,0:T(8,128)(2,1)S(1)}, u32[]{:S(2)}, u32[]{:S(2)}) collective-permute-start(bf16[2,32,4096]{2,1,0:T(8,128)(2,1)S(1)} %copy-done.62), channel_id=1, source_target_pairs={{0,6},{1,7},{2,4},{3,5},{4,2},{5,3},{6,0},{7,1},{8,14},{9,15},{10,... | collective-permute-start | bytes 1572872 | tf_op jit(solution)/shard_map/ppermute | solution.py:64
  385.5 30.7 %collective-permute-start.52 = (bf16[8,32,2048]{2,1,0:T(8,128)(2,1)S(1)}, bf16[8,32,2048]{2,1,0:T(8,128)(2,1)S(1)}, u32[]{:S(2)}, u32[]{:S(2)}) collective-permute-start(bf16[8,32,2048]{2,1,0:T(8,128)(2,1)S(1)} %get-tuple-element.209), channel_id=1, source_target_pairs={{0,1},{1,0},{2,3},{3,2},{4,5},{5,4},{6,7},{7,6},{8,9},{9,8},{10,11... | collective-permute-start | bytes 3145736 | tf_op jit(solution)/shard_map/ppermute | solution.py:64
  387.0 29.2 %collective-permute-start.53 = (bf16[8,32,2048]{2,1,0:T(8,128)(2,1)S(1)}, bf16[8,32,2048]{2,1,0:T(8,128)(2,1)S(1)}, u32[]{:S(2)}, u32[]{:S(2)}) collective-permute-start(bf16[8,32,2048]{2,1,0:T(8,128)(2,1)S(1)} %get-tuple-element.210), channel_id=1, source_target_pairs={{0,16},{1,17},{2,18},{3,19},{4,20},{5,21},{6,22},{7,23},{8,24},{9,... | collective-permute-start | bytes 3145736 | tf_op jit(solution)/shard_map/ppermute | solution.py:64
  417.3 21.9 %collective-permute-start.57 = (bf16[64,2048]{1,0:T(8,128)(2,1)S(1)}, bf16[64,2048]{1,0:T(8,128)(2,1)S(1)}, u32[]{:S(2)}, u32[]{:S(2)}) collective-permute-start(bf16[64,2048]{1,0:T(8,128)(2,1)S(1)} %get-tuple-element.263), channel_id=1, source_target_pairs={{0,6},{1,14},{2,4},{3,12},{4,2},{5,10},{6,0},{7,8},{8,7},{9,15},{1... | collective-permute-start | bytes 786440 | tf_op jit(solution)/shard_map/ppermute | solution.py:64
  422.8 32.6 %collective-permute-start.58 = (bf16[4,32,2048]{2,1,0:T(8,128)(2,1)}, bf16[4,32,2048]{2,1,0:T(8,128)(2,1)}, u32[]{:S(2)}, u32[]{:S(2)}) collective-permute-start(bf16[4,32,2048]{2,1,0:T(8,128)(2,1)} %get-tuple-element.219), channel_id=1, source_target_pairs={{0,16},{1,17},{2,18},{3,19},{4,20},{5,21},{6,22},{7,23},{8,24},{9,... | collective-permute-start | bytes 1572872 | tf_op jit(solution)/shard_map/ppermute | solution.py:64
  423.5 31.8 %collective-permute-start.59 = (bf16[4,32,2048]{2,1,0:T(8,128)(2,1)}, bf16[4,32,2048]{2,1,0:T(8,128)(2,1)}, u32[]{:S(2)}, u32[]{:S(2)}) collective-permute-start(bf16[4,32,2048]{2,1,0:T(8,128)(2,1)} %get-tuple-element.220), channel_id=1, source_target_pairs={{0,1},{1,0},{2,3},{3,2},{4,5},{5,4},{6,7},{7,6},{8,9},{9,8},{10,11... | collective-permute-start | bytes 1572872 | tf_op jit(solution)/shard_map/ppermute | solution.py:64
  426.1 25.9 %collective-permute-start.56 = (bf16[64,2048]{1,0:T(8,128)(2,1)}, bf16[64,2048]{1,0:T(8,128)(2,1)}, u32[]{:S(2)}, u32[]{:S(2)}) collective-permute-start(bf16[64,2048]{1,0:T(8,128)(2,1)} %get-tuple-element.264), channel_id=1, source_target_pairs={{0,4},{1,12},{2,6},{3,14},{4,0},{5,8},{6,2},{7,10},{8,5},{9,13},{1... | collective-permute-start | bytes 786440 | tf_op jit(solution)/shard_map/ppermute | solution.py:64
  439.2 12.8 %collective-permute-start.55 = (bf16[64,2048]{1,0:T(8,128)(2,1)}, bf16[64,2048]{1,0:T(8,128)(2,1)}, u32[]{:S(2)}, u32[]{:S(2)}) collective-permute-start(bf16[64,2048]{1,0:T(8,128)(2,1)} %get-tuple-element.265), channel_id=1, source_target_pairs={{0,2},{1,10},{2,0},{3,8},{4,6},{5,14},{6,4},{7,12},{8,3},{9,11},{1... | collective-permute-start | bytes 786440 | tf_op jit(solution)/shard_map/ppermute | solution.py:64
  440.0 12.0 %collective-permute-start.54 = (bf16[64,2048]{1,0:T(8,128)(2,1)}, bf16[64,2048]{1,0:T(8,128)(2,1)}, u32[]{:S(2)}, u32[]{:S(2)}) collective-permute-start(bf16[64,2048]{1,0:T(8,128)(2,1)} %get-tuple-element.266), channel_id=1, source_target_pairs={{0,0},{1,8},{2,2},{3,10},{4,4},{5,12},{6,6},{7,14},{8,1},{9,9},{10... | collective-permute-start | bytes 786440 | tf_op jit(solution)/shard_map/ppermute | solution.py:64
  467.4 40.5 %collective-permute-start.69 = (bf16[2,32,3072]{2,1,0:T(8,128)(2,1)}, bf16[2,32,3072]{2,1,0:T(8,128)(2,1)S(1)}, u32[]{:S(2)}, u32[]{:S(2)}) collective-permute-start(bf16[2,32,3072]{2,1,0:T(8,128)(2,1)} %constant_dynamic-update-slice_fusion.6), channel_id=1, source_target_pairs={{0,6},{1,7},{2,4},{3,5},{4,2},{5,3},{6,0},{7,1},{8,14},{9,15},{10,... | collective-permute-start | bytes 1179656 | tf_op jit(solution)/shard_map/ppermute | solution.py:64
  487.5 14.6 %collective-permute-start.67 = (bf16[2,32,3072]{2,1,0:T(8,128)(2,1)}, bf16[2,32,3072]{2,1,0:T(8,128)(2,1)S(1)}, u32[]{:S(2)}, u32[]{:S(2)}) collective-permute-start(bf16[2,32,3072]{2,1,0:T(8,128)(2,1)} %constant_dynamic-update-slice_fusion.2), channel_id=1, source_target_pairs={{0,2},{1,3},{2,0},{3,1},{4,6},{5,7},{6,4},{7,5},{8,10},{9,11},{10,... | collective-permute-start | bytes 1179656 | tf_op jit(solution)/shard_map/ppermute | solution.py:64
  487.5 20.2 %collective-permute-start.68 = (bf16[2,32,3072]{2,1,0:T(8,128)(2,1)}, bf16[2,32,3072]{2,1,0:T(8,128)(2,1)S(1)}, u32[]{:S(2)}, u32[]{:S(2)}) collective-permute-start(bf16[2,32,3072]{2,1,0:T(8,128)(2,1)} %constant_dynamic-update-slice_fusion.4), channel_id=1, source_target_pairs={{0,4},{1,5},{2,6},{3,7},{4,0},{5,1},{6,2},{7,3},{8,12},{9,13},{10,... | collective-permute-start | bytes 1179656 | tf_op jit(solution)/shard_map/ppermute | solution.py:64
  498.2 18.0 %collective-permute-start.61 = (bf16[128,1024]{1,0:T(8,128)(2,1)S(1)}, bf16[128,1024]{1,0:T(8,128)(2,1)}, u32[]{:S(2)}, u32[]{:S(2)}) collective-permute-start(bf16[128,1024]{1,0:T(8,128)(2,1)S(1)} %add_convert_fusion.3), channel_id=1, source_target_pairs={{0,1},{1,0},{2,3},{3,2},{4,5},{5,4},{6,7},{7,6},{8,9},{9,8},{10,11... | collective-permute-start | bytes 786440 | tf_op jit(solution)/shard_map/ppermute | solution.py:64
  (149 other events, 1854.1 us)
